TPU v7x, 32 devices: a whole 2x2x4 slice. The times are simulated.
32 devices in a mesh: store: 4 (over z), mp: 8 (over y, x, core).
Axes of the slice: x: 2, y: 2, z: 4, core: 2. Of those that a mesh axis runs over, the one named last changes fastest.
Arguments:
- tokens: bfloat16 [1024, 6144], P('store', 'mp'), may hold values from -6 to 6
- gain: float32 [6144], replicated, may hold values from 0.1 to 1.9
- base_projection_weight: bfloat16 [6144, 6144], P(None, 'mp'), may hold values from -0.078125 to 0.078125
- adapter_down_weight: bfloat16 [32, 64, 6144], P('store', None, 'mp'), may hold values from -0.078125 to 0.078125
- adapter_up_weight: bfloat16 [32, 64, 6144], P('store', None, 'mp'), may hold values from -0.75 to 0.75
- plan: int32 [4, 4], replicated, may hold values from 0 to 31, as said below
- target: int32 [1024, 1], P('store'), may hold values from 0 to 3; in each aligned block of 256 rows (0 to 255, 256 to 511, ...) at most 64 rows name the same one
- slot: int32 [1024], P('store'), may hold values from 0 to 11
Outputs:
- hidden_out: bfloat16 [1024, 6144], P('store', 'mp')
Inputs may be any that keep to these rules, and one draw needn't show every extreme that they name: plan[g, r] is an adapter owned by a store group other than g; adapter a is owned by group a // 8. `target`: among the 256 rows of one store group at most 64 name the same group, a bound that some block reaches.
All inputs are finite; a program needn't handle non-finite values.
Results may differ from a plain program's by a relative error of at most 0.0063.
Values may be sent and summed in bfloat16 or wider, within the bound.
No kernel may reach another device: no remote copies, remote signals or barrier semaphores. Data moves between devices by JAX's collectives and lax.ppermute only.
A program may use at most 64 MiB of HBM per device.

v0:
```python
import jax
import jax.numpy as jnp
from jax import lax
from jax.sharding import PartitionSpec as P

STEPS = 4
CAP = 64


adapter_scale = 0.5


def body(
    tokens, gain, base_projection_weight, adapter_down_weight, adapter_up_weight, plan, target, slot
):
    store_count = lax.axis_size("store")
    group = lax.axis_index("store")
    owned_adapters = adapter_down_weight.shape[0]
    rank_position = adapter_down_weight.shape[1]
    width_portion = adapter_down_weight.shape[2]
    replica_count = plan.shape[1]
    n_slots = owned_adapters + replica_count
    flattened_down = adapter_down_weight.reshape(owned_adapters, rank_position * width_portion)
    flattened_up = adapter_up_weight.reshape(owned_adapters, rank_position * width_portion)
    owner = plan // owned_adapters
    local = plan % owned_adapters
    select = jnp.logical_and(
        (owner == group)[:, :, None],
        local[:, :, None] == jnp.arange(owned_adapters, dtype=jnp.int32)[None, None, :],
    )
    select = select.astype(jnp.bfloat16).reshape(store_count * replica_count, owned_adapters)
    send_down = jnp.dot(select, flattened_down, preferred_element_type=jnp.float32).astype(
        jnp.bfloat16
    )
    send_up = jnp.dot(select, flattened_up, preferred_element_type=jnp.float32).astype(jnp.bfloat16)
    received = (
        lax.all_to_all(
            send_down.reshape(store_count, replica_count, rank_position * width_portion),
            "store",
            split_axis=0,
            concat_axis=0,
            tiled=True,
        ),
        lax.all_to_all(
            send_up.reshape(store_count, replica_count, rank_position * width_portion),
            "store",
            split_axis=0,
            concat_axis=0,
            tiled=True,
        ),
    )
    replica_down_factor = jnp.sum(received[0].astype(jnp.float32), axis=0)
    replica_up_factor = jnp.sum(received[1].astype(jnp.float32), axis=0)
    host_down = jnp.concatenate(
        [
            adapter_down_weight,
            replica_down_factor.astype(jnp.bfloat16).reshape(
                replica_count, rank_position, width_portion
            ),
        ],
        0,
    )
    host_down = host_down.reshape(n_slots * rank_position, width_portion)
    host_up = jnp.concatenate(
        [
            adapter_up_weight,
            replica_up_factor.astype(jnp.bfloat16).reshape(
                replica_count, rank_position, width_portion
            ),
        ],
        0,
    )
    host_up = host_up.reshape(n_slots * rank_position, width_portion)
    target_group = target[:, 0]
    member = (target_group[:, None] == jnp.arange(store_count, dtype=jnp.int32)[None, :]).astype(
        jnp.int32
    )
    earlier = jnp.cumsum(member, axis=0) - member
    bucket_place = jnp.sum(earlier * member, axis=1)
    row_index = target_group * CAP + bucket_place
    slot_buffer = (
        jnp.full((store_count * CAP,), -1, jnp.int32)
        .at[row_index]
        .set(slot)
        .reshape(store_count, CAP)
    )
    state = tokens
    column_start = lax.axis_index("mp") * width_portion
    for step in range(STEPS):
        whole = lax.all_gather(state, "mp", axis=1, tiled=True)
        values = whole.astype(jnp.float32)
        mean_sq = jnp.mean(values * values, axis=1, keepdims=True)
        normed = (values * lax.rsqrt(mean_sq + 1e-05) * gain[None, :]).astype(jnp.bfloat16)
        mine = lax.dynamic_slice_in_dim(normed, column_start, width_portion, 1)
        row_buffer = (
            jnp.zeros((store_count * CAP, width_portion), jnp.bfloat16).at[row_index].set(mine)
        )
        row_buffer = row_buffer.reshape(store_count, CAP, width_portion)
        rows = lax.all_to_all(row_buffer, "store", split_axis=0, concat_axis=0, tiled=True)
        slots_in = lax.all_to_all(slot_buffer, "store", split_axis=0, concat_axis=0, tiled=True)
        senders, count = slots_in.shape
        total_rows = senders * count
        flat_rows = rows.reshape(total_rows, width_portion)
        partial_value = lax.dot_general(
            flat_rows, host_down, (((1,), (1,)), ((), ())), preferred_element_type=jnp.float32
        )
        selected_adapter = (
            slots_in.reshape(total_rows)[:, None] == jnp.arange(n_slots, dtype=jnp.int32)[None, :]
        )
        partial_value = jnp.sum(
            partial_value.reshape(total_rows, n_slots, rank_position)
            * selected_adapter[:, :, None].astype(jnp.float32),
            axis=1,
        )
        summed_share = lax.psum_scatter(
            partial_value, "mp", scatter_dimension=0, tiled=True
        ).astype(jnp.bfloat16)
        inner = lax.all_gather(summed_share, "mp", axis=0, tiled=True)
        spread_rows = (
            selected_adapter[:, :, None].astype(jnp.bfloat16) * inner[:, None, :]
        ).reshape(total_rows, n_slots * rank_position)
        outer = jnp.dot(spread_rows, host_up, preferred_element_type=jnp.float32)
        outer = (adapter_scale * outer).astype(jnp.bfloat16).reshape(senders, count, width_portion)
        returned = lax.all_to_all(outer, "store", split_axis=0, concat_axis=0, tiled=True)
        delta = returned.reshape(store_count * CAP, width_portion)[row_index]
        base = jnp.dot(normed, base_projection_weight, preferred_element_type=jnp.float32)
        state = (state.astype(jnp.float32) + base + delta.astype(jnp.float32)).astype(jnp.bfloat16)
    return state


def solution(mesh):
    return jax.shard_map(
        body,
        mesh=mesh,
        in_specs=(
            P("store", "mp"),
            P(),
            P(None, "mp"),
            P("store", None, "mp"),
            P("store", None, "mp"),
            P(),
            P("store", None),
            P("store"),
        ),
        out_specs=P("store", "mp"),
        check_vma=False,
    )
```

profile of v0, /device:TPU:0, one launch (start us, length us, event | category | flops | bytes accessed | tf_op | source)
XLA Modules:
  0.0 576.0 jit_solution(5488597553345333319)
XLA Ops:
  13.1 6.3 %all-to-all-start = ((s32[4,1,64]{2,1,0:T(1,128)}), s32[4,1,64]{2,1,0:T(1,128)S(1)}, u32[]{:S(2)}, u32[]{:S(2)}) async-start(s32[4,1,64]{2,1,0:T(1,128)} %all_to_all.39), calls=%async_computation | async-start | bytes 4096 | tf_op jit(solution)/shard_map/all_to_all | solution.py:100
  24.9 4.9 all-to-all-start.3
  32.4 33.9 %all-to-all-done.3 = bf16[4,4,49152]{2,1,0:T(4,128)(2,1)S(1)} async-done(((bf16[4,4,49152]{2,1,0:T(4,128)(2,1)}), bf16[4,4,49152]{2,1,0:T(4,128)(2,1)S(1)}, u32[]{:S(2)}, u32[]{:S(2)}) %all-to-all-start.3) | async-done | bytes 1572896 | tf_op jit(solution)/shard_map/all_to_all | solution.py:44
  66.3 3.6 all-to-all-start.2
  69.9 2.1 constant_dynamic-update-slice_fusion
  71.9 2.7 fusion
  74.8 2.6 fusion.2
  77.3 2.8 scatter_custom_fusion.1
  80.2 26.1 %all-to-all-done.2 = bf16[4,4,49152]{2,1,0:T(4,128)(2,1)S(1)} async-done(((bf16[4,4,49152]{2,1,0:T(4,128)(2,1)}), bf16[4,4,49152]{2,1,0:T(4,128)(2,1)S(1)}, u32[]{:S(2)}, u32[]{:S(2)}) %all-to-all-start.2) | async-done | bytes 1572896 | tf_op jit(solution)/shard_map/all_to_all | solution.py:37
  106.3 4.1 all-to-all-start.1
  110.4 2.1 constant_dynamic-update-slice_fusion.1
  117.5 4.1 all-to-all-done.1
  121.6 1.9 fusion.28
  124.4 32.5 %reduce-scatter.13.cloned.1.call-done = f32[32,64]{1,0:T(8,128)} async-done(((f32[256,64]{1,0:T(8,128)}), f32[32,64]{1,0:T(8,128)}) %reduce-scatter.13.cloned.1.call-update) | async-done | bytes 8208 | tf_op jit(solution)/shard_map/reduce_scatter | solution.py:115
  157.6 9.2 %all_gather.25 = bf16[256,64]{1,0:T(8,128)(2,1)S(1)} all-gather(bf16[32,64]{1,0:T(8,128)(2,1)S(1)} %convert_element_type.132), channel_id=1, replica_groups=mesh['store'=4,'mp'=8] {'mp'}, dimensions={0}, use_global_device_ids=true | all-gather | bytes 36864 | tf_op jit(solution)/shard_map/all_gather | solution.py:118
  168.1 4.9 all-to-all-start.4
  174.4 10.8 %all-to-all-done.4 = bf16[4,64,768]{2,1,0:T(8,128)(2,1)S(1)} async-done(((bf16[4,64,768]{2,1,0:T(8,128)(2,1)}), bf16[4,64,768]{2,1,0:T(8,128)(2,1)S(1)}, u32[]{:S(2)}, u32[]{:S(2)}) %all-to-all-start.4) | async-done | bytes 393248 | tf_op jit(solution)/shard_map/all_to_all | solution.py:124
  185.2 2.1 gather_fusion
  187.3 7.2 %fusion.20 = bf16[256,768]{1,0:T(8,128)(2,1)} fusion(bf16[256,6144]{1,0:T(8,128)(2,1)S(1)} %copy-done.4, bf16[6144,768]{1,0:T(8,128)(2,1)} %param.10, bf16[256,768]{1,0:T(8,128)(2,1)} %gather_fusion, bf16[256,768]{1,0:T(8,128)(2,1)} %param.8), kind=kOutput, calls=%fused_computation.51 | convolution fusion | flops 2416902144 | bytes 13762560 | tf_op jit(solution)/shard_map/dot_general | solution.py:126
  194.6 30.5 %all-gather.7.cloned.1.call-done = bf16[256,6144]{1,0:T(8,128)(2,1)} async-done(((bf16[256,768]{1,0:T(8,128)(2,1)}), bf16[256,6144]{1,0:T(8,128)(2,1)}) %all-gather.7.cloned.1.call-update) | async-done | bytes 3145744 | tf_op jit(solution)/shard_map/all_gather | solution.py:90
  225.0 2.7 fusion.3
  229.0 1.9 scatter_custom_fusion.2
  230.8 16.5 %all_to_all.62 = bf16[4,64,768]{2,1,0:T(8,128)(2,1)S(1)} all-to-all(bf16[4,64,768]{2,1,0:T(8,128)(2,1)S(1)} %bitcast.123), channel_id=1, replica_groups=mesh['store'=4,'mp'=8] {'store'}, dimensions={0} | all-to-all | bytes 786432 | tf_op jit(solution)/shard_map/all_to_all | solution.py:99
  247.4 1.8 fusion.29
  250.0 31.6 %reduce-scatter.15.cloned.1.call-done = f32[32,64]{1,0:T(8,128)} async-done(((f32[256,64]{1,0:T(8,128)}), f32[32,64]{1,0:T(8,128)}) %reduce-scatter.15.cloned.1.call-update) | async-done | bytes 8208 | tf_op jit(solution)/shard_map/reduce_scatter | solution.py:115
  282.2 9.2 %all_gather.27 = bf16[256,64]{1,0:T(8,128)(2,1)S(1)} all-gather(bf16[32,64]{1,0:T(8,128)(2,1)S(1)} %convert_element_type.140), channel_id=1, replica_groups=mesh['store'=4,'mp'=8] {'mp'}, dimensions={0}, use_global_device_ids=true | all-gather | bytes 36864 | tf_op jit(solution)/shard_map/all_gather | solution.py:118
  293.3 16.6 %all_to_all.63 = bf16[4,64,768]{2,1,0:T(8,128)(2,1)S(1)} all-to-all(bf16[4,64,768]{2,1,0:T(8,128)(2,1)S(1)} %bitcast.129), channel_id=1, replica_groups=mesh['store'=4,'mp'=8] {'store'}, dimensions={0} | all-to-all | bytes 786432 | tf_op jit(solution)/shard_map/all_to_all | solution.py:124
  309.9 2.1 gather_fusion.1
  312.0 7.2 %fusion.21 = bf16[256,768]{1,0:T(8,128)(2,1)} fusion(bf16[256,6144]{1,0:T(8,128)(2,1)S(1)} %fusion.5, bf16[6144,768]{1,0:T(8,128)(2,1)} %param.10, bf16[256,768]{1,0:T(8,128)(2,1)} %gather_fusion.1, bf16[256,768]{1,0:T(8,128)(2,1)} %fusion.20), kind=kOutput, calls=%fused_computation.52 | convolution fusion | flops 2416902144 | bytes 13762560 | tf_op jit(solution)/shard_map/dot_general | solution.py:126
  319.4 30.3 %all-gather.9.cloned.1.call-done = bf16[256,6144]{1,0:T(8,128)(2,1)} async-done(((bf16[256,768]{1,0:T(8,128)(2,1)}), bf16[256,6144]{1,0:T(8,128)(2,1)}) %all-gather.9.cloned.1.call-update) | async-done | bytes 3145744 | tf_op jit(solution)/shard_map/all_gather | solution.py:90
  349.7 2.7 fusion.6
  353.6 1.9 scatter_custom_fusion.3
  355.5 16.5 %all_to_all.64 = bf16[4,64,768]{2,1,0:T(8,128)(2,1)S(1)} all-to-all(bf16[4,64,768]{2,1,0:T(8,128)(2,1)S(1)} %bitcast.124), channel_id=1, replica_groups=mesh['store'=4,'mp'=8] {'store'}, dimensions={0} | all-to-all | bytes 786432 | tf_op jit(solution)/shard_map/all_to_all | solution.py:99
  372.0 1.8 fusion.30
  374.6 31.6 %reduce-scatter.17.cloned.1.call-done = f32[32,64]{1,0:T(8,128)} async-done(((f32[256,64]{1,0:T(8,128)}), f32[32,64]{1,0:T(8,128)}) %reduce-scatter.17.cloned.1.call-update) | async-done | bytes 8208 | tf_op jit(solution)/shard_map/reduce_scatter | solution.py:115
  406.9 9.2 %all_gather.29 = bf16[256,64]{1,0:T(8,128)(2,1)S(1)} all-gather(bf16[32,64]{1,0:T(8,128)(2,1)S(1)} %convert_element_type.147), channel_id=1, replica_groups=mesh['store'=4,'mp'=8] {'mp'}, dimensions={0}, use_global_device_ids=true | all-gather | bytes 36864 | tf_op jit(solution)/shard_map/all_gather | solution.py:118
  418.0 16.6 %all_to_all.65 = bf16[4,64,768]{2,1,0:T(8,128)(2,1)S(1)} all-to-all(bf16[4,64,768]{2,1,0:T(8,128)(2,1)S(1)} %bitcast.131), channel_id=1, replica_groups=mesh['store'=4,'mp'=8] {'store'}, dimensions={0} | all-to-all | bytes 786432 | tf_op jit(solution)/shard_map/all_to_all | solution.py:124
  434.6 2.1 gather_fusion.2
  436.6 7.2 %fusion.22 = bf16[256,768]{1,0:T(8,128)(2,1)} fusion(bf16[256,6144]{1,0:T(8,128)(2,1)S(1)} %fusion.8, bf16[6144,768]{1,0:T(8,128)(2,1)} %param.10, bf16[256,768]{1,0:T(8,128)(2,1)} %gather_fusion.2, bf16[256,768]{1,0:T(8,128)(2,1)} %fusion.21), kind=kOutput, calls=%fused_computation.53 | convolution fusion | flops 2416902144 | bytes 13762560 | tf_op jit(solution)/shard_map/dot_general | solution.py:126
  443.9 30.5 %all-gather.11.cloned.1.call-done = bf16[256,6144]{1,0:T(8,128)(2,1)} async-done(((bf16[256,768]{1,0:T(8,128)(2,1)}), bf16[256,6144]{1,0:T(8,128)(2,1)}) %all-gather.11.cloned.1.call-update) | async-done | bytes 3145744 | tf_op jit(solution)/shard_map/all_gather | solution.py:90
  474.4 2.7 fusion.9
  478.3 1.9 scatter_custom_fusion.4
  480.2 16.5 %all_to_all.66 = bf16[4,64,768]{2,1,0:T(8,128)(2,1)S(1)} all-to-all(bf16[4,64,768]{2,1,0:T(8,128)(2,1)S(1)} %bitcast.121), channel_id=1, replica_groups=mesh['store'=4,'mp'=8] {'store'}, dimensions={0} | all-to-all | bytes 786432 | tf_op jit(solution)/shard_map/all_to_all | solution.py:99
  499.2 31.6 %reduce-scatter.19.cloned.1.call-done = f32[32,64]{1,0:T(8,128)} async-done(((f32[256,64]{1,0:T(8,128)}), f32[32,64]{1,0:T(8,128)}) %reduce-scatter.19.cloned.1.call-update) | async-done | bytes 8208 | tf_op jit(solution)/shard_map/reduce_scatter | solution.py:115
  531.6 9.4 %all_gather.31 = bf16[256,64]{1,0:T(8,128)(2,1)S(1)} all-gather(bf16[32,64]{1,0:T(8,128)(2,1)S(1)} %convert_element_type.154), channel_id=1, replica_groups=mesh['store'=4,'mp'=8] {'mp'}, dimensions={0}, use_global_device_ids=true | all-gather | bytes 36864 | tf_op jit(solution)/shard_map/all_gather | solution.py:118
  542.9 16.6 %all_to_all.67 = bf16[4,64,768]{2,1,0:T(8,128)(2,1)S(1)} all-to-all(bf16[4,64,768]{2,1,0:T(8,128)(2,1)S(1)} %bitcast.127), channel_id=1, replica_groups=mesh['store'=4,'mp'=8] {'store'}, dimensions={0} | all-to-all | bytes 786432 | tf_op jit(solution)/shard_map/all_to_all | solution.py:124
  559.5 2.1 gather_fusion.3
  561.6 7.2 %fusion.23 = bf16[256,768]{1,0:T(8,128)(2,1)} fusion(bf16[256,6144]{1,0:T(8,128)(2,1)S(1)} %fusion.11, bf16[6144,768]{1,0:T(8,128)(2,1)} %param.10, bf16[256,768]{1,0:T(8,128)(2,1)} %gather_fusion.3, bf16[256,768]{1,0:T(8,128)(2,1)} %fusion.22), kind=kOutput, calls=%fused_computation.54 | convolution fusion | flops 2416902144 | bytes 13762560 | tf_op jit(solution)/shard_map/dot_general | solution.py:126
  (107 shorter events, 39.7 us)
Async XLA Ops:
  6.5 65.4 %all-gather.5.cloned.1.call-start = ((), (), s32[]{:S(2)}) async-start(), calls=%async_computation.15 | async-start | bytes 3538944 | tf_op jit(solution)/shard_map/all_gather | solution.py:90
  10.9 66.4 %copy-start.16 = (s32[256,1]{0,1:T(1,128)}, s32[256,1]{0,1:T(1,128)S(1)}, u32[]{:S(2)}) copy-start(s32[256,1]{0,1:T(1,128)S(1)} %compare_select_fusion) | copy-start | bytes 3076
  13.1 11.8 %all-to-all-start = ((s32[4,1,64]{2,1,0:T(1,128)}), s32[4,1,64]{2,1,0:T(1,128)S(1)}, u32[]{:S(2)}, u32[]{:S(2)}) async-start(s32[4,1,64]{2,1,0:T(1,128)} %all_to_all.39), calls=%async_computation | async-start | bytes 4096 | tf_op jit(solution)/shard_map/all_to_all | solution.py:100
  23.2 6.6 %copy-start.5 = (bf16[8,64,768]{2,1,0:T(8,128)(2,1)S(1)}, bf16[8,64,768]{2,1,0:T(8,128)(2,1)}, u32[]{:S(2)}) copy-start(bf16[8,64,768]{2,1,0:T(8,128)(2,1)} %param.11) | copy-start | bytes 2359300
  24.9 41.3 %all-to-all-start.3 = ((bf16[4,4,49152]{2,1,0:T(4,128)(2,1)}), bf16[4,4,49152]{2,1,0:T(4,128)(2,1)S(1)}, u32[]{:S(2)}, u32[]{:S(2)}) async-start(bf16[4,4,49152]{2,1,0:T(4,128)(2,1)} %reshape.206), calls=%async_computation.3 | async-start | bytes 3145728 | tf_op jit(solution)/shard_map/all_to_all | solution.py:44
  66.3 40.0 %all-to-all-start.2 = ((bf16[4,4,49152]{2,1,0:T(4,128)(2,1)}), bf16[4,4,49152]{2,1,0:T(4,128)(2,1)S(1)}, u32[]{:S(2)}, u32[]{:S(2)}) async-start(bf16[4,4,49152]{2,1,0:T(4,128)(2,1)} %reshape.203), calls=%async_computation.2 | async-start | bytes 3145728 | tf_op jit(solution)/shard_map/all_to_all | solution.py:37
  69.8 4.9 copy-start.8
  71.9 2.8 copy-start
  106.3 15.3 %all-to-all-start.1 = ((bf16[4,64,768]{2,1,0:T(8,128)(2,1)}), bf16[4,64,768]{2,1,0:T(8,128)(2,1)}, u32[]{:S(2)}, u32[]{:S(2)}) async-start(bf16[4,64,768]{2,1,0:T(8,128)(2,1)} %bitcast.6), calls=%async_computation.1 | async-start | bytes 786432 | tf_op jit(solution)/shard_map/all_to_all | solution.py:99
  110.4 46.5 %reduce-scatter.13.cloned.1.call-start = ((), (), s32[]{:S(2)}) async-start(), calls=%async_computation.19 | async-start | bytes 147456 | tf_op jit(solution)/shard_map/reduce_scatter | solution.py:115
  115.5 8.7 %copy-start.6 = (bf16[12,64,768]{2,1,0:T(8,128)(2,1)S(1)}, bf16[12,64,768]{2,1,0:T(8,128)(2,1)}, u32[]{:S(2)}) copy-start(bf16[12,64,768]{2,1,0:T(8,128)(2,1)} %constant_dynamic-update-slice_fusion.1) | copy-start | bytes 3538948
  116.6 50.2 %copy-start.12 = (bf16[256,12]{0,1:T(8,128)(2,1)S(1)}, bf16[256,12]{0,1:T(8,128)(2,1)}, u32[]{:S(2)}) copy-start(bf16[256,12]{0,1:T(8,128)(2,1)} %get-tuple-element.5) | copy-start | bytes 18436
  124.3 42.5 %copy-start.7 = (bf16[12,64,768]{2,1,0:T(8,128)(2,1)}, bf16[12,64,768]{2,1,0:T(8,128)(2,1)S(1)}, u32[]{:S(2)}) copy-start(bf16[12,64,768]{2,1,0:T(8,128)(2,1)S(1)} %bitcast_dynamic-update-slice_fusion) | copy-start | bytes 3538948
  168.1 19.1 %copy-start.4 = (bf16[256,6144]{1,0:T(8,128)(2,1)S(1)}, bf16[256,6144]{1,0:T(8,128)(2,1)}, u32[]{:S(2)}) copy-start(bf16[256,6144]{1,0:T(8,128)(2,1)} %fusion.2) | copy-start | bytes 9437188
  168.1 17.0 %all-to-all-start.4 = ((bf16[4,64,768]{2,1,0:T(8,128)(2,1)}), bf16[4,64,768]{2,1,0:T(8,128)(2,1)S(1)}, u32[]{:S(2)}, u32[]{:S(2)}) async-start(bf16[4,64,768]{2,1,0:T(8,128)(2,1)} %bitcast.125), calls=%async_computation.4 | async-start | bytes 786432 | tf_op jit(solution)/shard_map/all_to_all | solution.py:124
  173.0 52.0 %all-gather.7.cloned.1.call-start = ((), (), s32[]{:S(2)}) async-start(), calls=%async_computation.16 | async-start | bytes 3538944 | tf_op jit(solution)/shard_map/all_gather | solution.py:90
  194.5 33.3 %copy-start.9 = (f32[6144]{0:T(1024)S(1)}, f32[6144]{0:T(1024)}, u32[]{:S(2)}) copy-start(f32[6144]{0:T(1024)} %param.9) | copy-start | bytes 73732
  194.5 87.0 %reduce-scatter.15.cloned.1.call-start = ((), (), s32[]{:S(2)}) async-start(), calls=%async_computation.20 | async-start | bytes 147456 | tf_op jit(solution)/shard_map/reduce_scatter | solution.py:115
  225.0 2.8 copy-start.1
  247.3 44.2 %copy-start.13 = (bf16[256,12]{0,1:T(8,128)(2,1)S(1)}, bf16[256,12]{0,1:T(8,128)(2,1)}, u32[]{:S(2)}) copy-start(bf16[256,12]{0,1:T(8,128)(2,1)} %get-tuple-element.5) | copy-start | bytes 18436
  249.9 99.8 %all-gather.9.cloned.1.call-start = ((), (), s32[]{:S(2)}) async-start(), calls=%async_computation.17 | async-start | bytes 3538944 | tf_op jit(solution)/shard_map/all_gather | solution.py:90
  319.2 33.3 %copy-start.10 = (f32[6144]{0:T(1024)S(1)}, f32[6144]{0:T(1024)}, u32[]{:S(2)}) copy-start(f32[6144]{0:T(1024)} %param.9) | copy-start | bytes 73732
  319.2 87.0 %reduce-scatter.17.cloned.1.call-start = ((), (), s32[]{:S(2)}) async-start(), calls=%async_computation.21 | async-start | bytes 147456 | tf_op jit(solution)/shard_map/reduce_scatter | solution.py:115
  349.7 2.8 copy-start.2
  372.0 44.2 %copy-start.14 = (bf16[256,12]{0,1:T(8,128)(2,1)S(1)}, bf16[256,12]{0,1:T(8,128)(2,1)}, u32[]{:S(2)}) copy-start(bf16[256,12]{0,1:T(8,128)(2,1)} %get-tuple-element.5) | copy-start | bytes 18436
  374.6 99.8 %all-gather.11.cloned.1.call-start = ((), (), s32[]{:S(2)}) async-start(), calls=%async_computation.18 | async-start | bytes 3538944 | tf_op jit(solution)/shard_map/all_gather | solution.py:90
  443.8 33.3 %copy-start.11 = (f32[6144]{0:T(1024)S(1)}, f32[6144]{0:T(1024)}, u32[]{:S(2)}) copy-start(f32[6144]{0:T(1024)} %param.9) | copy-start | bytes 73732
  443.8 87.0 %reduce-scatter.19.cloned.1.call-start = ((), (), s32[]{:S(2)}) async-start(), calls=%async_computation.22 | async-start | bytes 147456 | tf_op jit(solution)/shard_map/reduce_scatter | solution.py:115
  474.4 2.8 copy-start.3
  496.7 44.4 %copy-start.15 = (bf16[256,12]{0,1:T(8,128)(2,1)S(1)}, bf16[256,12]{0,1:T(8,128)(2,1)}, u32[]{:S(2)}) copy-start(bf16[256,12]{0,1:T(8,128)(2,1)} %get-tuple-element.5) | copy-start | bytes 18436
Sparse Core Ops, SparseCore 0:
  9.3 34.9 all-gather.4
  124.4 32.4 reduce-scatter.12
  194.6 30.3 all-gather.6
  250.0 31.4 reduce-scatter.14
  319.3 30.3 all-gather.8
  374.7 31.4 reduce-scatter.16
  444.0 30.3 all-gather.10
  499.4 31.4 reduce-scatter.18
where the time goes:
time: 586 us; the launch traced here: 576 us
  waiting for transfers between devices  294 us (50%)
  blocking collectives  136 us (23%)
  matrix products  43.9 us (7%)
  local copies, waits for them, and re-layouts  33.7 us (6%)
  other arithmetic  29.1 us (5%)
  starting transfers between devices  24.4 us (4%)
  between operations  14.3 us (2%)
    reduce_scatter x4, waiting for transfers between devices, body(): lax.psum_scatter(partial_value, 'mp', scatter_dimension=0, tiled=True)  127 us
    all_gather x4, waiting for transfers between devices, body(): whole = lax.all_gather(state, 'mp', axis=1, tiled=True)  91.2 us
    all_to_all x3, blocking collectives, body(): lax.all_to_all(outer, 'store', split_axis=0, concat_axis=0, tiled=True)  49.7 us
    all_to_all x3, blocking collectives, body(): lax.all_to_all(row_buffer, 'store', split_axis=0, concat_axis=0, tiled=True)  49.5 us
    all_gather x4, blocking collectives, body(): inner = lax.all_gather(summed_share, 'mp', axis=0, tiled=True)  37 us
    all_to_all x1, waiting for transfers between devices, body(): lax.all_to_all(send_up.reshape(store_count, replica_count, rank_position...  33.9 us
    dot_general x4, matrix products, body(): jnp.dot(normed, base_projection_weight, preferred_element_type=jnp.float32)  28.8 us
    all_to_all x1, waiting for transfers between devices, body(): lax.all_to_all(send_down.reshape(store_count, replica_count, rank_positio...  26.1 us
  transfers between devices with their start and end apart: 13, of which 12 were waited for; matrix products, arithmetic and copies ran while one was open for 5% of the time, Pallas kernels for 0%

commit v1 on v0

v1 whole, which is shorter than its diff:
```python
import functools
import math

import jax
import jax.numpy as jnp
from jax import lax
from jax.experimental import pallas as pl
from jax.experimental.pallas import tpu as pltpu
from jax.sharding import PartitionSpec as P

STEPS = 4
CAP = 64
EPS = 1e-05
EXT = 16
MIB = 2**20

adapter_scale = 0.5

F32 = jnp.float32
BF16 = jnp.bfloat16
IN_VMEM = pl.BlockSpec(memory_space=pltpu.VMEM)
IN_SMEM = pl.BlockSpec(memory_space=pltpu.SMEM)
CONTRACT_LAST = (((1,), (1,)), ((), ()))
CONTRACT_FIRST = (((0,), (0,)), ((), ()))


def call(kernel, out, specs, *args, flops=0, name=None):
    many = isinstance(out, list)
    shapes = [jax.ShapeDtypeStruct(s, d) for s, d in (out if many else [out])]
    moved = sum(a.size * a.dtype.itemsize for a in args if a.size < 2**20)
    r = pl.pallas_call(
        kernel,
        out_shape=shapes,
        in_specs=specs,
        out_specs=[IN_VMEM] * len(shapes),
        compiler_params=pltpu.CompilerParams(vmem_limit_bytes=24 * MIB),
        cost_estimate=pl.CostEstimate(flops=flops, bytes_accessed=moved, transcendentals=0),
        name=name,
    )(*args)
    return r if many else r[0]


def dot(a, b, dims=(((1,), (0,)), ((), ()))):
    return lax.dot_general(a, b, dims, preferred_element_type=F32)


def iota(shape, dim):
    return lax.broadcasted_iota(jnp.int32, shape, dim)


def sort_kernel(me_ref, tokens_ref, target_ref, slot_ref, perm_ref, *chunk_refs):
    n_tokens, width = tokens_ref.shape
    groups = len(chunk_refs)
    rows = groups * CAP
    apart = jnp.bitwise_xor(target_ref[...], me_ref[0])
    member = (iota((max(8, groups), n_tokens), 0) == apart).astype(F32)
    before = (iota((n_tokens, n_tokens), 0) < iota((n_tokens, n_tokens), 1)).astype(BF16)
    earlier = dot(member.astype(BF16), before)
    place = jnp.sum(earlier * member, axis=0, keepdims=True).astype(jnp.int32)
    perm = (iota((rows, n_tokens), 0) == apart * CAP + place).astype(F32).astype(BF16)
    perm_ref[...] = perm
    sorted_rows = dot(perm, tokens_ref[...]).astype(BF16)
    slots = jnp.broadcast_to((slot_ref[...] + 1).astype(F32), (8, n_tokens)).astype(BF16)
    slots = dot(slots, perm, CONTRACT_LAST)
    lanes = 2 * CAP
    for k, ref in enumerate(chunk_refs):
        ref[:, :width] = sorted_rows[k * CAP : (k + 1) * CAP]
        half = slots[:, (k // 2) * lanes : (k // 2 + 1) * lanes]
        ref[:, width:] = jnp.concatenate([half, jnp.zeros((CAP - 8, lanes), F32)], 0).astype(BF16)


def unsort_kernel(perm_ref, *refs):
    rows = jnp.concatenate([r[...] for r in refs[:-1]], axis=0)
    refs[-1][...] = dot(perm_ref[...], rows, CONTRACT_FIRST).astype(BF16)


def pick_kernel(owned, where_ref, plan_ref, own_ref, carry_ref, out_ref):
    rank = own_ref.shape[0] // owned
    for r in range(plan_ref.shape[1]):
        adapter = plan_ref[where_ref[1], r]
        mine = adapter // owned == where_ref[0]
        at = slice(r * rank, (r + 1) * rank)

        @pl.when(mine)
        def _():
            out_ref[at, :] = own_ref[pl.ds((adapter % owned) * rank, rank), :]

        @pl.when(jnp.logical_not(mine))
        def _():
            out_ref[at, :] = carry_ref[at, :]


def fetch_copies(plan, own, owned, group, groups):
    copies = plan.shape[1]
    rank = own[0].shape[0] // owned
    zero = jnp.zeros((copies * rank, own[0].shape[1]), BF16)
    up, down = [zero] * len(own), [zero] * len(own)
    for r in range(1, groups):
        for i, factor in enumerate(own):
            for carry, step in ((up, 1), (down, -1)):
                place = group if step > 0 else groups - 1 - group
                dest = jnp.clip(groups + place - r, 0, groups - 1)
                dest = dest if step > 0 else groups - 1 - dest
                send = call(
                    functools.partial(pick_kernel, owned),
                    (zero.shape, BF16),
                    [IN_SMEM, IN_SMEM, IN_VMEM, IN_VMEM],
                    jnp.stack([group, dest]).astype(jnp.int32),
                    plan,
                    factor,
                    carry[i],
                    name="pick",
                )
                chain = [(g, g + 1) for g in range(r)]
                if step < 0:
                    chain = [(groups - 1 - a, groups - 1 - b) for a, b in chain]
                carry[i] = lax.ppermute(send, "store", chain)
    return [a + b for a, b in zip(up, down)]


def two_parts(row):
    high = row.astype(BF16).astype(F32)
    at = iota((EXT, row.shape[1]), 0)
    return jnp.where(at == 0, high, jnp.where(at == 1, row - high, 0.0)).astype(BF16)


def put_extra(msg_ref, rows, inner, squares):
    width = msg_ref.shape[1]
    groups = 0 if inner is None else inner.shape[0] // EXT
    rank_groups = width // rows
    msg_ref[rows:, :] = jnp.zeros((EXT, width), BF16)
    for g in range(groups):
        msg_ref[rows:, g * rows : (g + 1) * rows] = inner[g * EXT : (g + 1) * EXT].astype(BF16)
    msg_ref[rows:, (rank_groups - 1) * rows :] = two_parts(squares)


def squares_row(state):
    total = jnp.sum(state * state, axis=1, keepdims=True)
    rows = state.shape[0]
    return jnp.transpose(jnp.broadcast_to(total, (rows, rows)))[0:1, :]


def slot_masks(slots, first, count, shape):
    return [jnp.broadcast_to(slots[0:1, :] == float(j), shape) for j in range(first, first + count)]


def inner_partial(u, slots, down_refs, rank):
    first, total = 0, None
    rows = u.shape[0]
    for ref in down_refs:
        count = ref.shape[0] // rank
        product = dot(ref[...], u, CONTRACT_LAST)
        for j, mask in enumerate(slot_masks(slots, first, count, (rank, rows))):
            term = jnp.where(mask, product[j * rank : (j + 1) * rank], 0.0)
            total = term if total is None else total + term
        first += count
    return total


def first_kernel(even_ref, odd_ref, gain_ref, state_ref, slots_ref, msg_ref):
    cap = even_ref.shape[0]
    rows, width = state_ref.shape
    state_ref[:cap] = even_ref[:, :width]
    state_ref[cap:] = odd_ref[:, :width]
    lane = iota((8, rows), 1)
    even, odd = even_ref[:, width:].astype(F32)[0:8], odd_ref[:, width:].astype(F32)[0:8]
    slots_ref[...] = jnp.where(lane < cap, even, odd) - 1.0
    state = state_ref[...].astype(F32)
    msg_ref[:rows, :] = (state * gain_ref[...]).astype(BF16)
    put_extra(msg_ref, rows, None, squares_row(state))


def first_inner_kernel(msg0_ref, msg1_ref, slots0_ref, slots1_ref, own_ref, copy_ref, out_ref):
    rank, rows = out_ref.shape[0], out_ref.shape[1] // 2
    for h, (msg, slots) in enumerate(((msg0_ref, slots0_ref), (msg1_ref, slots1_ref))):
        out_ref[:, h * rows : (h + 1) * rows] = inner_partial(
            msg[:rows, :], slots[...], (own_ref, copy_ref), rank
        )


def block_kernel(n_blocks, at, last, place_ref, weight_ref, other_ref, *refs):
    msgs, refs = refs[:n_blocks], refs[n_blocks:]
    width = weight_ref.shape[1]
    rows = msgs[0].shape[0] - EXT
    if at[0] == 0:
        old = None
        outs = refs
    else:
        old, outs = refs[:3], refs[3:]
    mine = theirs = extra = None
    for i, msg in enumerate(msgs):
        q = place_ref[at[i]]
        u = msg[:rows, :]
        a = dot(u, weight_ref[pl.ds(pl.multiple_of((2 * q + place_ref[4]) * width, width), width), :])
        b = dot(u, other_ref[pl.ds(pl.multiple_of(q * width, width), width), :])
        e = msg[rows:, :].astype(F32)
        mine, theirs, extra = (a, b, e) if mine is None else (mine + a, theirs + b, extra + e)
    if old is not None:
        mine, theirs, extra = mine + old[0][...], theirs + old[1][...], extra + old[2][...]
    outs[0][...] = mine
    outs[2][...] = extra
    if not last:
        outs[1][...] = theirs
        return
    outs[1][:rows, :] = theirs.astype(BF16)
    outs[1][rows:, :] = extra.astype(BF16)
    tail = extra[:, width - rows :]
    outs[1][rows:, width - rows :] = two_parts(tail[0:1] + tail[1:2])


def finish_kernel(
    first, last, width_all, rank, mine_ref, extra_ref, got_ref, state_ref, slots_ref, gain_ref, down_ref, downc_ref, up_ref, upc_ref, *refs
):
    rows, width = state_ref.shape
    if first:
        inner_ref, refs = refs[0], refs[1:]
    extra = extra_ref[...] + got_ref[rows:, :].astype(F32)
    if first:
        inner = inner_ref[...]
    else:
        inner = jnp.concatenate(
            [extra[:, g * rows : (g + 1) * rows] for g in range(rank // EXT)], axis=0
        )
    tail = extra[:, width - rows :]
    scale = lax.rsqrt((tail[0:1] + tail[1:2]) / width_all + EPS)
    inner = (inner * scale).astype(BF16).astype(F32)
    slots = slots_ref[...]
    outer, begin = None, 0
    for ref in (up_ref, upc_ref):
        count = ref.shape[0] // rank
        spread = jnp.concatenate(
            [jnp.where(m, inner, 0.0) for m in slot_masks(slots, begin, count, (rank, rows))], axis=0
        ).astype(BF16)
        term = dot(spread, ref[...], CONTRACT_FIRST)
        outer = term if outer is None else outer + term
        begin += count
    delta = (adapter_scale * outer).astype(BF16).astype(F32)
    column = jnp.transpose(jnp.broadcast_to(scale, (rows, rows)))
    column = jnp.concatenate([column] * (width // rows), axis=1)
    base = (mine_ref[...] + got_ref[:rows, :].astype(F32)) * column
    state = (state_ref[...].astype(F32) + base + delta).astype(BF16)
    refs[0][...] = state
    if last:
        return
    msg_ref = refs[1]
    state = state.astype(F32)
    u = (state * gain_ref[...]).astype(BF16)
    msg_ref[:rows, :] = u
    put_extra(msg_ref, rows, inner_partial(u, slots, (down_ref, downc_ref), rank), squares_row(state))


def body(tokens, gain, base_projection_weight, adapter_down_weight, adapter_up_weight, plan, target, slot):
    groups = lax.axis_size("store")
    parts = lax.axis_size("mp")
    group = lax.axis_index("store")
    part = lax.axis_index("mp")
    n_tokens, width = tokens.shape
    owned, rank = adapter_down_weight.shape[:2]
    rows = 2 * CAP
    quarter = parts // 2
    place = part // 2
    core = part % 2

    def mp(x, pairs_of):
        return lax.ppermute(x, "mp", [(i, pairs_of(i)) for i in range(parts)])

    def sibling(x):
        return mp(x, lambda i: i ^ 1)

    def side_a(x):
        return mp(x, lambda i: i ^ (4 if i % 2 else 2))

    def side_b(x):
        return mp(x, lambda i: i ^ (2 if i % 2 else 4))

    def store(x, k):
        return lax.ppermute(x, "store", [(g, g ^ k) for g in range(groups)])

    perm, *chunks = call(
        sort_kernel,
        [((groups * CAP, n_tokens), BF16)] + [((CAP, width + rows), BF16)] * groups,
        [IN_SMEM] + [IN_VMEM] * 3,
        group.reshape(1).astype(jnp.int32),
        tokens,
        target.reshape(1, n_tokens),
        slot.reshape(1, n_tokens),
        name="sort",
    )
    chunks = [c if k == 0 else store(c, k) for k, c in enumerate(chunks)]

    blocks = base_projection_weight.reshape(quarter, 2, width, width)
    other = sibling(lax.dynamic_index_in_dim(blocks, 1 - core, 1, keepdims=False))
    other = other.reshape(quarter * width, width)

    down = adapter_down_weight.reshape(owned * rank, width)
    up = adapter_up_weight.reshape(owned * rank, width)
    down_copy, up_copy = fetch_copies(plan, [down, up], owned, group, groups)

    my_gain = lax.dynamic_slice_in_dim(gain, part * width, width, 0).reshape(1, width)
    near, far = jnp.where(core == 0, 1, 2), jnp.where(core == 0, 2, 1)
    places = jnp.stack([place, place ^ near, place ^ far, place ^ 3, core]).astype(jnp.int32)

    halves = range(groups // 2)
    state, slots, msg = [], [], []
    for h in halves:
        s, l, m = call(
            first_kernel,
            [((rows, width), BF16), ((8, rows), F32), ((rows + EXT, width), BF16)],
            [IN_VMEM] * 3,
            chunks[2 * h],
            chunks[2 * h + 1],
            my_gain,
            name="first",
        )
        state.append(s)
        slots.append(l)
        msg.append(m)
    inner = call(
        first_inner_kernel,
        ((rank, 2 * rows), F32),
        [IN_VMEM] * 6,
        msg[0],
        msg[1],
        slots[0],
        slots[1],
        down,
        down_copy,
        name="first_inner",
    )
    for k in (2, 4, 1):
        inner = inner + mp(inner, lambda i: i ^ k)

    acc = ((rows, width), F32)
    ext = ((EXT, width), F32)
    message = ((rows + EXT, width), BF16)
    work = 4 * rows * width * width

    def blocks_of(msgs, at, old, last):
        return call(
            functools.partial(block_kernel, len(msgs), at, last),
            [acc, message if last else acc, ext],
            [IN_SMEM] + [IN_VMEM] * (2 + len(msgs) + len(old)),
            places,
            base_projection_weight,
            other,
            *msgs,
            *old,
            flops=work * len(msgs),
            name="blocks",
        )

    for step in range(STEPS):
        final = step == STEPS - 1
        for h in halves:
            a = side_a(msg[h])
            b = side_b(msg[h])
            old = blocks_of([msg[h]], (0,), (), False)
            d = side_b(a)
            old = blocks_of([a, b], (1, 2), old, False)
            mine, theirs, extra = blocks_of([d], (3,), old, True)
            got = sibling(theirs)
            args = [mine, extra, got, state[h], slots[h], my_gain, down, down_copy, up, up_copy]
            if step == 0:
                args.append(inner[:, h * rows : (h + 1) * rows])
            outs = call(
                functools.partial(finish_kernel, step == 0, final, parts * width, rank),
                [((rows, width), BF16)] + ([] if final else [message]),
                [IN_VMEM] * len(args),
                *args,
                flops=work,
                name="finish",
            )
            state[h] = outs[0]
            if not final:
                msg[h] = outs[1]

    back = []
    for h in halves:
        for j in range(2):
            k = 2 * h + j
            chunk = state[h][j * CAP : (j + 1) * CAP]
            back.append(chunk if k == 0 else store(chunk, k))
    return call(
        unsort_kernel,
        ((n_tokens, width), BF16),
        [IN_VMEM] * (1 + groups),
        perm,
        *back,
        name="unsort",
    )


def plain_body(
    tokens, gain, base_projection_weight, adapter_down_weight, adapter_up_weight, plan, target, slot
):
    store_count = lax.axis_size("store")
    group = lax.axis_index("store")
    owned_adapters, rank, width = adapter_down_weight.shape
    replica_count = plan.shape[1]
    n_slots = owned_adapters + replica_count
    owner = plan // owned_adapters
    local = plan % owned_adapters
    select = jnp.logical_and(
        (owner == group)[:, :, None],
        local[:, :, None] == jnp.arange(owned_adapters, dtype=jnp.int32)[None, None, :],
    )
    select = select.astype(BF16).reshape(store_count * replica_count, owned_adapters)

    def held(own):
        send = jnp.dot(select, own.reshape(owned_adapters, rank * width), preferred_element_type=F32)
        send = send.astype(BF16).reshape(store_count, replica_count, rank * width)
        got = lax.all_to_all(send, "store", split_axis=0, concat_axis=0, tiled=True)
        got = jnp.sum(got.astype(F32), axis=0).astype(BF16)
        both = jnp.concatenate([own, got.reshape(replica_count, rank, width)], 0)
        return both.reshape(n_slots * rank, width)

    host_down, host_up = held(adapter_down_weight), held(adapter_up_weight)
    target_group = target[:, 0]
    n_tokens = target_group.shape[0]
    member = (target_group[:, None] == jnp.arange(store_count, dtype=jnp.int32)[None, :]).astype(BF16)
    order = jnp.arange(n_tokens)
    before = (order[:, None] > order[None, :]).astype(BF16)
    earlier = jnp.dot(before, member, preferred_element_type=F32)
    place = jnp.sum(earlier * member.astype(F32), axis=1).astype(jnp.int32)
    row_index = target_group * CAP + place
    slots = jnp.full((store_count * CAP,), -1, jnp.int32).at[row_index].set(slot)
    state = jnp.zeros((store_count * CAP, width), BF16).at[row_index].set(tokens)

    def exchange(x):
        return lax.all_to_all(
            x.reshape(store_count, CAP, -1), "store", split_axis=0, concat_axis=0, tiled=True
        ).reshape(store_count * CAP, -1)

    state = exchange(state)
    selected = exchange(slots) == jnp.arange(n_slots, dtype=jnp.int32)[None, :]
    total_rows = state.shape[0]
    column_start = lax.axis_index("mp") * width
    for step in range(STEPS):
        whole = lax.all_gather(state, "mp", axis=1, tiled=True)
        values = whole.astype(F32)
        mean_sq = jnp.mean(values * values, axis=1, keepdims=True)
        normed = (values * lax.rsqrt(mean_sq + EPS) * gain[None, :]).astype(BF16)
        mine = lax.dynamic_slice_in_dim(normed, column_start, width, 1)
        partial_value = lax.dot_general(mine, host_down, CONTRACT_LAST, preferred_element_type=F32)
        partial_value = jnp.sum(
            partial_value.reshape(total_rows, n_slots, rank) * selected[:, :, None].astype(F32), axis=1
        )
        inner = lax.psum(partial_value, "mp").astype(BF16)
        spread = (selected[:, :, None].astype(BF16) * inner[:, None, :]).reshape(total_rows, -1)
        outer = jnp.dot(spread, host_up, preferred_element_type=F32)
        delta = (adapter_scale * outer).astype(BF16).astype(F32)
        base = jnp.dot(normed, base_projection_weight, preferred_element_type=F32)
        state = (state.astype(F32) + base + delta).astype(BF16)
    return exchange(state)[row_index]


def solution(mesh):
    parts, groups = mesh.shape["mp"], mesh.shape["store"]

    def run(tokens, *rest):
        width = tokens.shape[1] // parts
        rank = rest[2].shape[1]
        rows = 2 * CAP
        cube = parts == 8 and groups == 4
        fits = rank % EXT == 0 and width % rows == 0 and rank // EXT + 1 <= width // rows
        return jax.shard_map(
            body if cube and fits else plain_body,
            mesh=mesh,
            in_specs=(
                P("store", "mp"),
                P(),
                P(None, "mp"),
                P("store", None, "mp"),
                P("store", None, "mp"),
                P(),
                P("store", None),
                P("store"),
            ),
            out_specs=P("store", "mp"),
            check_vma=False,
        )(tokens, *rest)

    return run
```

time: 586 us -> 229 us (0.39); the launches traced: 576 us -> 227 us
  waiting for transfers between devices: 294 us -> 34.7 us
  blocking collectives: 136 us -> 0 us
  Pallas kernels: 0 us -> 95.3 us
  starting transfers between devices: 24.4 us -> 79.5 us
  matrix products: 43.9 us -> 0 us
  other arithmetic: 29.1 us -> 2.97 us
  local copies, waits for them, and re-layouts: 33.7 us -> 14.1 us
  between operations: 14.3 us -> 0.79 us
    reduce_scatter x4 -> x0, waiting for transfers between devices: 127 us -> none  [body(): lax.psum_scatter(partial_value, 'mp', scatter_dimension=0, tiled=True)]
    all_to_all x6 -> x0, blocking collectives: 99.3 us -> none  [the longest x3 49.7 us: body(): lax.all_to_all(outer, 'store', split_axis=0, concat_axis=0, tiled=True)]
    pallas_call x0 -> x49, Pallas kernels: none -> 95.3 us  [call(): pl.pallas_call(kernel, out_shape=shapes, in_specs=specs, out_specs=[IN_VM...]
    all_gather x4 -> x0, waiting for transfers between devices: 91.2 us -> none  [body(): whole = lax.all_gather(state, 'mp', axis=1, tiled=True)]
    ppermute x0 -> x54, starting transfers between devices: none -> 79.5 us  [the longest x12 36.7 us: fetch_copies(): carry[i] = lax.ppermute(send, 'store', chain)]
    all_to_all x5 -> x0, waiting for transfers between devices: 75.1 us -> none  [the longest x1 33.9 us: body(): lax.all_to_all(send_up.reshape(store_count, replica_count, rank_position...]
    dot_general x14 -> x0, matrix products: 43.9 us -> none  [the longest x4 28.8 us: body(): jnp.dot(normed, base_projection_weight, preferred_element_type=jnp.float32)]
    all_gather x4 -> x0, blocking collectives: 37 us -> none  [body(): inner = lax.all_gather(summed_share, 'mp', axis=0, tiled=True)]
  transfers between devices with their start and end apart: 13 -> 54, of which waited for: 12 -> 13; matrix products, arithmetic and copies ran while one was open for 5% -> 2% of each run, Pallas kernels for 0% -> 41%
where the time goes in v1:
time: 229 us; the launch traced here: 227 us
  Pallas kernels  95.3 us (42%)
  starting transfers between devices  79.5 us (35%)
  waiting for transfers between devices  34.7 us (15%)
  local copies, waits for them, and re-layouts  14.1 us (6%)
  other arithmetic  2.97 us (1%)
    pallas_call x49, Pallas kernels, call(): pl.pallas_call(kernel, out_shape=shapes, in_specs=specs, out_specs=[IN_VM...  95.3 us
    ppermute x12, starting transfers between devices, fetch_copies(): carry[i] = lax.ppermute(send, 'store', chain)  36.7 us
    ppermute x36, starting transfers between devices, mp(): return lax.ppermute(x, 'mp', [(i, pairs_of(i)) for i in range(parts)])  31.6 us
    ppermute x6, waiting for transfers between devices, store(): return lax.ppermute(x, 'store', [(g, g ^ k) for g in range(groups)])  15.4 us
    ppermute x36, waiting for transfers between devices, mp(): return lax.ppermute(x, 'mp', [(i, pairs_of(i)) for i in range(parts)])  14.3 us
    ppermute x6, starting transfers between devices, store(): return lax.ppermute(x, 'store', [(g, g ^ k) for g in range(groups)])  11.2 us
    unnamed x48, local copies, waits for them, and re-layouts  8.22 us
    squeeze x1, local copies, waits for them, and re-layouts, body(): lax.dynamic_index_in_dim(blocks, 1 - core, 1, keepdims=False)  4.98 us
  transfers between devices with their start and end apart: 54, of which 13 were waited for; matrix products, arithmetic and copies ran while one was open for 2% of the time, Pallas kernels for 41%

profile of v1, /device:TPU:0, one launch (start us, length us, event | category | flops | bytes accessed | tf_op | source)
XLA Modules:
  0.0 227.3 jit_solution(6407248493965664907)
XLA Ops:
  0.0 5.0 %dynamic-slice_bitcast_fusion = bf16[4,768,768]{2,1,0:T(8,128)(2,1)} fusion(bf16[4,2,768,768]{3,2,1,0:T(8,128)(2,1)} %bitcast.20, s32[]{:T(128)S(6)} %select_n.29), kind=kLoop, calls=%fused_computation | loop fusion | bytes 9437188 | tf_op jit(solution)/shard_map/jit(dynamic_index_in_dim)/squeeze | solution.py:292
  9.2 5.2 %collective-permute-start.6 = (bf16[256,768]{1,0:T(8,128)(2,1)}, bf16[256,768]{1,0:T(8,128)(2,1)}, u32[]{:S(2)}, u32[]{:S(2)}) collective-permute-start(bf16[256,768]{1,0:T(8,128)(2,1)} %pick.12), channel_id=1, source_target_pairs={{0,8},{1,9},{2,10},{3,11},{4,12},{5,13},{6,14},{7,15}} | collective-permute-start | bytes 1179656 | tf_op jit(solution)/shard_map/ppermute | solution.py:117
  18.1 4.9 %collective-permute-done.6.carry_ref = bf16[256,768]{1,0:T(8,128)(2,1)} collective-permute-done((bf16[256,768]{1,0:T(8,128)(2,1)}, bf16[256,768]{1,0:T(8,128)(2,1)}, u32[]{:S(2)}, u32[]{:S(2)}) %collective-permute-start.6) | collective-permute-done | bytes 393248 | tf_op jit(solution)/shard_map/ppermute | solution.py:117
  23.0 1.9 pick.13
  24.9 5.1 %collective-permute-start.7 = (bf16[256,768]{1,0:T(8,128)(2,1)}, bf16[256,768]{1,0:T(8,128)(2,1)}, u32[]{:S(2)}, u32[]{:S(2)}) collective-permute-start(bf16[256,768]{1,0:T(8,128)(2,1)} %pick.13), channel_id=1, source_target_pairs={{0,8},{8,16},{1,9},{9,17},{2,10},{10,18},{3,11},{11,19},{4,12},{12... | collective-permute-start | bytes 1179656 | tf_op jit(solution)/shard_map/ppermute | solution.py:117
  31.4 5.0 %collective-permute-start.12 = (bf16[256,768]{1,0:T(8,128)(2,1)}, bf16[256,768]{1,0:T(8,128)(2,1)}, u32[]{:S(2)}, u32[]{:S(2)}) collective-permute-start(bf16[256,768]{1,0:T(8,128)(2,1)} %pick.18), channel_id=1, source_target_pairs={{0,8},{1,9},{2,10},{3,11},{4,12},{5,13},{6,14},{7,15}} | collective-permute-start | bytes 1179656 | tf_op jit(solution)/shard_map/ppermute | solution.py:117
  41.2 5.6 %collective-permute-start.19 = (bf16[64,896]{1,0:T(8,128)(2,1)}, bf16[64,896]{1,0:T(8,128)(2,1)S(1)}, u32[]{:S(2)}, u32[]{:S(2)}) collective-permute-start(bf16[64,896]{1,0:T(8,128)(2,1)} %copy-done.20), channel_id=1, source_target_pairs={{0,24},{8,16},{16,8},{24,0},{1,25},{9,17},{17,9},{25,1},{2,26},{10... | collective-permute-start | bytes 344072 | tf_op jit(solution)/shard_map/ppermute | solution.py:277
  51.2 5.3 %collective-permute-start.8 = (bf16[256,768]{1,0:T(8,128)(2,1)S(1)}, bf16[256,768]{1,0:T(8,128)(2,1)}, u32[]{:S(2)}, u32[]{:S(2)}) collective-permute-start(bf16[256,768]{1,0:T(8,128)(2,1)S(1)} %pick.14), channel_id=1, source_target_pairs={{0,8},{8,16},{16,24},{1,9},{9,17},{17,25},{2,10},{10,18},{18,26},{... | collective-permute-start | bytes 1179656 | tf_op jit(solution)/shard_map/ppermute | solution.py:117
  56.5 1.9 pick.19
  58.4 4.4 %collective-permute-start.13 = (bf16[256,768]{1,0:T(8,128)(2,1)}, bf16[256,768]{1,0:T(8,128)(2,1)}, u32[]{:S(2)}, u32[]{:S(2)}) collective-permute-start(bf16[256,768]{1,0:T(8,128)(2,1)} %pick.19), channel_id=1, source_target_pairs={{0,8},{8,16},{1,9},{9,17},{2,10},{10,18},{3,11},{11,19},{4,12},{12... | collective-permute-start | bytes 1179656 | tf_op jit(solution)/shard_map/ppermute | solution.py:117
  65.4 7.3 %collective-permute-done.1.odd_ref = bf16[64,896]{1,0:T(8,128)(2,1)S(1)} collective-permute-done((bf16[64,896]{1,0:T(8,128)(2,1)}, bf16[64,896]{1,0:T(8,128)(2,1)S(1)}, u32[]{:S(2)}, u32[]{:S(2)}) %collective-permute-start.1) | collective-permute-done | bytes 114720 | tf_op jit(solution)/shard_map/ppermute | solution.py:277
  80.3 1.6 collective-permute-start.20
  83.0 5.7 %collective-permute-start.14 = (bf16[256,768]{1,0:T(8,128)(2,1)S(1)}, bf16[256,768]{1,0:T(8,128)(2,1)}, u32[]{:S(2)}, u32[]{:S(2)}) collective-permute-start(bf16[256,768]{1,0:T(8,128)(2,1)S(1)} %pick.20), channel_id=1, source_target_pairs={{0,8},{8,16},{16,24},{1,9},{9,17},{17,25},{2,10},{10,18},{18,26},{... | collective-permute-start | bytes 1179656 | tf_op jit(solution)/shard_map/ppermute | solution.py:117
  90.7 3.9 %collective-permute-done.36.refs_0_ = bf16[144,768]{1,0:T(8,128)(2,1)S(1)} collective-permute-done((bf16[144,768]{1,0:T(8,128)(2,1)S(1)}, bf16[144,768]{1,0:T(8,128)(2,1)S(1)}, u32[]{:S(2)}, u32[]{:S(2)}) %collective-permute-start.36) | collective-permute-done | bytes 221216 | tf_op jit(solution)/shard_map/ppermute | solution.py:265
  97.1 1.5 collective-permute-start.38
  103.9 3.7 %copy-done = bf16[6144,768]{1,0:T(8,128)(2,1)S(1)} copy-done((bf16[6144,768]{1,0:T(8,128)(2,1)S(1)}, bf16[6144,768]{1,0:T(8,128)(2,1)}, u32[]{:S(2)}) %copy-start) | copy-done | bytes 9437208
  107.6 2.8 %blocks.36 = (f32[128,768]{1,0:T(8,128)S(1)}, f32[128,768]{1,0:T(8,128)S(1)}, f32[16,768]{1,0:T(8,128)S(1)}) custom-call(s32[5]{0:T(128)S(1)} %stack.41.place_ref, bf16[6144,768]{1,0:T(8,128)(2,1)S(1)} %copy-done, bf16[3072,768]{1,0:T(8,128)(2,1)} %bitcast.10.other_ref, bf16[144,768]{1,0:T(8,128)(2,1)S(1)} %get-tuple-element.117.msg1_ref.refs_0_), custom_call_target="tpu_custom_call" | custom-call | flops 301989888 | bytes 221204 | tf_op jit(solution)/shard_map/blocks/pallas_call | solution.py:31
  110.4 3.2 %blocks.37 = (f32[128,768]{1,0:T(8,128)S(1)}, f32[128,768]{1,0:T(8,128)S(1)}, f32[16,768]{1,0:T(8,128)S(1)}) custom-call(s32[5]{0:T(128)S(1)} %stack.41.place_ref, bf16[6144,768]{1,0:T(8,128)(2,1)S(1)} %copy-done, bf16[3072,768]{1,0:T(8,128)(2,1)} %bitcast.10.other_ref, bf16[144,768]{1,0:T(8,128)(2,1)S(1)} %collective-permute-done.36.refs_0_, ...), custom_call_target="tpu_custom_call" | custom-call | flops 603979776 | bytes 1277972 | tf_op jit(solution)/shard_map/blocks/pallas_call | solution.py:31
  113.6 2.9 %blocks.38 = (f32[128,768]{1,0:T(8,128)S(1)}, bf16[144,768]{1,0:T(8,128)(2,1)S(1)}, f32[16,768]{1,0:T(8,128)S(1)}) custom-call(s32[5]{0:T(128)S(1)} %stack.41.place_ref, bf16[6144,768]{1,0:T(8,128)(2,1)S(1)} %copy-done, bf16[3072,768]{1,0:T(8,128)(2,1)} %bitcast.10.other_ref, bf16[144,768]{1,0:T(8,128)(2,1)} %collective-permute-done.37.refs_0_, ...), custom_call_target="tpu_custom_call" | custom-call | flops 301989888 | bytes 1056788 | tf_op jit(solution)/shard_map/blocks/pallas_call | solution.py:31
  116.6 2.8 %blocks.24 = (f32[128,768]{1,0:T(8,128)S(1)}, f32[128,768]{1,0:T(8,128)S(1)}, f32[16,768]{1,0:T(8,128)S(1)}) custom-call(s32[5]{0:T(128)S(1)} %stack.41.place_ref, bf16[6144,768]{1,0:T(8,128)(2,1)S(1)} %copy-done, bf16[3072,768]{1,0:T(8,128)(2,1)} %bitcast.10.other_ref, bf16[144,768]{1,0:T(8,128)(2,1)S(1)} %get-tuple-element.103.refs_0_.msg0_ref), custom_call_target="tpu_custom_call" | custom-call | flops 301989888 | bytes 221204 | tf_op jit(solution)/shard_map/blocks/pallas_call | solution.py:31
  119.4 3.2 %blocks.25 = (f32[128,768]{1,0:T(8,128)S(1)}, f32[128,768]{1,0:T(8,128)S(1)}, f32[16,768]{1,0:T(8,128)S(1)}) custom-call(s32[5]{0:T(128)S(1)} %stack.41.place_ref, bf16[6144,768]{1,0:T(8,128)(2,1)S(1)} %copy-done, bf16[3072,768]{1,0:T(8,128)(2,1)} %bitcast.10.other_ref, bf16[144,768]{1,0:T(8,128)(2,1)S(1)} %collective-permute-done.2.refs_0_, ...), custom_call_target="tpu_custom_call" | custom-call | flops 603979776 | bytes 1277972 | tf_op jit(solution)/shard_map/blocks/pallas_call | solution.py:31
  122.6 3.0 %blocks.26 = (f32[128,768]{1,0:T(8,128)S(1)}, bf16[144,768]{1,0:T(8,128)(2,1)S(1)}, f32[16,768]{1,0:T(8,128)S(1)}) custom-call(s32[5]{0:T(128)S(1)} %stack.41.place_ref, bf16[6144,768]{1,0:T(8,128)(2,1)S(1)} %copy-done, bf16[3072,768]{1,0:T(8,128)(2,1)} %bitcast.10.other_ref, bf16[144,768]{1,0:T(8,128)(2,1)S(1)} %collective-permute-done.3.refs_0_, ...), custom_call_target="tpu_custom_call" | custom-call | flops 301989888 | bytes 1056788 | tf_op jit(solution)/shard_map/blocks/pallas_call | solution.py:31
  128.6 1.5 collective-permute-start.23
  131.3 2.7 %collective-permute-done.40.refs_0_ = bf16[144,768]{1,0:T(8,128)(2,1)S(1)} collective-permute-done((bf16[144,768]{1,0:T(8,128)(2,1)S(1)}, bf16[144,768]{1,0:T(8,128)(2,1)S(1)}, u32[]{:S(2)}, u32[]{:S(2)}) %collective-permute-start.40) | collective-permute-done | bytes 221216 | tf_op jit(solution)/shard_map/ppermute | solution.py:265
  136.0 2.8 %blocks.39 = (f32[128,768]{1,0:T(8,128)S(1)}, f32[128,768]{1,0:T(8,128)S(1)}, f32[16,768]{1,0:T(8,128)S(1)}) custom-call(s32[5]{0:T(128)S(1)} %stack.41.place_ref, bf16[6144,768]{1,0:T(8,128)(2,1)S(1)} %bitcast.22, bf16[3072,768]{1,0:T(8,128)(2,1)} %bitcast.10.other_ref, bf16[144,768]{1,0:T(8,128)(2,1)S(1)} %get-tuple-element.162.refs_0_), custom_call_target="tpu_custom_call" | custom-call | flops 301989888 | bytes 221204 | tf_op jit(solution)/shard_map/blocks/pallas_call | solution.py:31
  140.1 3.2 %blocks.40 = (f32[128,768]{1,0:T(8,128)S(1)}, f32[128,768]{1,0:T(8,128)S(1)}, f32[16,768]{1,0:T(8,128)S(1)}) custom-call(s32[5]{0:T(128)S(1)} %stack.41.place_ref, bf16[6144,768]{1,0:T(8,128)(2,1)S(1)} %bitcast.22, bf16[3072,768]{1,0:T(8,128)(2,1)} %bitcast.10.other_ref, bf16[144,768]{1,0:T(8,128)(2,1)S(1)} %collective-permute-done.40.refs_0_, ...), custom_call_target="tpu_custom_call" | custom-call | flops 603979776 | bytes 1277972 | tf_op jit(solution)/shard_map/blocks/pallas_call | solution.py:31
  143.3 2.9 %blocks.41 = (f32[128,768]{1,0:T(8,128)S(1)}, bf16[144,768]{1,0:T(8,128)(2,1)S(1)}, f32[16,768]{1,0:T(8,128)S(1)}) custom-call(s32[5]{0:T(128)S(1)} %stack.41.place_ref, bf16[6144,768]{1,0:T(8,128)(2,1)S(1)} %bitcast.22, bf16[3072,768]{1,0:T(8,128)(2,1)} %bitcast.10.other_ref, bf16[144,768]{1,0:T(8,128)(2,1)S(1)} %collective-permute-done.41.refs_0_, ...), custom_call_target="tpu_custom_call" | custom-call | flops 301989888 | bytes 1056788 | tf_op jit(solution)/shard_map/blocks/pallas_call | solution.py:31
  146.2 2.9 %blocks.27 = (f32[128,768]{1,0:T(8,128)S(1)}, f32[128,768]{1,0:T(8,128)S(1)}, f32[16,768]{1,0:T(8,128)S(1)}) custom-call(s32[5]{0:T(128)S(1)} %stack.41.place_ref, bf16[6144,768]{1,0:T(8,128)(2,1)S(1)} %bitcast.22, bf16[3072,768]{1,0:T(8,128)(2,1)} %bitcast.10.other_ref, bf16[144,768]{1,0:T(8,128)(2,1)S(1)} %get-tuple-element.119.refs_0_), custom_call_target="tpu_custom_call" | custom-call | flops 301989888 | bytes 221204 | tf_op jit(solution)/shard_map/blocks/pallas_call | solution.py:31
  149.1 3.2 %blocks.28 = (f32[128,768]{1,0:T(8,128)S(1)}, f32[128,768]{1,0:T(8,128)S(1)}, f32[16,768]{1,0:T(8,128)S(1)}) custom-call(s32[5]{0:T(128)S(1)} %stack.41.place_ref, bf16[6144,768]{1,0:T(8,128)(2,1)S(1)} %bitcast.22, bf16[3072,768]{1,0:T(8,128)(2,1)} %bitcast.10.other_ref, bf16[144,768]{1,0:T(8,128)(2,1)S(1)} %collective-permute-done.23.refs_0_, ...), custom_call_target="tpu_custom_call" | custom-call | flops 603979776 | bytes 1277972 | tf_op jit(solution)/shard_map/blocks/pallas_call | solution.py:31
  152.3 2.9 %blocks.29 = (f32[128,768]{1,0:T(8,128)S(1)}, bf16[144,768]{1,0:T(8,128)(2,1)S(1)}, f32[16,768]{1,0:T(8,128)S(1)}) custom-call(s32[5]{0:T(128)S(1)} %stack.41.place_ref, bf16[6144,768]{1,0:T(8,128)(2,1)S(1)} %bitcast.22, bf16[3072,768]{1,0:T(8,128)(2,1)} %bitcast.10.other_ref, bf16[144,768]{1,0:T(8,128)(2,1)S(1)} %collective-permute-done.24.refs_0_, ...), custom_call_target="tpu_custom_call" | custom-call | flops 301989888 | bytes 1056788 | tf_op jit(solution)/shard_map/blocks/pallas_call | solution.py:31
  158.0 1.6 collective-permute-start.27
  160.5 2.9 %collective-permute-done.44.refs_0_ = bf16[144,768]{1,0:T(8,128)(2,1)S(1)} collective-permute-done((bf16[144,768]{1,0:T(8,128)(2,1)S(1)}, bf16[144,768]{1,0:T(8,128)(2,1)S(1)}, u32[]{:S(2)}, u32[]{:S(2)}) %collective-permute-start.44) | collective-permute-done | bytes 221216 | tf_op jit(solution)/shard_map/ppermute | solution.py:265
  165.5 2.8 %blocks.42 = (f32[128,768]{1,0:T(8,128)S(1)}, f32[128,768]{1,0:T(8,128)S(1)}, f32[16,768]{1,0:T(8,128)S(1)}) custom-call(s32[5]{0:T(128)S(1)} %stack.41.place_ref, bf16[6144,768]{1,0:T(8,128)(2,1)S(1)} %bitcast.22, bf16[3072,768]{1,0:T(8,128)(2,1)} %bitcast.10.other_ref, bf16[144,768]{1,0:T(8,128)(2,1)S(1)} %get-tuple-element.173.refs_0_), custom_call_target="tpu_custom_call" | custom-call | flops 301989888 | bytes 221204 | tf_op jit(solution)/shard_map/blocks/pallas_call | solution.py:31
  169.3 3.3 %blocks.43 = (f32[128,768]{1,0:T(8,128)S(1)}, f32[128,768]{1,0:T(8,128)S(1)}, f32[16,768]{1,0:T(8,128)S(1)}) custom-call(s32[5]{0:T(128)S(1)} %stack.41.place_ref, bf16[6144,768]{1,0:T(8,128)(2,1)S(1)} %bitcast.22, bf16[3072,768]{1,0:T(8,128)(2,1)} %bitcast.10.other_ref, bf16[144,768]{1,0:T(8,128)(2,1)S(1)} %collective-permute-done.44.refs_0_, ...), custom_call_target="tpu_custom_call" | custom-call | flops 603979776 | bytes 1277972 | tf_op jit(solution)/shard_map/blocks/pallas_call | solution.py:31
  172.6 2.8 %blocks.44 = (f32[128,768]{1,0:T(8,128)S(1)}, bf16[144,768]{1,0:T(8,128)(2,1)S(1)}, f32[16,768]{1,0:T(8,128)S(1)}) custom-call(s32[5]{0:T(128)S(1)} %stack.41.place_ref, bf16[6144,768]{1,0:T(8,128)(2,1)S(1)} %bitcast.22, bf16[3072,768]{1,0:T(8,128)(2,1)} %bitcast.10.other_ref, bf16[144,768]{1,0:T(8,128)(2,1)S(1)} %collective-permute-done.45.refs_0_, ...), custom_call_target="tpu_custom_call" | custom-call | flops 301989888 | bytes 1056788 | tf_op jit(solution)/shard_map/blocks/pallas_call | solution.py:31
  175.6 2.9 %blocks.30 = (f32[128,768]{1,0:T(8,128)S(1)}, f32[128,768]{1,0:T(8,128)S(1)}, f32[16,768]{1,0:T(8,128)S(1)}) custom-call(s32[5]{0:T(128)S(1)} %stack.41.place_ref, bf16[6144,768]{1,0:T(8,128)(2,1)S(1)} %bitcast.22, bf16[3072,768]{1,0:T(8,128)(2,1)} %bitcast.10.other_ref, bf16[144,768]{1,0:T(8,128)(2,1)S(1)} %get-tuple-element.130.refs_0_), custom_call_target="tpu_custom_call" | custom-call | flops 301989888 | bytes 221204 | tf_op jit(solution)/shard_map/blocks/pallas_call | solution.py:31
  178.4 3.2 %blocks.31 = (f32[128,768]{1,0:T(8,128)S(1)}, f32[128,768]{1,0:T(8,128)S(1)}, f32[16,768]{1,0:T(8,128)S(1)}) custom-call(s32[5]{0:T(128)S(1)} %stack.41.place_ref, bf16[6144,768]{1,0:T(8,128)(2,1)S(1)} %bitcast.22, bf16[3072,768]{1,0:T(8,128)(2,1)} %bitcast.10.other_ref, bf16[144,768]{1,0:T(8,128)(2,1)S(1)} %collective-permute-done.27.refs_0_, ...), custom_call_target="tpu_custom_call" | custom-call | flops 603979776 | bytes 1277972 | tf_op jit(solution)/shard_map/blocks/pallas_call | solution.py:31
  181.6 2.9 %blocks.32 = (f32[128,768]{1,0:T(8,128)S(1)}, bf16[144,768]{1,0:T(8,128)(2,1)S(1)}, f32[16,768]{1,0:T(8,128)S(1)}) custom-call(s32[5]{0:T(128)S(1)} %stack.41.place_ref, bf16[6144,768]{1,0:T(8,128)(2,1)S(1)} %bitcast.22, bf16[3072,768]{1,0:T(8,128)(2,1)} %bitcast.10.other_ref, bf16[144,768]{1,0:T(8,128)(2,1)S(1)} %collective-permute-done.28.refs_0_, ...), custom_call_target="tpu_custom_call" | custom-call | flops 301989888 | bytes 1056788 | tf_op jit(solution)/shard_map/blocks/pallas_call | solution.py:31
  187.0 1.9 collective-permute-start.31
  190.1 2.7 %collective-permute-done.48.refs_0_ = bf16[144,768]{1,0:T(8,128)(2,1)S(1)} collective-permute-done((bf16[144,768]{1,0:T(8,128)(2,1)S(1)}, bf16[144,768]{1,0:T(8,128)(2,1)S(1)}, u32[]{:S(2)}, u32[]{:S(2)}) %collective-permute-start.48) | collective-permute-done | bytes 221216 | tf_op jit(solution)/shard_map/ppermute | solution.py:265
  194.8 2.9 %blocks.45 = (f32[128,768]{1,0:T(8,128)S(1)}, f32[128,768]{1,0:T(8,128)S(1)}, f32[16,768]{1,0:T(8,128)S(1)}) custom-call(s32[5]{0:T(128)S(1)} %stack.41.place_ref, bf16[6144,768]{1,0:T(8,128)(2,1)S(1)} %bitcast.22, bf16[3072,768]{1,0:T(8,128)(2,1)} %bitcast.10.other_ref, bf16[144,768]{1,0:T(8,128)(2,1)S(1)} %get-tuple-element.184.refs_0_), custom_call_target="tpu_custom_call" | custom-call | flops 301989888 | bytes 221204 | tf_op jit(solution)/shard_map/blocks/pallas_call | solution.py:31
  198.8 3.2 %blocks.46 = (f32[128,768]{1,0:T(8,128)S(1)}, f32[128,768]{1,0:T(8,128)S(1)}, f32[16,768]{1,0:T(8,128)S(1)}) custom-call(s32[5]{0:T(128)S(1)} %stack.41.place_ref, bf16[6144,768]{1,0:T(8,128)(2,1)S(1)} %bitcast.22, bf16[3072,768]{1,0:T(8,128)(2,1)} %bitcast.10.other_ref, bf16[144,768]{1,0:T(8,128)(2,1)S(1)} %collective-permute-done.48.refs_0_, ...), custom_call_target="tpu_custom_call" | custom-call | flops 603979776 | bytes 1277972 | tf_op jit(solution)/shard_map/blocks/pallas_call | solution.py:31
  202.0 2.8 %blocks.47 = (f32[128,768]{1,0:T(8,128)S(1)}, bf16[144,768]{1,0:T(8,128)(2,1)S(1)}, f32[16,768]{1,0:T(8,128)S(1)}) custom-call(s32[5]{0:T(128)S(1)} %stack.41.place_ref, bf16[6144,768]{1,0:T(8,128)(2,1)S(1)} %bitcast.22, bf16[3072,768]{1,0:T(8,128)(2,1)} %bitcast.10.other_ref, bf16[144,768]{1,0:T(8,128)(2,1)S(1)} %collective-permute-done.49.refs_0_, ...), custom_call_target="tpu_custom_call" | custom-call | flops 301989888 | bytes 1056788 | tf_op jit(solution)/shard_map/blocks/pallas_call | solution.py:31
  205.0 2.9 %blocks.33 = (f32[128,768]{1,0:T(8,128)S(1)}, f32[128,768]{1,0:T(8,128)S(1)}, f32[16,768]{1,0:T(8,128)S(1)}) custom-call(s32[5]{0:T(128)S(1)} %stack.41.place_ref, bf16[6144,768]{1,0:T(8,128)(2,1)S(1)} %bitcast.22, bf16[3072,768]{1,0:T(8,128)(2,1)} %bitcast.10.other_ref, bf16[144,768]{1,0:T(8,128)(2,1)S(1)} %get-tuple-element.141.refs_0_), custom_call_target="tpu_custom_call" | custom-call | flops 301989888 | bytes 221204 | tf_op jit(solution)/shard_map/blocks/pallas_call | solution.py:31
  207.8 3.2 %blocks.34 = (f32[128,768]{1,0:T(8,128)S(1)}, f32[128,768]{1,0:T(8,128)S(1)}, f32[16,768]{1,0:T(8,128)S(1)}) custom-call(s32[5]{0:T(128)S(1)} %stack.41.place_ref, bf16[6144,768]{1,0:T(8,128)(2,1)S(1)} %bitcast.22, bf16[3072,768]{1,0:T(8,128)(2,1)} %bitcast.10.other_ref, bf16[144,768]{1,0:T(8,128)(2,1)S(1)} %collective-permute-done.31.refs_0_, ...), custom_call_target="tpu_custom_call" | custom-call | flops 603979776 | bytes 1277972 | tf_op jit(solution)/shard_map/blocks/pallas_call | solution.py:31
  211.0 2.9 %blocks.35 = (f32[128,768]{1,0:T(8,128)S(1)}, bf16[144,768]{1,0:T(8,128)(2,1)S(1)}, f32[16,768]{1,0:T(8,128)S(1)}) custom-call(s32[5]{0:T(128)S(1)} %stack.41.place_ref, bf16[6144,768]{1,0:T(8,128)(2,1)S(1)} %bitcast.22, bf16[3072,768]{1,0:T(8,128)(2,1)} %bitcast.10.other_ref, bf16[144,768]{1,0:T(8,128)(2,1)S(1)} %collective-permute-done.32.refs_0_, ...), custom_call_target="tpu_custom_call" | custom-call | flops 301989888 | bytes 1056788 | tf_op jit(solution)/shard_map/blocks/pallas_call | solution.py:31
  215.9 2.9 %collective-permute-start.53 = (bf16[64,768]{1,0:T(8,128)(2,1)S(1)}, bf16[64,768]{1,0:T(8,128)(2,1)S(1)}, u32[]{:S(2)}, u32[]{:S(2)}) collective-permute-start(bf16[64,768]{1,0:T(8,128)(2,1)S(1)} %get-tuple-element.195), channel_id=1, source_target_pairs={{0,24},{8,16},{16,8},{24,0},{1,25},{9,17},{17,9},{25,1},{2,26},{10... | collective-permute-start | bytes 294920 | tf_op jit(solution)/shard_map/ppermute | solution.py:277
  219.3 6.4 %collective-permute-done.52.refs_2_ = bf16[64,768]{1,0:T(8,128)(2,1)S(1)} collective-permute-done((bf16[64,768]{1,0:T(8,128)(2,1)S(1)}, bf16[64,768]{1,0:T(8,128)(2,1)S(1)}, u32[]{:S(2)}, u32[]{:S(2)}) %collective-permute-start.52) | collective-permute-done | bytes 98336 | tf_op jit(solution)/shard_map/ppermute | solution.py:277
  (177 shorter events, 64.8 us)
Async XLA Ops:
  5.0 98.9 %collective-permute-start = (bf16[4,768,768]{2,1,0:T(8,128)(2,1)}, bf16[4,768,768]{2,1,0:T(8,128)(2,1)}, u32[]{:S(2)}, u32[]{:S(2)}) collective-permute-start(bf16[4,768,768]{2,1,0:T(8,128)(2,1)} %dynamic-slice_bitcast_fusion), channel_id=1, source_target_pairs={{0,1},{1,0},{2,3},{3,2},{4,5},{5,4},{6,7},{7,6},{8,9},{9,8},{10,11... | collective-permute-start | bytes 14155784 | tf_op jit(solution)/shard_map/ppermute | solution.py:265
  7.0 8.9 %collective-permute-start.9 = (bf16[256,768]{1,0:T(8,128)(2,1)}, bf16[256,768]{1,0:T(8,128)(2,1)S(1)}, u32[]{:S(2)}, u32[]{:S(2)}) collective-permute-start(bf16[256,768]{1,0:T(8,128)(2,1)} %pick.15), channel_id=1, source_target_pairs={{24,16},{25,17},{26,18},{27,19},{28,20},{29,21},{30,22},{31,23}} | collective-permute-start | bytes 1179656 | tf_op jit(solution)/shard_map/ppermute | solution.py:117
  9.2 13.8 %collective-permute-start.6 = (bf16[256,768]{1,0:T(8,128)(2,1)}, bf16[256,768]{1,0:T(8,128)(2,1)}, u32[]{:S(2)}, u32[]{:S(2)}) collective-permute-start(bf16[256,768]{1,0:T(8,128)(2,1)} %pick.12), channel_id=1, source_target_pairs={{0,8},{1,9},{2,10},{3,11},{4,12},{5,13},{6,14},{7,15}} | collective-permute-start | bytes 1179656 | tf_op jit(solution)/shard_map/ppermute | solution.py:117
  15.1 23.8 %collective-permute-start.15 = (bf16[256,768]{1,0:T(8,128)(2,1)S(1)}, bf16[256,768]{1,0:T(8,128)(2,1)S(1)}, u32[]{:S(2)}, u32[]{:S(2)}) collective-permute-start(bf16[256,768]{1,0:T(8,128)(2,1)S(1)} %pick.21), channel_id=1, source_target_pairs={{24,16},{25,17},{26,18},{27,19},{28,20},{29,21},{30,22},{31,23}} | collective-permute-start | bytes 1179656 | tf_op jit(solution)/shard_map/ppermute | solution.py:117
  17.3 22.3 %collective-permute-start.10 = (bf16[256,768]{1,0:T(8,128)(2,1)}, bf16[256,768]{1,0:T(8,128)(2,1)S(1)}, u32[]{:S(2)}, u32[]{:S(2)}) collective-permute-start(bf16[256,768]{1,0:T(8,128)(2,1)} %pick.16), channel_id=1, source_target_pairs={{24,16},{16,8},{25,17},{17,9},{26,18},{18,10},{27,19},{19,11},{28,... | collective-permute-start | bytes 1179656 | tf_op jit(solution)/shard_map/ppermute | solution.py:117
  24.9 16.3 %collective-permute-start.7 = (bf16[256,768]{1,0:T(8,128)(2,1)}, bf16[256,768]{1,0:T(8,128)(2,1)}, u32[]{:S(2)}, u32[]{:S(2)}) collective-permute-start(bf16[256,768]{1,0:T(8,128)(2,1)} %pick.13), channel_id=1, source_target_pairs={{0,8},{8,16},{1,9},{9,17},{2,10},{10,18},{3,11},{11,19},{4,12},{12... | collective-permute-start | bytes 1179656 | tf_op jit(solution)/shard_map/ppermute | solution.py:117
  31.4 19.8 %collective-permute-start.12 = (bf16[256,768]{1,0:T(8,128)(2,1)}, bf16[256,768]{1,0:T(8,128)(2,1)}, u32[]{:S(2)}, u32[]{:S(2)}) collective-permute-start(bf16[256,768]{1,0:T(8,128)(2,1)} %pick.18), channel_id=1, source_target_pairs={{0,8},{1,9},{2,10},{3,11},{4,12},{5,13},{6,14},{7,15}} | collective-permute-start | bytes 1179656 | tf_op jit(solution)/shard_map/ppermute | solution.py:117
  38.9 11.0 %collective-permute-start.18 = (bf16[64,896]{1,0:T(8,128)(2,1)}, bf16[64,896]{1,0:T(8,128)(2,1)S(1)}, u32[]{:S(2)}, u32[]{:S(2)}) collective-permute-start(bf16[64,896]{1,0:T(8,128)(2,1)} %get-tuple-element.115), channel_id=1, source_target_pairs={{0,16},{8,24},{16,0},{24,8},{1,17},{9,25},{17,1},{25,9},{2,18},{10... | collective-permute-start | bytes 344072 | tf_op jit(solution)/shard_map/ppermute | solution.py:277
  39.7 23.1 %collective-permute-start.16 = (bf16[256,768]{1,0:T(8,128)(2,1)S(1)}, bf16[256,768]{1,0:T(8,128)(2,1)}, u32[]{:S(2)}, u32[]{:S(2)}) collective-permute-start(bf16[256,768]{1,0:T(8,128)(2,1)S(1)} %pick.22), channel_id=1, source_target_pairs={{24,16},{16,8},{25,17},{17,9},{26,18},{18,10},{27,19},{19,11},{28,... | collective-permute-start | bytes 1179656 | tf_op jit(solution)/shard_map/ppermute | solution.py:117
  41.2 17.2 %collective-permute-start.19 = (bf16[64,896]{1,0:T(8,128)(2,1)}, bf16[64,896]{1,0:T(8,128)(2,1)S(1)}, u32[]{:S(2)}, u32[]{:S(2)}) collective-permute-start(bf16[64,896]{1,0:T(8,128)(2,1)} %copy-done.20), channel_id=1, source_target_pairs={{0,24},{8,16},{16,8},{24,0},{1,25},{9,17},{17,9},{25,1},{2,26},{10... | collective-permute-start | bytes 344072 | tf_op jit(solution)/shard_map/ppermute | solution.py:277
  49.9 28.3 %collective-permute-start.11 = (bf16[256,768]{1,0:T(8,128)(2,1)S(1)}, bf16[256,768]{1,0:T(8,128)(2,1)}, u32[]{:S(2)}, u32[]{:S(2)}) collective-permute-start(bf16[256,768]{1,0:T(8,128)(2,1)S(1)} %pick.17), channel_id=1, source_target_pairs={{24,16},{16,8},{8,0},{25,17},{17,9},{9,1},{26,18},{18,10},{10,2},{... | collective-permute-start | bytes 1179656 | tf_op jit(solution)/shard_map/ppermute | solution.py:117
  51.2 27.0 %collective-permute-start.8 = (bf16[256,768]{1,0:T(8,128)(2,1)S(1)}, bf16[256,768]{1,0:T(8,128)(2,1)}, u32[]{:S(2)}, u32[]{:S(2)}) collective-permute-start(bf16[256,768]{1,0:T(8,128)(2,1)S(1)} %pick.14), channel_id=1, source_target_pairs={{0,8},{8,16},{16,24},{1,9},{9,17},{17,25},{2,10},{10,18},{18,26},{... | collective-permute-start | bytes 1179656 | tf_op jit(solution)/shard_map/ppermute | solution.py:117
  58.4 23.4 %collective-permute-start.13 = (bf16[256,768]{1,0:T(8,128)(2,1)}, bf16[256,768]{1,0:T(8,128)(2,1)}, u32[]{:S(2)}, u32[]{:S(2)}) collective-permute-start(bf16[256,768]{1,0:T(8,128)(2,1)} %pick.19), channel_id=1, source_target_pairs={{0,8},{8,16},{1,9},{9,17},{2,10},{10,18},{3,11},{11,19},{4,12},{12... | collective-permute-start | bytes 1179656 | tf_op jit(solution)/shard_map/ppermute | solution.py:117
  62.8 9.9 %collective-permute-start.1 = (bf16[64,896]{1,0:T(8,128)(2,1)}, bf16[64,896]{1,0:T(8,128)(2,1)S(1)}, u32[]{:S(2)}, u32[]{:S(2)}) collective-permute-start(bf16[64,896]{1,0:T(8,128)(2,1)} %copy-done.19), channel_id=1, source_target_pairs={{0,8},{8,0},{16,24},{24,16},{1,9},{9,1},{17,25},{25,17},{2,10},{10... | collective-permute-start | bytes 344072 | tf_op jit(solution)/shard_map/ppermute | solution.py:277
  73.3 27.1 %collective-permute-start.17 = (bf16[256,768]{1,0:T(8,128)(2,1)S(1)}, bf16[256,768]{1,0:T(8,128)(2,1)}, u32[]{:S(2)}, u32[]{:S(2)}) collective-permute-start(bf16[256,768]{1,0:T(8,128)(2,1)S(1)} %pick.23), channel_id=1, source_target_pairs={{24,16},{16,8},{8,0},{25,17},{17,9},{9,1},{26,18},{18,10},{10,2},{... | collective-permute-start | bytes 1179656 | tf_op jit(solution)/shard_map/ppermute | solution.py:117
  80.3 8.9 %collective-permute-start.20 = (f32[64,256]{1,0:T(8,128)S(1)}, f32[64,256]{1,0:T(8,128)S(1)}, u32[]{:S(2)}, u32[]{:S(2)}) collective-permute-start(f32[64,256]{1,0:T(8,128)S(1)} %first_inner.1), channel_id=1, source_target_pairs={{0,2},{1,3},{2,0},{3,1},{4,6},{5,7},{6,4},{7,5},{8,10},{9,11},{10,... | collective-permute-start | bytes 196616 | tf_op jit(solution)/shard_map/ppermute | solution.py:265
  83.0 17.5 %collective-permute-start.14 = (bf16[256,768]{1,0:T(8,128)(2,1)S(1)}, bf16[256,768]{1,0:T(8,128)(2,1)}, u32[]{:S(2)}, u32[]{:S(2)}) collective-permute-start(bf16[256,768]{1,0:T(8,128)(2,1)S(1)} %pick.20), channel_id=1, source_target_pairs={{0,8},{8,16},{16,24},{1,9},{9,17},{17,25},{2,10},{10,18},{18,26},{... | collective-permute-start | bytes 1179656 | tf_op jit(solution)/shard_map/ppermute | solution.py:117
  88.6 5.9 %collective-permute-start.36 = (bf16[144,768]{1,0:T(8,128)(2,1)S(1)}, bf16[144,768]{1,0:T(8,128)(2,1)S(1)}, u32[]{:S(2)}, u32[]{:S(2)}) collective-permute-start(bf16[144,768]{1,0:T(8,128)(2,1)S(1)} %get-tuple-element.117.msg1_ref.refs_0_), channel_id=1, source_target_pairs={{0,2},{1,5},{2,0},{3,7},{4,6},{5,1},{6,4},{7,3},{8,10},{9,13},{10,... | collective-permute-start | bytes 663560 | tf_op jit(solution)/shard_map/ppermute | solution.py:265
  89.2 8.0 %collective-permute-start.2 = (bf16[144,768]{1,0:T(8,128)(2,1)S(1)}, bf16[144,768]{1,0:T(8,128)(2,1)S(1)}, u32[]{:S(2)}, u32[]{:S(2)}) collective-permute-start(bf16[144,768]{1,0:T(8,128)(2,1)S(1)} %get-tuple-element.103.refs_0_.msg0_ref), channel_id=1, source_target_pairs={{0,2},{1,5},{2,0},{3,7},{4,6},{5,1},{6,4},{7,3},{8,10},{9,13},{10,... | collective-permute-start | bytes 663560 | tf_op jit(solution)/shard_map/ppermute | solution.py:265
  97.1 13.3 %collective-permute-start.38 = (bf16[144,768]{1,0:T(8,128)(2,1)S(1)}, bf16[144,768]{1,0:T(8,128)(2,1)}, u32[]{:S(2)}, u32[]{:S(2)}) collective-permute-start(bf16[144,768]{1,0:T(8,128)(2,1)S(1)} %get-tuple-element.117.msg1_ref.refs_0_), channel_id=1, source_target_pairs={{0,4},{1,3},{2,6},{3,1},{4,0},{5,7},{6,2},{7,5},{8,12},{9,11},{10,... | collective-permute-start | bytes 663560 | tf_op jit(solution)/shard_map/ppermute | solution.py:265
  98.8 14.8 %collective-permute-start.37 = (bf16[144,768]{1,0:T(8,128)(2,1)S(1)}, bf16[144,768]{1,0:T(8,128)(2,1)}, u32[]{:S(2)}, u32[]{:S(2)}) collective-permute-start(bf16[144,768]{1,0:T(8,128)(2,1)S(1)} %collective-permute-done.36.refs_0_), channel_id=1, source_target_pairs={{0,4},{1,3},{2,6},{3,1},{4,0},{5,7},{6,2},{7,5},{8,12},{9,11},{10,... | collective-permute-start | bytes 663560 | tf_op jit(solution)/shard_map/ppermute | solution.py:265
  100.5 18.9 %collective-permute-start.4 = (bf16[144,768]{1,0:T(8,128)(2,1)S(1)}, bf16[144,768]{1,0:T(8,128)(2,1)}, u32[]{:S(2)}, u32[]{:S(2)}) collective-permute-start(bf16[144,768]{1,0:T(8,128)(2,1)S(1)} %get-tuple-element.103.refs_0_.msg0_ref), channel_id=1, source_target_pairs={{0,4},{1,3},{2,6},{3,1},{4,0},{5,7},{6,2},{7,5},{8,12},{9,11},{10,... | collective-permute-start | bytes 663560 | tf_op jit(solution)/shard_map/ppermute | solution.py:265
  101.7 20.9 %collective-permute-start.3 = (bf16[144,768]{1,0:T(8,128)(2,1)S(1)}, bf16[144,768]{1,0:T(8,128)(2,1)S(1)}, u32[]{:S(2)}, u32[]{:S(2)}) collective-permute-start(bf16[144,768]{1,0:T(8,128)(2,1)S(1)} %collective-permute-done.2.refs_0_), channel_id=1, source_target_pairs={{0,4},{1,3},{2,6},{3,1},{4,0},{5,7},{6,2},{7,5},{8,12},{9,11},{10,... | collective-permute-start | bytes 663560 | tf_op jit(solution)/shard_map/ppermute | solution.py:265
  116.5 9.7 %collective-permute-start.39 = (bf16[144,768]{1,0:T(8,128)(2,1)S(1)}, bf16[144,768]{1,0:T(8,128)(2,1)S(1)}, u32[]{:S(2)}, u32[]{:S(2)}) collective-permute-start(bf16[144,768]{1,0:T(8,128)(2,1)S(1)} %get-tuple-element.160), channel_id=1, source_target_pairs={{0,1},{1,0},{2,3},{3,2},{4,5},{5,4},{6,7},{7,6},{8,9},{9,8},{10,11... | collective-permute-start | bytes 663560 | tf_op jit(solution)/shard_map/ppermute | solution.py:265
  127.1 6.9 %collective-permute-start.40 = (bf16[144,768]{1,0:T(8,128)(2,1)S(1)}, bf16[144,768]{1,0:T(8,128)(2,1)S(1)}, u32[]{:S(2)}, u32[]{:S(2)}) collective-permute-start(bf16[144,768]{1,0:T(8,128)(2,1)S(1)} %get-tuple-element.162.refs_0_), channel_id=1, source_target_pairs={{0,2},{1,5},{2,0},{3,7},{4,6},{5,1},{6,4},{7,3},{8,10},{9,13},{10,... | collective-permute-start | bytes 663560 | tf_op jit(solution)/shard_map/ppermute | solution.py:265
  128.6 10.3 %collective-permute-start.23 = (bf16[144,768]{1,0:T(8,128)(2,1)S(1)}, bf16[144,768]{1,0:T(8,128)(2,1)S(1)}, u32[]{:S(2)}, u32[]{:S(2)}) collective-permute-start(bf16[144,768]{1,0:T(8,128)(2,1)S(1)} %get-tuple-element.119.refs_0_), channel_id=1, source_target_pairs={{0,2},{1,5},{2,0},{3,7},{4,6},{5,1},{6,4},{7,3},{8,10},{9,13},{10,... | collective-permute-start | bytes 663560 | tf_op jit(solution)/shard_map/ppermute | solution.py:265
  130.2 9.9 %collective-permute-start.42 = (bf16[144,768]{1,0:T(8,128)(2,1)S(1)}, bf16[144,768]{1,0:T(8,128)(2,1)S(1)}, u32[]{:S(2)}, u32[]{:S(2)}) collective-permute-start(bf16[144,768]{1,0:T(8,128)(2,1)S(1)} %get-tuple-element.162.refs_0_), channel_id=1, source_target_pairs={{0,4},{1,3},{2,6},{3,1},{4,0},{5,7},{6,2},{7,5},{8,12},{9,11},{10,... | collective-permute-start | bytes 663560 | tf_op jit(solution)/shard_map/ppermute | solution.py:265
  134.0 9.3 %collective-permute-start.41 = (bf16[144,768]{1,0:T(8,128)(2,1)S(1)}, bf16[144,768]{1,0:T(8,128)(2,1)S(1)}, u32[]{:S(2)}, u32[]{:S(2)}) collective-permute-start(bf16[144,768]{1,0:T(8,128)(2,1)S(1)} %collective-permute-done.40.refs_0_), channel_id=1, source_target_pairs={{0,4},{1,3},{2,6},{3,1},{4,0},{5,7},{6,2},{7,5},{8,12},{9,11},{10,... | collective-permute-start | bytes 663560 | tf_op jit(solution)/shard_map/ppermute | solution.py:265
  135.1 14.0 %collective-permute-start.25 = (bf16[144,768]{1,0:T(8,128)(2,1)S(1)}, bf16[144,768]{1,0:T(8,128)(2,1)S(1)}, u32[]{:S(2)}, u32[]{:S(2)}) collective-permute-start(bf16[144,768]{1,0:T(8,128)(2,1)S(1)} %get-tuple-element.119.refs_0_), channel_id=1, source_target_pairs={{0,4},{1,3},{2,6},{3,1},{4,0},{5,7},{6,2},{7,5},{8,12},{9,11},{10,... | collective-permute-start | bytes 663560 | tf_op jit(solution)/shard_map/ppermute | solution.py:265
  138.9 13.4 %collective-permute-start.24 = (bf16[144,768]{1,0:T(8,128)(2,1)S(1)}, bf16[144,768]{1,0:T(8,128)(2,1)S(1)}, u32[]{:S(2)}, u32[]{:S(2)}) collective-permute-start(bf16[144,768]{1,0:T(8,128)(2,1)S(1)} %collective-permute-done.23.refs_0_), channel_id=1, source_target_pairs={{0,4},{1,3},{2,6},{3,1},{4,0},{5,7},{6,2},{7,5},{8,12},{9,11},{10,... | collective-permute-start | bytes 663560 | tf_op jit(solution)/shard_map/ppermute | solution.py:265
  146.1 9.6 %collective-permute-start.43 = (bf16[144,768]{1,0:T(8,128)(2,1)S(1)}, bf16[144,768]{1,0:T(8,128)(2,1)S(1)}, u32[]{:S(2)}, u32[]{:S(2)}) collective-permute-start(bf16[144,768]{1,0:T(8,128)(2,1)S(1)} %get-tuple-element.171), channel_id=1, source_target_pairs={{0,1},{1,0},{2,3},{3,2},{4,5},{5,4},{6,7},{7,6},{8,9},{9,8},{10,11... | collective-permute-start | bytes 663560 | tf_op jit(solution)/shard_map/ppermute | solution.py:265
  156.6 6.9 %collective-permute-start.44 = (bf16[144,768]{1,0:T(8,128)(2,1)S(1)}, bf16[144,768]{1,0:T(8,128)(2,1)S(1)}, u32[]{:S(2)}, u32[]{:S(2)}) collective-permute-start(bf16[144,768]{1,0:T(8,128)(2,1)S(1)} %get-tuple-element.173.refs_0_), channel_id=1, source_target_pairs={{0,2},{1,5},{2,0},{3,7},{4,6},{5,1},{6,4},{7,3},{8,10},{9,13},{10,... | collective-permute-start | bytes 663560 | tf_op jit(solution)/shard_map/ppermute | solution.py:265
  158.0 10.3 %collective-permute-start.27 = (bf16[144,768]{1,0:T(8,128)(2,1)S(1)}, bf16[144,768]{1,0:T(8,128)(2,1)S(1)}, u32[]{:S(2)}, u32[]{:S(2)}) collective-permute-start(bf16[144,768]{1,0:T(8,128)(2,1)S(1)} %get-tuple-element.130.refs_0_), channel_id=1, source_target_pairs={{0,2},{1,5},{2,0},{3,7},{4,6},{5,1},{6,4},{7,3},{8,10},{9,13},{10,... | collective-permute-start | bytes 663560 | tf_op jit(solution)/shard_map/ppermute | solution.py:265
  159.6 9.7 %collective-permute-start.46 = (bf16[144,768]{1,0:T(8,128)(2,1)S(1)}, bf16[144,768]{1,0:T(8,128)(2,1)S(1)}, u32[]{:S(2)}, u32[]{:S(2)}) collective-permute-start(bf16[144,768]{1,0:T(8,128)(2,1)S(1)} %get-tuple-element.173.refs_0_), channel_id=1, source_target_pairs={{0,4},{1,3},{2,6},{3,1},{4,0},{5,7},{6,2},{7,5},{8,12},{9,11},{10,... | collective-permute-start | bytes 663560 | tf_op jit(solution)/shard_map/ppermute | solution.py:265
  163.4 9.2 %collective-permute-start.45 = (bf16[144,768]{1,0:T(8,128)(2,1)S(1)}, bf16[144,768]{1,0:T(8,128)(2,1)S(1)}, u32[]{:S(2)}, u32[]{:S(2)}) collective-permute-start(bf16[144,768]{1,0:T(8,128)(2,1)S(1)} %collective-permute-done.44.refs_0_), channel_id=1, source_target_pairs={{0,4},{1,3},{2,6},{3,1},{4,0},{5,7},{6,2},{7,5},{8,12},{9,11},{10,... | collective-permute-start | bytes 663560 | tf_op jit(solution)/shard_map/ppermute | solution.py:265
  164.3 14.1 %collective-permute-start.29 = (bf16[144,768]{1,0:T(8,128)(2,1)S(1)}, bf16[144,768]{1,0:T(8,128)(2,1)S(1)}, u32[]{:S(2)}, u32[]{:S(2)}) collective-permute-start(bf16[144,768]{1,0:T(8,128)(2,1)S(1)} %get-tuple-element.130.refs_0_), channel_id=1, source_target_pairs={{0,4},{1,3},{2,6},{3,1},{4,0},{5,7},{6,2},{7,5},{8,12},{9,11},{10,... | collective-permute-start | bytes 663560 | tf_op jit(solution)/shard_map/ppermute | solution.py:265
  168.3 13.3 %collective-permute-start.28 = (bf16[144,768]{1,0:T(8,128)(2,1)S(1)}, bf16[144,768]{1,0:T(8,128)(2,1)S(1)}, u32[]{:S(2)}, u32[]{:S(2)}) collective-permute-start(bf16[144,768]{1,0:T(8,128)(2,1)S(1)} %collective-permute-done.27.refs_0_), channel_id=1, source_target_pairs={{0,4},{1,3},{2,6},{3,1},{4,0},{5,7},{6,2},{7,5},{8,12},{9,11},{10,... | collective-permute-start | bytes 663560 | tf_op jit(solution)/shard_map/ppermute | solution.py:265
  175.5 9.6 %collective-permute-start.47 = (bf16[144,768]{1,0:T(8,128)(2,1)S(1)}, bf16[144,768]{1,0:T(8,128)(2,1)S(1)}, u32[]{:S(2)}, u32[]{:S(2)}) collective-permute-start(bf16[144,768]{1,0:T(8,128)(2,1)S(1)} %get-tuple-element.182), channel_id=1, source_target_pairs={{0,1},{1,0},{2,3},{3,2},{4,5},{5,4},{6,7},{7,6},{8,9},{9,8},{10,11... | collective-permute-start | bytes 663560 | tf_op jit(solution)/shard_map/ppermute | solution.py:265
  185.9 6.8 %collective-permute-start.48 = (bf16[144,768]{1,0:T(8,128)(2,1)S(1)}, bf16[144,768]{1,0:T(8,128)(2,1)S(1)}, u32[]{:S(2)}, u32[]{:S(2)}) collective-permute-start(bf16[144,768]{1,0:T(8,128)(2,1)S(1)} %get-tuple-element.184.refs_0_), channel_id=1, source_target_pairs={{0,2},{1,5},{2,0},{3,7},{4,6},{5,1},{6,4},{7,3},{8,10},{9,13},{10,... | collective-permute-start | bytes 663560 | tf_op jit(solution)/shard_map/ppermute | solution.py:265
  187.0 10.6 %collective-permute-start.31 = (bf16[144,768]{1,0:T(8,128)(2,1)S(1)}, bf16[144,768]{1,0:T(8,128)(2,1)S(1)}, u32[]{:S(2)}, u32[]{:S(2)}) collective-permute-start(bf16[144,768]{1,0:T(8,128)(2,1)S(1)} %get-tuple-element.141.refs_0_), channel_id=1, source_target_pairs={{0,2},{1,5},{2,0},{3,7},{4,6},{5,1},{6,4},{7,3},{8,10},{9,13},{10,... | collective-permute-start | bytes 663560 | tf_op jit(solution)/shard_map/ppermute | solution.py:265
  189.0 9.9 %collective-permute-start.50 = (bf16[144,768]{1,0:T(8,128)(2,1)S(1)}, bf16[144,768]{1,0:T(8,128)(2,1)S(1)}, u32[]{:S(2)}, u32[]{:S(2)}) collective-permute-start(bf16[144,768]{1,0:T(8,128)(2,1)S(1)} %get-tuple-element.184.refs_0_), channel_id=1, source_target_pairs={{0,4},{1,3},{2,6},{3,1},{4,0},{5,7},{6,2},{7,5},{8,12},{9,11},{10,... | collective-permute-start | bytes 663560 | tf_op jit(solution)/shard_map/ppermute | solution.py:265
  192.8 9.3 %collective-permute-start.49 = (bf16[144,768]{1,0:T(8,128)(2,1)S(1)}, bf16[144,768]{1,0:T(8,128)(2,1)S(1)}, u32[]{:S(2)}, u32[]{:S(2)}) collective-permute-start(bf16[144,768]{1,0:T(8,128)(2,1)S(1)} %collective-permute-done.48.refs_0_), channel_id=1, source_target_pairs={{0,4},{1,3},{2,6},{3,1},{4,0},{5,7},{6,2},{7,5},{8,12},{9,11},{10,... | collective-permute-start | bytes 663560 | tf_op jit(solution)/shard_map/ppermute | solution.py:265
  193.9 13.9 %collective-permute-start.33 = (bf16[144,768]{1,0:T(8,128)(2,1)S(1)}, bf16[144,768]{1,0:T(8,128)(2,1)S(1)}, u32[]{:S(2)}, u32[]{:S(2)}) collective-permute-start(bf16[144,768]{1,0:T(8,128)(2,1)S(1)} %get-tuple-element.141.refs_0_), channel_id=1, source_target_pairs={{0,4},{1,3},{2,6},{3,1},{4,0},{5,7},{6,2},{7,5},{8,12},{9,11},{10,... | collective-permute-start | bytes 663560 | tf_op jit(solution)/shard_map/ppermute | solution.py:265
  197.6 13.4 %collective-permute-start.32 = (bf16[144,768]{1,0:T(8,128)(2,1)S(1)}, bf16[144,768]{1,0:T(8,128)(2,1)S(1)}, u32[]{:S(2)}, u32[]{:S(2)}) collective-permute-start(bf16[144,768]{1,0:T(8,128)(2,1)S(1)} %collective-permute-done.31.refs_0_), channel_id=1, source_target_pairs={{0,4},{1,3},{2,6},{3,1},{4,0},{5,7},{6,2},{7,5},{8,12},{9,11},{10,... | collective-permute-start | bytes 663560 | tf_op jit(solution)/shard_map/ppermute | solution.py:265
  204.9 9.6 %collective-permute-start.51 = (bf16[144,768]{1,0:T(8,128)(2,1)S(1)}, bf16[144,768]{1,0:T(8,128)(2,1)S(1)}, u32[]{:S(2)}, u32[]{:S(2)}) collective-permute-start(bf16[144,768]{1,0:T(8,128)(2,1)S(1)} %get-tuple-element.193), channel_id=1, source_target_pairs={{0,1},{1,0},{2,3},{3,2},{4,5},{5,4},{6,7},{7,6},{8,9},{9,8},{10,11... | collective-permute-start | bytes 663560 | tf_op jit(solution)/shard_map/ppermute | solution.py:265
  214.9 10.8 %collective-permute-start.52 = (bf16[64,768]{1,0:T(8,128)(2,1)S(1)}, bf16[64,768]{1,0:T(8,128)(2,1)S(1)}, u32[]{:S(2)}, u32[]{:S(2)}) collective-permute-start(bf16[64,768]{1,0:T(8,128)(2,1)S(1)} %get-tuple-element.196), channel_id=1, source_target_pairs={{0,16},{8,24},{16,0},{24,8},{1,17},{9,25},{17,1},{25,9},{2,18},{10... | collective-permute-start | bytes 294920 | tf_op jit(solution)/shard_map/ppermute | solution.py:277
  215.9 9.8 %collective-permute-start.53 = (bf16[64,768]{1,0:T(8,128)(2,1)S(1)}, bf16[64,768]{1,0:T(8,128)(2,1)S(1)}, u32[]{:S(2)}, u32[]{:S(2)}) collective-permute-start(bf16[64,768]{1,0:T(8,128)(2,1)S(1)} %get-tuple-element.195), channel_id=1, source_target_pairs={{0,24},{8,16},{16,8},{24,0},{1,25},{9,17},{17,9},{25,1},{2,26},{10... | collective-permute-start | bytes 294920 | tf_op jit(solution)/shard_map/ppermute | solution.py:277
  219.2 7.1 %collective-permute-start.35 = (bf16[64,768]{1,0:T(8,128)(2,1)S(1)}, bf16[64,768]{1,0:T(8,128)(2,1)S(1)}, u32[]{:S(2)}, u32[]{:S(2)}) collective-permute-start(bf16[64,768]{1,0:T(8,128)(2,1)S(1)} %get-tuple-element.197), channel_id=1, source_target_pairs={{0,8},{8,0},{16,24},{24,16},{1,9},{9,1},{17,25},{25,17},{2,10},{10... | collective-permute-start | bytes 294920 | tf_op jit(solution)/shard_map/ppermute | solution.py:277
  (30 other events, 209.8 us)

commit v2 on v1

v2 whole, which is shorter than its diff:
```python
import functools
import math

import jax
import jax.numpy as jnp
from jax import lax
from jax.experimental import pallas as pl
from jax.experimental.pallas import tpu as pltpu
from jax.sharding import PartitionSpec as P

STEPS = 4
CAP = 64
EPS = 1e-05
EXT = 16
MIB = 2**20

adapter_scale = 0.5

F32 = jnp.float32
BF16 = jnp.bfloat16
IN_VMEM = pl.BlockSpec(memory_space=pltpu.VMEM)
IN_SMEM = pl.BlockSpec(memory_space=pltpu.SMEM)
CONTRACT_LAST = (((1,), (1,)), ((), ()))
CONTRACT_FIRST = (((0,), (0,)), ((), ()))


def pinned(x):
    return pltpu.with_memory_space_constraint(x, pltpu.VMEM)


def call(kernel, out, specs, *args, name=None, scratch=(), pin=False, after=()):
    many = isinstance(out, list)
    n_args, kernel_of = len(args), kernel
    if after:
        args, specs = (*args, *after), [*specs] + [pl.BlockSpec(memory_space=pl.ANY)] * len(after)

        def kernel(*refs):
            kernel_of(*refs[:n_args], *refs[n_args + len(after) :])

    kind = pltpu.VMEM if pin else jax.ShapeDtypeStruct
    shapes = [kind(s, d) for s, d in (out if many else [out])]
    r = pl.pallas_call(
        kernel,
        out_shape=shapes,
        in_specs=specs,
        out_specs=[IN_VMEM] * len(shapes),
        scratch_shapes=scratch,
        compiler_params=pltpu.CompilerParams(vmem_limit_bytes=12 * MIB),
        cost_estimate=pl.CostEstimate(flops=0, bytes_accessed=0, transcendentals=0),
        name=name,
    )(*args)
    return r if many else r[0]


def dot(a, b, dims=(((1,), (0,)), ((), ()))):
    return lax.dot_general(a, b, dims, preferred_element_type=F32)


def iota(shape, dim):
    return lax.broadcasted_iota(jnp.int32, shape, dim)


def sort_kernel(tokens_ref, target_ref, slot_ref, perm_ref, *chunk_refs):
    n_tokens, width = tokens_ref.shape
    groups = len(chunk_refs)
    rows = groups * CAP
    apart = jnp.bitwise_xor(target_ref[...], lax.axis_index("store"))
    member = (iota((max(8, groups), n_tokens), 0) == apart).astype(F32)
    before = (iota((n_tokens, n_tokens), 0) < iota((n_tokens, n_tokens), 1)).astype(BF16)
    earlier = dot(member.astype(BF16), before)
    place = jnp.sum(earlier * member, axis=0, keepdims=True).astype(jnp.int32)
    perm = (iota((rows, n_tokens), 0) == apart * CAP + place).astype(F32).astype(BF16)
    perm_ref[...] = perm
    sorted_rows = dot(perm, tokens_ref[...]).astype(BF16)
    slots = jnp.broadcast_to((slot_ref[...] + 1).astype(F32), (8, n_tokens)).astype(BF16)
    slots = dot(slots, perm, CONTRACT_LAST)
    lanes = 2 * CAP
    for k, ref in enumerate(chunk_refs):
        ref[:, :width] = sorted_rows[k * CAP : (k + 1) * CAP]
        half = slots[:, (k // 2) * lanes : (k // 2 + 1) * lanes]
        ref[:, width:] = jnp.concatenate([half, jnp.zeros((CAP - 8, lanes), F32)], 0).astype(BF16)


def unsort_kernel(perm_ref, *refs):
    rows = jnp.concatenate([r[...] for r in refs[:-1]], axis=0)
    refs[-1][...] = dot(perm_ref[...], rows, CONTRACT_FIRST).astype(BF16)


def order_of(plan_ref, owned, end, far):
    asked = []
    for l in range(owned):
        hit = [plan_ref[far, i] == end * owned + l for i in range(plan_ref.shape[1])]
        asked.append(functools.reduce(jnp.logical_or, hit).astype(jnp.int32))
    total, seen, places = sum(asked), 0, []
    for l in range(owned):
        places.append(jnp.where(asked[l] == 1, seen, total + l - seen))
        seen = seen + asked[l]
    return places


def chosen(values, index):
    out = values[0]
    for i in range(1, len(values)):
        out = jnp.where(index == i, values[i], out)
    return out


def end_blocks(owned, plan_ref, own_ref, out_refs):
    copies = plan_ref.shape[1]
    rank = own_ref.shape[0] // owned
    group = lax.axis_index("store")
    end = jnp.where(group < 2, 0, 3)
    for l, place in enumerate(order_of(plan_ref, owned, end, 3 - end)):
        for block, out_ref in enumerate(out_refs):

            @pl.when(jnp.logical_and(place // copies == block, group == end))
            def _():
                at = pl.multiple_of((place % copies) * rank, rank)
                out_ref[pl.ds(at, rank), :] = own_ref[l * rank : (l + 1) * rank, :]

    for i in range(copies):

        @pl.when(group != end)
        def _():
            at = pl.multiple_of((plan_ref[end, i] % owned) * rank, rank)
            out_refs[0][i * rank : (i + 1) * rank, :] = own_ref[pl.ds(at, rank), :]


def end_blocks_kernel(owned, plan_ref, own_ref, low_ref, high_ref):
    end_blocks(owned, plan_ref, own_ref, (low_ref, high_ref))


def front_kernel(owned, plan_ref, own_ref, tokens_ref, target_ref, slot_ref, low_ref, high_ref, *refs):
    end_blocks(owned, plan_ref, own_ref, (low_ref, high_ref))
    sort_kernel(tokens_ref, target_ref, slot_ref, *refs)


def pass_kernel(owned, dest_of, n_blocks, plan_ref, own_ref, *refs):
    out_ref = refs[-1]
    copies = plan_ref.shape[1]
    rank = own_ref.shape[0] // owned
    group = lax.axis_index("store")
    end = jnp.where(group < 2, 0, 3)
    places = order_of(plan_ref, owned, end, 3 - end)
    for i in range(copies):
        adapter = plan_ref[chosen(dest_of, group), i]
        owner, local = adapter // owned, adapter % owned
        at = slice(i * rank, (i + 1) * rank)

        @pl.when(owner == group)
        def _():
            out_ref[at, :] = own_ref[pl.ds(pl.multiple_of(local * rank, rank), rank), :]

        place = chosen(places, local)
        begin = pl.multiple_of((place % copies) * rank, rank)
        for j in range(n_blocks):

            @pl.when(jnp.logical_and(owner != group, place // copies == j))
            def _():
                out_ref[at, :] = refs[j][pl.ds(begin, rank), :]

        if n_blocks == 1:

            @pl.when(jnp.logical_and(owner != group, place // copies > 0))
            def _():
                out_ref[at, :] = refs[0][at, :]


def gather_kernel(owned, plan_ref, low_ref, high_ref, passed_ref, far_ref, out_ref):
    copies = plan_ref.shape[1]
    rank = out_ref.shape[0] // copies
    group = lax.axis_index("store")
    end = jnp.where(group < 2, 0, 3)
    beside = jnp.where(group < 2, 1, 2)
    places = order_of(plan_ref, owned, end, 3 - end)
    for i in range(copies):
        adapter = plan_ref[group, i]
        owner, local = adapter // owned, adapter % owned
        at = slice(i * rank, (i + 1) * rank)
        place = chosen(places, local)
        begin = pl.multiple_of((place % copies) * rank, rank)
        middle = group == beside

        def put(condition, value_of):
            @pl.when(condition)
            def _():
                out_ref[at, :] = value_of()

        raw = jnp.logical_and(middle, owner == end)
        put(jnp.logical_and(raw, place < copies), lambda: low_ref[pl.ds(begin, rank), :])
        put(jnp.logical_and(raw, place >= copies), lambda: high_ref[pl.ds(begin, rank), :])
        put(jnp.logical_and(middle, owner != end), lambda: passed_ref[at, :])
        put(jnp.logical_and(group == end, owner == beside), lambda: low_ref[at, :])
        put(jnp.logical_and(group == end, owner != beside), lambda: far_ref[at, :])


def fetch_copies(plan, own, owned, front):
    copies = plan.shape[1]
    rank = own[0].shape[0] // owned
    shape = ((copies * rank, own[0].shape[1]), BF16)

    def make(kernel, *args, out=shape, after=()):
        return call(kernel, out, [IN_SMEM] + [IN_VMEM] * len(args), plan, *args, name="pick", after=after)

    def send(x, pairs):
        return lax.ppermute(x, "store", pairs)

    def passing(dest_of, i, *blocks, after=()):
        return make(functools.partial(pass_kernel, owned, dest_of, len(blocks)), own[i], *blocks, after=after)

    pairs, ends, middle, across = [(0, 1), (1, 0), (2, 3), (3, 2)], [(0, 1), (3, 2)], [(1, 2), (2, 1)], [(1, 3), (2, 0)]
    low, high, got = {}, {}, []
    (low[0], high[0]), chunks, rest = front(shape)
    low[0], high[0] = send(low[0], pairs), send(high[0], ends)
    low[1], high[1] = make(
        functools.partial(end_blocks_kernel, owned), own[1], out=[shape, shape], after=[low[0], *chunks[1:]]
    )
    low[1], high[1] = send(low[1], pairs), send(high[1], ends)
    for i in range(2):
        far = send(passing((3, 3, 0, 0), i, low[i]), across)
        passed = send(passing((2, 2, 1, 1), i, low[i], high[i]), middle)
        got.append(make(functools.partial(gather_kernel, owned), low[i], high[i], passed, far))
    return got, chunks, rest, low[0]


def apart_kernel(weight_ref, sent_ref, sems):
    width = weight_ref.shape[1]
    other = 1 - lax.axis_index("mp") % 2
    copies = []
    for q in range(sent_ref.shape[0] // width):
        start = pl.multiple_of((2 * q + other) * width, width)
        copies.append(
            pltpu.make_async_copy(
                weight_ref.at[pl.ds(start, width), :], sent_ref.at[pl.ds(q * width, width), :], sems.at[q]
            )
        )
    for copy in copies:
        copy.start()
    for copy in copies:
        copy.wait()


def two_parts(row):
    high = row.astype(BF16).astype(F32)
    at = iota((EXT, row.shape[1]), 0)
    return jnp.where(at == 0, high, jnp.where(at == 1, row - high, 0.0)).astype(BF16)


def put_extra(msg_ref, rows, inner, squares):
    width = msg_ref.shape[1]
    groups = 0 if inner is None else inner.shape[0] // EXT
    rank_groups = width // rows
    msg_ref[rows:, :] = jnp.zeros((EXT, width), BF16)
    for g in range(groups):
        msg_ref[rows:, g * rows : (g + 1) * rows] = inner[g * EXT : (g + 1) * EXT].astype(BF16)
    msg_ref[rows:, (rank_groups - 1) * rows :] = two_parts(squares)


def squares_row(state):
    total = jnp.sum(state * state, axis=1, keepdims=True)
    rows = state.shape[0]
    return jnp.transpose(jnp.broadcast_to(total, (rows, rows)))[0:1, :]


def slot_masks(slots, first, count, shape):
    return [jnp.broadcast_to(slots[0:1, :] == float(j), shape) for j in range(first, first + count)]


def inner_partial(u, slots, down_refs, rank):
    first, total = 0, None
    rows = u.shape[0]
    for ref in down_refs:
        count = ref.shape[0] // rank
        product = dot(ref[...], u, CONTRACT_LAST)
        for j, mask in enumerate(slot_masks(slots, first, count, (rank, rows))):
            term = jnp.where(mask, product[j * rank : (j + 1) * rank], 0.0)
            total = term if total is None else total + term
        first += count
    return total


def my_columns(gain_ref, width):
    return gain_ref[:, pl.ds(pl.multiple_of(lax.axis_index("mp") * width, width), width)]


def first_kernel(gain_ref, *refs):
    n = (len(refs) - 1) // 4
    chunk_refs, state_refs, slots_refs, msg_ref = refs[: 2 * n], refs[2 * n : 3 * n], refs[3 * n : 4 * n], refs[4 * n]
    for h in range(n):
        even_ref, odd_ref, state_ref, slots_ref = chunk_refs[2 * h], chunk_refs[2 * h + 1], state_refs[h], slots_refs[h]
        cap = even_ref.shape[0]
        rows, width = state_ref.shape
        state_ref[:cap] = even_ref[:, :width]
        state_ref[cap:] = odd_ref[:, :width]
        lane = iota((8, rows), 1)
        even, odd = even_ref[:, width:].astype(F32)[0:8], odd_ref[:, width:].astype(F32)[0:8]
        slots_ref[...] = jnp.where(lane < cap, even, odd) - 1.0
        state = state_ref[...].astype(F32)
        part_ref = msg_ref.at[h * (rows + EXT) : (h + 1) * (rows + EXT)]
        part_ref[:rows, :] = (state * my_columns(gain_ref, width)).astype(BF16)
        put_extra(part_ref, rows, None, squares_row(state))


def first_inner_kernel(msg_ref, slots0_ref, slots1_ref, own_ref, copy_ref, out_ref):
    rank, rows = out_ref.shape[0], out_ref.shape[1] // 2
    for h, slots in enumerate((slots0_ref, slots1_ref)):
        u = msg_ref[h * (rows + EXT) : h * (rows + EXT) + rows, :]
        out_ref[:, h * rows : (h + 1) * rows] = inner_partial(u, slots[...], (own_ref, copy_ref), rank)


def block_kernel(n_blocks, n_halves, at, last, weight_ref, other_ref, *refs):
    msgs, refs = refs[:n_blocks], refs[n_blocks:]
    width = weight_ref.shape[1]
    rows = msgs[0].shape[0] // n_halves - EXT
    if at[0] == 0:
        old = None
        outs = refs
    else:
        old, outs = refs[:3], refs[3:]
    mine = theirs = extra = None
    part = lax.axis_index("mp")
    core = part % 2

    def both(msg, under):
        parts = []
        for h in range(n_halves):
            begin = h * (rows + EXT)
            parts.append(msg[begin + rows : begin + rows + EXT, :] if under else msg[begin : begin + rows, :])
        return parts[0] if n_halves == 1 else jnp.concatenate(parts, axis=0)

    for i, msg in enumerate(msgs):
        q = jnp.bitwise_xor(part // 2, (0, 1 + core, 2 - core, 3)[at[i]])
        u = both(msg, False)
        a = dot(u, weight_ref[pl.ds(pl.multiple_of((2 * q + core) * width, width), width), :])
        b = dot(u, other_ref[pl.ds(pl.multiple_of(q * width, width), width), :])
        e = both(msg, True).astype(F32)
        mine, theirs, extra = (a, b, e) if mine is None else (mine + a, theirs + b, extra + e)
    if old is not None:
        mine, theirs, extra = mine + old[0][...], theirs + old[1][...], extra + old[2][...]
    outs[0][...] = mine
    outs[2][...] = extra
    if not last:
        outs[1][...] = theirs
        return
    for h in range(n_halves):
        begin = h * (rows + EXT)
        outs[1][begin : begin + rows, :] = theirs[h * rows : (h + 1) * rows].astype(BF16)
        under = extra[h * EXT : (h + 1) * EXT]
        outs[1][begin + rows : begin + rows + EXT, :] = under.astype(BF16)
        tail = under[:, width - rows :]
        outs[1][begin + rows : begin + rows + EXT, width - rows :] = two_parts(tail[0:1] + tail[1:2])


def finish_kernel(
    n_halves, h, last, rank, mine_ref, extra_ref, got_ref, state_ref, slots_ref, gain_ref, down_ref, downc_ref, up_ref, upc_ref, *refs
):
    rows, width = state_ref.shape
    width_all = gain_ref.shape[1]
    if n_halves > 1:
        inner_ref, refs = refs[0], refs[1:]
    begin = h * (rows + EXT)
    extra = extra_ref[h * EXT : (h + 1) * EXT, :] + got_ref[begin + rows : begin + rows + EXT, :].astype(F32)
    if n_halves > 1:
        inner = inner_ref[:, h * rows : (h + 1) * rows]
    else:
        inner = jnp.concatenate(
            [extra[:, g * rows : (g + 1) * rows] for g in range(rank // EXT)], axis=0
        )
    tail = extra[:, width - rows :]
    scale = lax.rsqrt((tail[0:1] + tail[1:2]) / width_all + EPS)
    inner = (inner * scale).astype(BF16).astype(F32)
    slots = slots_ref[...]
    outer, held = None, 0
    for ref in (up_ref, upc_ref):
        count = ref.shape[0] // rank
        spread = jnp.concatenate(
            [jnp.where(m, inner, 0.0) for m in slot_masks(slots, held, count, (rank, rows))], axis=0
        ).astype(BF16)
        term = dot(spread, ref[...], CONTRACT_FIRST)
        outer = term if outer is None else outer + term
        held += count
    delta = (adapter_scale * outer).astype(BF16).astype(F32)
    column = jnp.transpose(jnp.broadcast_to(scale, (rows, rows)))
    column = jnp.concatenate([column] * (width // rows), axis=1)
    base = (mine_ref[h * rows : (h + 1) * rows, :] + got_ref[begin : begin + rows, :].astype(F32)) * column
    state = (state_ref[...].astype(F32) + base + delta).astype(BF16)
    if last:
        refs[0][...] = state[: rows // 2]
        refs[1][...] = state[rows // 2 :]
        return
    refs[0][...] = state
    msg_ref = refs[1]
    state = state.astype(F32)
    u = (state * my_columns(gain_ref, width)).astype(BF16)
    msg_ref[:rows, :] = u
    put_extra(msg_ref, rows, inner_partial(u, slots, (down_ref, downc_ref), rank), squares_row(state))


def body(tokens, gain, base_projection_weight, adapter_down_weight, adapter_up_weight, plan, target, slot):
    groups = lax.axis_size("store")
    parts = lax.axis_size("mp")
    n_tokens, width = tokens.shape
    owned, rank = adapter_down_weight.shape[:2]
    rows = 2 * CAP
    gain = gain.reshape(1, parts * width)

    def mp(x, pairs_of):
        return lax.ppermute(x, "mp", [(i, pairs_of(i)) for i in range(parts)])

    def sibling(x):
        return mp(x, lambda i: i ^ 1)

    def side_a(x):
        return mp(x, lambda i: i ^ (4 if i % 2 else 2))

    def side_b(x):
        return mp(x, lambda i: i ^ (2 if i % 2 else 4))

    def store(x, k):
        return lax.ppermute(x, "store", [(g, g ^ k) for g in range(groups)])

    down = adapter_down_weight.reshape(owned * rank, width)
    up = adapter_up_weight.reshape(owned * rank, width)

    def front(shape):
        low, high, perm, *chunks = call(
            functools.partial(front_kernel, owned),
            [shape, shape, ((groups * CAP, n_tokens), BF16)] + [((CAP, width + rows), BF16)] * groups,
            [IN_SMEM] + [IN_VMEM] * 4,
            plan,
            *(
                pltpu.with_memory_space_constraint(x, pltpu.HBM)
                for x in (down, tokens, target.reshape(1, n_tokens), slot.reshape(1, n_tokens))
            ),
            name="front",
        )
        return (low, high), [c if k == 0 else store(c, k) for k, c in enumerate(chunks)], perm

    (down_copy, up_copy), chunks, perm, early = fetch_copies(plan, [down, up], owned, front)

    other = call(
        apart_kernel,
        ((parts // 2 * width, width), BF16),
        [pl.BlockSpec(memory_space=pl.ANY)],
        pltpu.with_memory_space_constraint(base_projection_weight, pltpu.HBM),
        name="apart",
        scratch=[pltpu.SemaphoreType.DMA((parts // 2,))],
        after=[perm],
    )
    weight, other = pinned(base_projection_weight), pinned(sibling(other))

    halves = range(groups // 2)
    n = len(halves)
    acc = ((rows, width), F32)
    message = ((rows + EXT, width), BF16)

    def blocks_of(n_halves, msgs, at, old, last):
        many = [((n_halves * r, c), d) for (r, c), d in (acc, message if last else acc, ((EXT, width), F32))]
        return call(
            functools.partial(block_kernel, len(msgs), n_halves, at, last),
            many,
            [IN_VMEM] * (2 + len(msgs) + len(old)),
            weight,
            other,
            *msgs,
            *old,
            name="blocks",
        )

    def exchange(n_halves, msg):
        a = side_a(msg)
        b = side_b(msg)
        old = blocks_of(n_halves, [msg], (0,), (), False)
        d = side_b(a)
        old = blocks_of(n_halves, [a, b], (1, 2), old, False)
        mine, theirs, extra = blocks_of(n_halves, [d], (3,), old, True)
        return mine, extra, sibling(theirs)

    def finish(n_halves, h, final, sums, state, slots, inner=()):
        args = [*sums, state, slots, gain, down, down_copy, up, up_copy, *inner]
        return call(
            functools.partial(finish_kernel, n_halves, h, final, rank),
            [((CAP, width), BF16)] * 2 if final else [((rows, width), BF16), message],
            [IN_VMEM] * len(args),
            *args,
            name="finish",
        )

    outs = call(
        first_kernel,
        [((rows, width), BF16)] * n + [((8, rows), F32)] * n + [((n * (rows + EXT), width), BF16)],
        [IN_VMEM] * (1 + groups),
        gain,
        *chunks,
        name="first",
        after=[early, other],
    )
    state, slots, msg = outs[:n], outs[n : 2 * n], outs[-1]
    sums = exchange(n, msg)
    inner = call(
        first_inner_kernel, ((rank, n * rows), F32), [IN_VMEM] * 5, msg, *slots, down, down_copy, name="first_inner"
    )
    for k in (2, 4, 1):
        inner = inner + mp(inner, lambda i: i ^ k)
    outs = [finish(n, h, False, sums, state[h], slots[h], [inner]) for h in halves]
    state, msg = [o[0] for o in outs], [o[1] for o in outs]
    for step in range(1, STEPS):
        final = step == STEPS - 1
        for h in halves:
            outs = finish(1, 0, final, exchange(1, msg[h]), state[h], slots[h])
            if final:
                state[h] = outs
            else:
                state[h], msg[h] = outs

    back = [c if k == 0 else store(c, k) for k, c in enumerate(sum(map(list, state), []))]
    return call(
        unsort_kernel,
        ((n_tokens, width), BF16),
        [IN_VMEM] * (1 + groups),
        perm,
        *back,
        name="unsort",
    )


def plain_body(
    tokens, gain, base_projection_weight, adapter_down_weight, adapter_up_weight, plan, target, slot
):
    store_count = lax.axis_size("store")
    group = lax.axis_index("store")
    owned_adapters, rank, width = adapter_down_weight.shape
    replica_count = plan.shape[1]
    n_slots = owned_adapters + replica_count
    owner = plan // owned_adapters
    local = plan % owned_adapters
    select = jnp.logical_and(
        (owner == group)[:, :, None],
        local[:, :, None] == jnp.arange(owned_adapters, dtype=jnp.int32)[None, None, :],
    )
    select = select.astype(BF16).reshape(store_count * replica_count, owned_adapters)

    def held(own):
        send = jnp.dot(select, own.reshape(owned_adapters, rank * width), preferred_element_type=F32)
        send = send.astype(BF16).reshape(store_count, replica_count, rank * width)
        got = lax.all_to_all(send, "store", split_axis=0, concat_axis=0, tiled=True)
        got = jnp.sum(got.astype(F32), axis=0).astype(BF16)
        both = jnp.concatenate([own, got.reshape(replica_count, rank, width)], 0)
        return both.reshape(n_slots * rank, width)

    host_down, host_up = held(adapter_down_weight), held(adapter_up_weight)
    target_group = target[:, 0]
    n_tokens = target_group.shape[0]
    member = (target_group[:, None] == jnp.arange(store_count, dtype=jnp.int32)[None, :]).astype(BF16)
    order = jnp.arange(n_tokens)
    before = (order[:, None] > order[None, :]).astype(BF16)
    earlier = jnp.dot(before, member, preferred_element_type=F32)
    place = jnp.sum(earlier * member.astype(F32), axis=1).astype(jnp.int32)
    row_index = target_group * CAP + place
    slots = jnp.full((store_count * CAP,), -1, jnp.int32).at[row_index].set(slot)
    state = jnp.zeros((store_count * CAP, width), BF16).at[row_index].set(tokens)

    def exchange(x):
        return lax.all_to_all(
            x.reshape(store_count, CAP, -1), "store", split_axis=0, concat_axis=0, tiled=True
        ).reshape(store_count * CAP, -1)

    state = exchange(state)
    selected = exchange(slots) == jnp.arange(n_slots, dtype=jnp.int32)[None, :]
    total_rows = state.shape[0]
    column_start = lax.axis_index("mp") * width
    for step in range(STEPS):
        whole = lax.all_gather(state, "mp", axis=1, tiled=True)
        values = whole.astype(F32)
        mean_sq = jnp.mean(values * values, axis=1, keepdims=True)
        normed = (values * lax.rsqrt(mean_sq + EPS) * gain[None, :]).astype(BF16)
        mine = lax.dynamic_slice_in_dim(normed, column_start, width, 1)
        partial_value = lax.dot_general(mine, host_down, CONTRACT_LAST, preferred_element_type=F32)
        partial_value = jnp.sum(
            partial_value.reshape(total_rows, n_slots, rank) * selected[:, :, None].astype(F32), axis=1
        )
        inner = lax.psum(partial_value, "mp").astype(BF16)
        spread = (selected[:, :, None].astype(BF16) * inner[:, None, :]).reshape(total_rows, -1)
        outer = jnp.dot(spread, host_up, preferred_element_type=F32)
        delta = (adapter_scale * outer).astype(BF16).astype(F32)
        base = jnp.dot(normed, base_projection_weight, preferred_element_type=F32)
        state = (state.astype(F32) + base + delta).astype(BF16)
    return exchange(state)[row_index]


def solution(mesh):
    parts, groups = mesh.shape["mp"], mesh.shape["store"]

    def run(tokens, *rest):
        width = tokens.shape[1] // parts
        rank = rest[2].shape[1]
        rows = 2 * CAP
        cube = parts == 8 and groups == 4
        cube = cube and rest[2].shape[0] == 2 * groups * rest[4].shape[1]
        fits = rank % EXT == 0 and width % rows == 0 and rank // EXT + 1 <= width // rows
        return jax.shard_map(
            body if cube and fits else plain_body,
            mesh=mesh,
            in_specs=(
                P("store", "mp"),
                P(),
                P(None, "mp"),
                P("store", None, "mp"),
                P("store", None, "mp"),
                P(),
                P("store", None),
                P("store"),
            ),
            out_specs=P("store", "mp"),
            check_vma=False,
        )(tokens, *rest)

    return run
```

time: 229 us -> 154 us (0.67)
  Pallas kernels: 95.3 us -> 32.5 us
  waiting for transfers between devices: 34.7 us -> 71.1 us
  starting transfers between devices: 79.5 us -> 48.3 us
  local copies, waits for them, and re-layouts: 14.1 us -> 0.73 us
  other arithmetic: 2.97 us -> 0.03 us
    pallas_call x49 -> x41, Pallas kernels: 95.3 us -> 32.5 us  [call(): pl.pallas_call(kernel, out_shape=shapes, in_specs=specs, out_specs=[IN_VM...]
    ppermute x12 -> x8, starting transfers between devices: 36.7 us -> 11.9 us  [send(): return lax.ppermute(x, 'store', pairs)]
    ppermute x36 -> x32, waiting for transfers between devices: 14.3 us -> 35.3 us  [mp(): return lax.ppermute(x, 'mp', [(i, pairs_of(i)) for i in range(parts)])]
    ppermute x12 -> x8, waiting for transfers between devices: 4.96 us -> 14.4 us  [send(): return lax.ppermute(x, 'store', pairs)]
    unnamed x48 -> x16, local copies, waits for them, and re-layouts: 8.22 us -> 0.73 us
    ppermute x6, waiting for transfers between devices: 15.4 us -> 21.4 us  [store(): return lax.ppermute(x, 'store', [(g, g ^ k) for g in range(groups)])]
    squeeze x1 -> x0, local copies, waits for them, and re-layouts: 4.98 us -> none  [body(): lax.dynamic_index_in_dim(blocks, 1 - core, 1, keepdims=False)]
    ppermute x6, starting transfers between devices: 11.2 us -> 8 us  [store(): return lax.ppermute(x, 'store', [(g, g ^ k) for g in range(groups)])]
  transfers between devices with their start and end apart: 54 -> 46, of which waited for: 13 -> 20; matrix products, arithmetic and copies ran while one was open for 2% -> 0% of each run, Pallas kernels for 41% -> 17%
where the time goes in v2:
time: 154 us; the launch traced here: 153 us
  waiting for transfers between devices  71.1 us (46%)
  starting transfers between devices  48.3 us (31%)
  Pallas kernels  32.5 us (21%)
    ppermute x32, waiting for transfers between devices, mp(): return lax.ppermute(x, 'mp', [(i, pairs_of(i)) for i in range(parts)])  35.3 us
    pallas_call x41, Pallas kernels, call(): pl.pallas_call(kernel, out_shape=shapes, in_specs=specs, out_specs=[IN_VM...  32.5 us
    ppermute x32, starting transfers between devices, mp(): return lax.ppermute(x, 'mp', [(i, pairs_of(i)) for i in range(parts)])  28.4 us
    ppermute x6, waiting for transfers between devices, store(): return lax.ppermute(x, 'store', [(g, g ^ k) for g in range(groups)])  21.4 us
    ppermute x8, waiting for transfers between devices, send(): return lax.ppermute(x, 'store', pairs)  14.4 us
    ppermute x8, starting transfers between devices, send(): return lax.ppermute(x, 'store', pairs)  11.9 us
    ppermute x6, starting transfers between devices, store(): return lax.ppermute(x, 'store', [(g, g ^ k) for g in range(groups)])  8 us
  transfers between devices with their start and end apart: 46, of which 20 were waited for; matrix products, arithmetic and copies ran while one was open for 0% of the time, Pallas kernels for 17%

profile of v2, /device:TPU:0, one launch (start us, length us, event | category | flops | bytes accessed | tf_op | source)
XLA Modules:
  0.0 153.3 jit_solution(4208777185220618971)
XLA Ops:
  0.7 2.0 %front.1 = (bf16[256,768]{1,0:T(8,128)(2,1)S(1)}, bf16[256,768]{1,0:T(8,128)(2,1)S(1)}, bf16[256,256]{1,0:T(8,128)(2,1)S(1)}, bf16[64,896]{1,0:T(8,128)(2,1)S(1)...) custom-call(s32[4,4]{1,0:T(4,128)S(1)} %copy-done.3, ...), custom_call_target="tpu_custom_call" | custom-call | tf_op jit(solution)/shard_map/front/pallas_call | solution.py:42
  2.7 2.5 %apart.1 = bf16[3072,768]{1,0:T(8,128)(2,1)S(1)} custom-call(bf16[6144,768]{1,0:T(8,128)(2,1)} %weight_ref.41, bf16[256,256]{1,0:T(8,128)(2,1)S(1)} %get-tuple-element.98.refs_1_.perm_ref), custom_call_target="tpu_custom_call" | custom-call | tf_op jit(solution)/shard_map/apart/pallas_call | solution.py:42
  5.8 2.6 %collective-permute-start.4 = (bf16[256,768]{1,0:T(8,128)(2,1)S(1)}, bf16[256,768]{1,0:T(8,128)(2,1)S(1)}, u32[]{:S(2)}, u32[]{:S(2)}) collective-permute-start(bf16[256,768]{1,0:T(8,128)(2,1)S(1)} %get-tuple-element.103), channel_id=1, source_target_pairs={{0,8},{8,0},{16,24},{24,16},{1,9},{9,1},{17,25},{25,17},{2,10},{10... | collective-permute-start | bytes 1179656 | tf_op jit(solution)/shard_map/ppermute | solution.py:206
  8.5 2.9 %collective-permute-start.2 = (bf16[64,896]{1,0:T(8,128)(2,1)S(1)}, bf16[64,896]{1,0:T(8,128)(2,1)S(1)}, u32[]{:S(2)}, u32[]{:S(2)}) collective-permute-start(bf16[64,896]{1,0:T(8,128)(2,1)S(1)} %get-tuple-element.101), channel_id=1, source_target_pairs={{0,16},{8,24},{16,0},{24,8},{1,17},{9,25},{17,1},{25,9},{2,18},{10... | collective-permute-start | bytes 344072 | tf_op jit(solution)/shard_map/ppermute | solution.py:420
  11.4 1.3 collective-permute-start.3
  12.8 10.2 %collective-permute-done.1.refs_2_.refs_3_ = bf16[64,896]{1,0:T(8,128)(2,1)S(1)} collective-permute-done((bf16[64,896]{1,0:T(8,128)(2,1)S(1)}, bf16[64,896]{1,0:T(8,128)(2,1)S(1)}, u32[]{:S(2)}, u32[]{:S(2)}) %collective-permute-start.1) | collective-permute-done | bytes 114720 | tf_op jit(solution)/shard_map/ppermute | solution.py:420
  23.0 4.7 %collective-permute-done.3.refs_4_.refs_5_ = bf16[64,896]{1,0:T(8,128)(2,1)S(1)} collective-permute-done((bf16[64,896]{1,0:T(8,128)(2,1)S(1)}, bf16[64,896]{1,0:T(8,128)(2,1)S(1)}, u32[]{:S(2)}, u32[]{:S(2)}) %collective-permute-start.3) | collective-permute-done | bytes 114720 | tf_op jit(solution)/shard_map/ppermute | solution.py:420
  27.9 1.5 %collective-permute-start.5 = (bf16[288,768]{1,0:T(8,128)(2,1)S(1)}, bf16[288,768]{1,0:T(8,128)(2,1)S(1)}, u32[]{:S(2)}, u32[]{:S(2)}) collective-permute-start(bf16[288,768]{1,0:T(8,128)(2,1)S(1)} %get-tuple-element.104.refs_0_.msg_ref), channel_id=1, source_target_pairs={{0,2},{1,5},{2,0},{3,7},{4,6},{5,1},{6,4},{7,3},{8,10},{9,13},{10,... | collective-permute-start | bytes 1327112 | tf_op jit(solution)/shard_map/ppermute | solution.py:408
  29.5 1.5 collective-permute-start.7
  31.0 1.3 collective-permute-start.9
  32.3 8.7 %collective-permute-done.5.refs_0_ = bf16[288,768]{1,0:T(8,128)(2,1)S(1)} collective-permute-done((bf16[288,768]{1,0:T(8,128)(2,1)S(1)}, bf16[288,768]{1,0:T(8,128)(2,1)S(1)}, u32[]{:S(2)}, u32[]{:S(2)}) %collective-permute-start.5) | collective-permute-done | bytes 442400 | tf_op jit(solution)/shard_map/ppermute | solution.py:408
  42.4 3.9 %collective-permute-start.13 = (bf16[256,768]{1,0:T(8,128)(2,1)S(1)}, bf16[256,768]{1,0:T(8,128)(2,1)S(1)}, u32[]{:S(2)}, u32[]{:S(2)}) collective-permute-start(bf16[256,768]{1,0:T(8,128)(2,1)S(1)} %get-tuple-element.118), channel_id=1, source_target_pairs={{0,8},{24,16},{1,9},{25,17},{2,10},{26,18},{3,11},{27,19},{4,12},{... | collective-permute-start | bytes 1179656 | tf_op jit(solution)/shard_map/ppermute | solution.py:206
  48.6 1.3 collective-permute-start.11
  50.7 1.4 blocks.22
  53.1 4.2 %collective-permute-done.13.refs_1_.high_ref = bf16[256,768]{1,0:T(8,128)(2,1)S(1)} collective-permute-done((bf16[256,768]{1,0:T(8,128)(2,1)S(1)}, bf16[256,768]{1,0:T(8,128)(2,1)S(1)}, u32[]{:S(2)}, u32[]{:S(2)}) %collective-permute-start.13) | collective-permute-done | bytes 393248 | tf_op jit(solution)/shard_map/ppermute | solution.py:206
  59.5 1.3 collective-permute-start.15
  60.8 6.9 %collective-permute-done.11.far_ref = bf16[256,768]{1,0:T(8,128)(2,1)S(1)} collective-permute-done((bf16[256,768]{1,0:T(8,128)(2,1)S(1)}, bf16[256,768]{1,0:T(8,128)(2,1)S(1)}, u32[]{:S(2)}, u32[]{:S(2)}) %collective-permute-start.11) | collective-permute-done | bytes 393248 | tf_op jit(solution)/shard_map/ppermute | solution.py:206
  69.4 4.3 %collective-permute-done.16 = f32[64,256]{1,0:T(8,128)S(1)} collective-permute-done((f32[64,256]{1,0:T(8,128)S(1)}, f32[64,256]{1,0:T(8,128)S(1)}, u32[]{:S(2)}, u32[]{:S(2)}) %collective-permute-start.16) | collective-permute-done | bytes 65568 | tf_op jit(solution)/shard_map/ppermute | solution.py:408
  73.7 1.7 %collective-permute-start.17 = (f32[64,256]{1,0:T(8,128)S(1)}, f32[64,256]{1,0:T(8,128)S(1)}, u32[]{:S(2)}, u32[]{:S(2)}) collective-permute-start(f32[64,256]{1,0:T(8,128)S(1)} %add.9), channel_id=1, source_target_pairs={{0,4},{1,5},{2,6},{3,7},{4,0},{5,1},{6,2},{7,3},{8,12},{9,13},{10,... | collective-permute-start | bytes 196616 | tf_op jit(solution)/shard_map/ppermute | solution.py:408
  75.3 2.7 %collective-permute-done.17 = f32[64,256]{1,0:T(8,128)S(1)} collective-permute-done((f32[64,256]{1,0:T(8,128)S(1)}, f32[64,256]{1,0:T(8,128)S(1)}, u32[]{:S(2)}, u32[]{:S(2)}) %collective-permute-start.17) | collective-permute-done | bytes 65568 | tf_op jit(solution)/shard_map/ppermute | solution.py:408
  78.1 3.4 %collective-permute-done.15.far_ref = bf16[256,768]{1,0:T(8,128)(2,1)S(1)} collective-permute-done((bf16[256,768]{1,0:T(8,128)(2,1)S(1)}, bf16[256,768]{1,0:T(8,128)(2,1)S(1)}, u32[]{:S(2)}, u32[]{:S(2)}) %collective-permute-start.15) | collective-permute-done | bytes 393248 | tf_op jit(solution)/shard_map/ppermute | solution.py:206
  81.5 1.0 pick.13.upc_ref
  84.7 1.8 %collective-permute-start.19 = (bf16[144,768]{1,0:T(8,128)(2,1)S(1)}, bf16[144,768]{1,0:T(8,128)(2,1)S(1)}, u32[]{:S(2)}, u32[]{:S(2)}) collective-permute-start(bf16[144,768]{1,0:T(8,128)(2,1)S(1)} %get-tuple-element.120.refs_0_), channel_id=1, source_target_pairs={{0,2},{1,5},{2,0},{3,7},{4,6},{5,1},{6,4},{7,3},{8,10},{9,13},{10,... | collective-permute-start | bytes 663560 | tf_op jit(solution)/shard_map/ppermute | solution.py:408
  86.5 1.5 collective-permute-start.34
  88.0 3.9 %collective-permute-done.32.refs_0_ = bf16[144,768]{1,0:T(8,128)(2,1)S(1)} collective-permute-done((bf16[144,768]{1,0:T(8,128)(2,1)S(1)}, bf16[144,768]{1,0:T(8,128)(2,1)S(1)}, u32[]{:S(2)}, u32[]{:S(2)}) %collective-permute-start.32) | collective-permute-done | bytes 221216 | tf_op jit(solution)/shard_map/ppermute | solution.py:408
  91.9 1.5 collective-permute-start.33
  93.9 2.7 %collective-permute-done.19.refs_0_ = bf16[144,768]{1,0:T(8,128)(2,1)S(1)} collective-permute-done((bf16[144,768]{1,0:T(8,128)(2,1)S(1)}, bf16[144,768]{1,0:T(8,128)(2,1)S(1)}, u32[]{:S(2)}, u32[]{:S(2)}) %collective-permute-start.19) | collective-permute-done | bytes 221216 | tf_op jit(solution)/shard_map/ppermute | solution.py:408
  96.6 1.5 collective-permute-start.20
  101.4 1.1 collective-permute-done.20.refs_0_
  103.1 0.9 finish.13
  105.4 1.6 %collective-permute-start.23 = (bf16[144,768]{1,0:T(8,128)(2,1)S(1)}, bf16[144,768]{1,0:T(8,128)(2,1)S(1)}, u32[]{:S(2)}, u32[]{:S(2)}) collective-permute-start(bf16[144,768]{1,0:T(8,128)(2,1)S(1)} %get-tuple-element.131.refs_0_), channel_id=1, source_target_pairs={{0,2},{1,5},{2,0},{3,7},{4,6},{5,1},{6,4},{7,3},{8,10},{9,13},{10,... | collective-permute-start | bytes 663560 | tf_op jit(solution)/shard_map/ppermute | solution.py:408
  107.1 1.5 collective-permute-start.38
  108.6 1.8 %collective-permute-done.36.refs_0_ = bf16[144,768]{1,0:T(8,128)(2,1)S(1)} collective-permute-done((bf16[144,768]{1,0:T(8,128)(2,1)S(1)}, bf16[144,768]{1,0:T(8,128)(2,1)S(1)}, u32[]{:S(2)}, u32[]{:S(2)}) %collective-permute-start.36) | collective-permute-done | bytes 221216 | tf_op jit(solution)/shard_map/ppermute | solution.py:408
  110.4 1.5 collective-permute-start.37
  112.4 2.7 %collective-permute-done.23.refs_0_ = bf16[144,768]{1,0:T(8,128)(2,1)S(1)} collective-permute-done((bf16[144,768]{1,0:T(8,128)(2,1)S(1)}, bf16[144,768]{1,0:T(8,128)(2,1)S(1)}, u32[]{:S(2)}, u32[]{:S(2)}) %collective-permute-start.23) | collective-permute-done | bytes 221216 | tf_op jit(solution)/shard_map/ppermute | solution.py:408
  115.1 1.5 collective-permute-start.24
  119.9 1.5 collective-permute-done.24.refs_0_
  124.3 1.9 %collective-permute-start.27 = (bf16[144,768]{1,0:T(8,128)(2,1)S(1)}, bf16[144,768]{1,0:T(8,128)(2,1)S(1)}, u32[]{:S(2)}, u32[]{:S(2)}) collective-permute-start(bf16[144,768]{1,0:T(8,128)(2,1)S(1)} %get-tuple-element.142.refs_0_), channel_id=1, source_target_pairs={{0,2},{1,5},{2,0},{3,7},{4,6},{5,1},{6,4},{7,3},{8,10},{9,13},{10,... | collective-permute-start | bytes 663560 | tf_op jit(solution)/shard_map/ppermute | solution.py:408
  126.2 1.5 collective-permute-start.42
  127.7 2.0 %collective-permute-done.40.refs_0_ = bf16[144,768]{1,0:T(8,128)(2,1)S(1)} collective-permute-done((bf16[144,768]{1,0:T(8,128)(2,1)S(1)}, bf16[144,768]{1,0:T(8,128)(2,1)S(1)}, u32[]{:S(2)}, u32[]{:S(2)}) %collective-permute-start.40) | collective-permute-done | bytes 221216 | tf_op jit(solution)/shard_map/ppermute | solution.py:408
  129.7 1.6 %collective-permute-start.41 = (bf16[144,768]{1,0:T(8,128)(2,1)S(1)}, bf16[144,768]{1,0:T(8,128)(2,1)S(1)}, u32[]{:S(2)}, u32[]{:S(2)}) collective-permute-start(bf16[144,768]{1,0:T(8,128)(2,1)S(1)} %collective-permute-done.40.refs_0_), channel_id=1, source_target_pairs={{0,4},{1,3},{2,6},{3,1},{4,0},{5,7},{6,2},{7,5},{8,12},{9,11},{10,... | collective-permute-start | bytes 663560 | tf_op jit(solution)/shard_map/ppermute | solution.py:408
  131.7 2.7 %collective-permute-done.27.refs_0_ = bf16[144,768]{1,0:T(8,128)(2,1)S(1)} collective-permute-done((bf16[144,768]{1,0:T(8,128)(2,1)S(1)}, bf16[144,768]{1,0:T(8,128)(2,1)S(1)}, u32[]{:S(2)}, u32[]{:S(2)}) %collective-permute-start.27) | collective-permute-done | bytes 221216 | tf_op jit(solution)/shard_map/ppermute | solution.py:408
  134.4 1.6 %collective-permute-start.28 = (bf16[144,768]{1,0:T(8,128)(2,1)S(1)}, bf16[144,768]{1,0:T(8,128)(2,1)S(1)}, u32[]{:S(2)}, u32[]{:S(2)}) collective-permute-start(bf16[144,768]{1,0:T(8,128)(2,1)S(1)} %collective-permute-done.27.refs_0_), channel_id=1, source_target_pairs={{0,4},{1,3},{2,6},{3,1},{4,0},{5,7},{6,2},{7,5},{8,12},{9,11},{10,... | collective-permute-start | bytes 663560 | tf_op jit(solution)/shard_map/ppermute | solution.py:408
  141.8 1.2 collective-permute-start.45
  143.4 2.4 %collective-permute-start.31 = (bf16[64,768]{1,0:T(8,128)(2,1)S(1)}, bf16[64,768]{1,0:T(8,128)(2,1)S(1)}, u32[]{:S(2)}, u32[]{:S(2)}) collective-permute-start(bf16[64,768]{1,0:T(8,128)(2,1)S(1)} %get-tuple-element.154), channel_id=1, source_target_pairs={{0,8},{8,0},{16,24},{24,16},{1,9},{9,1},{17,25},{25,17},{2,10},{10... | collective-permute-start | bytes 294920 | tf_op jit(solution)/shard_map/ppermute | solution.py:420
  145.8 4.8 %collective-permute-done.44.refs_2_ = bf16[64,768]{1,0:T(8,128)(2,1)S(1)} collective-permute-done((bf16[64,768]{1,0:T(8,128)(2,1)S(1)}, bf16[64,768]{1,0:T(8,128)(2,1)S(1)}, u32[]{:S(2)}, u32[]{:S(2)}) %collective-permute-start.44) | collective-permute-done | bytes 98336 | tf_op jit(solution)/shard_map/ppermute | solution.py:420
  150.5 1.7 %collective-permute-done.31.refs_1_ = bf16[64,768]{1,0:T(8,128)(2,1)S(1)} collective-permute-done((bf16[64,768]{1,0:T(8,128)(2,1)S(1)}, bf16[64,768]{1,0:T(8,128)(2,1)S(1)}, u32[]{:S(2)}, u32[]{:S(2)}) %collective-permute-start.31) | collective-permute-done | bytes 98336 | tf_op jit(solution)/shard_map/ppermute | solution.py:420
  152.3 1.1 unsort.1
  (105 shorter events, 31.9 us)
Async XLA Ops:
  2.7 47.3 %slice-start = ((s8[9437184]{0:T(1024)(128)(4,1)}), s8[4194304]{0:T(1024)(128)(4,1)S(1)}, s32[]{:S(2)}) async-start(s8[9437184]{0:T(1024)(128)(4,1)} %bitcast.5), calls=%async_computation | async-start | bytes 8388608
  2.7 47.2 %slice-start.1 = ((s8[9437184]{0:T(1024)(128)(4,1)}), s8[4194304]{0:T(1024)(128)(4,1)S(1)}, s32[]{:S(2)}) async-start(s8[9437184]{0:T(1024)(128)(4,1)} %bitcast.5), calls=%async_computation.1 | async-start | bytes 8388608
  5.3 22.4 %collective-permute-start = (bf16[3072,768]{1,0:T(8,128)(2,1)S(1)}, bf16[3072,768]{1,0:T(8,128)(2,1)S(1)}, u32[]{:S(2)}, u32[]{:S(2)}) collective-permute-start(bf16[3072,768]{1,0:T(8,128)(2,1)S(1)} %apart.1), channel_id=1, source_target_pairs={{0,1},{1,0},{2,3},{3,2},{4,5},{5,4},{6,7},{7,6},{8,9},{9,8},{10,11... | collective-permute-start | bytes 14155784 | tf_op jit(solution)/shard_map/ppermute | solution.py:408
  5.8 21.9 %collective-permute-start.4 = (bf16[256,768]{1,0:T(8,128)(2,1)S(1)}, bf16[256,768]{1,0:T(8,128)(2,1)S(1)}, u32[]{:S(2)}, u32[]{:S(2)}) collective-permute-start(bf16[256,768]{1,0:T(8,128)(2,1)S(1)} %get-tuple-element.103), channel_id=1, source_target_pairs={{0,8},{8,0},{16,24},{24,16},{1,9},{9,1},{17,25},{25,17},{2,10},{10... | collective-permute-start | bytes 1179656 | tf_op jit(solution)/shard_map/ppermute | solution.py:206
  8.4 14.6 %collective-permute-start.1 = (bf16[64,896]{1,0:T(8,128)(2,1)S(1)}, bf16[64,896]{1,0:T(8,128)(2,1)S(1)}, u32[]{:S(2)}, u32[]{:S(2)}) collective-permute-start(bf16[64,896]{1,0:T(8,128)(2,1)S(1)} %get-tuple-element.100), channel_id=1, source_target_pairs={{0,8},{8,0},{16,24},{24,16},{1,9},{9,1},{17,25},{25,17},{2,10},{10... | collective-permute-start | bytes 344072 | tf_op jit(solution)/shard_map/ppermute | solution.py:420
  8.5 14.5 %collective-permute-start.2 = (bf16[64,896]{1,0:T(8,128)(2,1)S(1)}, bf16[64,896]{1,0:T(8,128)(2,1)S(1)}, u32[]{:S(2)}, u32[]{:S(2)}) collective-permute-start(bf16[64,896]{1,0:T(8,128)(2,1)S(1)} %get-tuple-element.101), channel_id=1, source_target_pairs={{0,16},{8,24},{16,0},{24,8},{1,17},{9,25},{17,1},{25,9},{2,18},{10... | collective-permute-start | bytes 344072 | tf_op jit(solution)/shard_map/ppermute | solution.py:420
  11.4 16.2 %collective-permute-start.3 = (bf16[64,896]{1,0:T(8,128)(2,1)S(1)}, bf16[64,896]{1,0:T(8,128)(2,1)S(1)}, u32[]{:S(2)}, u32[]{:S(2)}) collective-permute-start(bf16[64,896]{1,0:T(8,128)(2,1)S(1)} %get-tuple-element.102), channel_id=1, source_target_pairs={{0,24},{8,16},{16,8},{24,0},{1,25},{9,17},{17,9},{25,1},{2,26},{10... | collective-permute-start | bytes 344072 | tf_op jit(solution)/shard_map/ppermute | solution.py:420
  27.9 13.1 %collective-permute-start.5 = (bf16[288,768]{1,0:T(8,128)(2,1)S(1)}, bf16[288,768]{1,0:T(8,128)(2,1)S(1)}, u32[]{:S(2)}, u32[]{:S(2)}) collective-permute-start(bf16[288,768]{1,0:T(8,128)(2,1)S(1)} %get-tuple-element.104.refs_0_.msg_ref), channel_id=1, source_target_pairs={{0,2},{1,5},{2,0},{3,7},{4,6},{5,1},{6,4},{7,3},{8,10},{9,13},{10,... | collective-permute-start | bytes 1327112 | tf_op jit(solution)/shard_map/ppermute | solution.py:408
  29.5 19.1 %collective-permute-start.7 = (bf16[288,768]{1,0:T(8,128)(2,1)S(1)}, bf16[288,768]{1,0:T(8,128)(2,1)S(1)}, u32[]{:S(2)}, u32[]{:S(2)}) collective-permute-start(bf16[288,768]{1,0:T(8,128)(2,1)S(1)} %get-tuple-element.104.refs_0_.msg_ref), channel_id=1, source_target_pairs={{0,4},{1,3},{2,6},{3,1},{4,0},{5,7},{6,2},{7,5},{8,12},{9,11},{10,... | collective-permute-start | bytes 1327112 | tf_op jit(solution)/shard_map/ppermute | solution.py:408
  31.0 15.3 %collective-permute-start.9 = (bf16[256,768]{1,0:T(8,128)(2,1)S(1)}, bf16[256,768]{1,0:T(8,128)(2,1)S(1)}, u32[]{:S(2)}, u32[]{:S(2)}) collective-permute-start(bf16[256,768]{1,0:T(8,128)(2,1)S(1)} %get-tuple-element.116), channel_id=1, source_target_pairs={{0,8},{24,16},{1,9},{25,17},{2,10},{26,18},{3,11},{27,19},{4,12},{... | collective-permute-start | bytes 1179656 | tf_op jit(solution)/shard_map/ppermute | solution.py:206
  41.0 11.2 %collective-permute-start.6 = (bf16[288,768]{1,0:T(8,128)(2,1)S(1)}, bf16[288,768]{1,0:T(8,128)(2,1)S(1)}, u32[]{:S(2)}, u32[]{:S(2)}) collective-permute-start(bf16[288,768]{1,0:T(8,128)(2,1)S(1)} %collective-permute-done.5.refs_0_), channel_id=1, source_target_pairs={{0,4},{1,3},{2,6},{3,1},{4,0},{5,7},{6,2},{7,5},{8,12},{9,11},{10,... | collective-permute-start | bytes 1327112 | tf_op jit(solution)/shard_map/ppermute | solution.py:408
  42.3 10.8 %collective-permute-start.12 = (bf16[256,768]{1,0:T(8,128)(2,1)S(1)}, bf16[256,768]{1,0:T(8,128)(2,1)S(1)}, u32[]{:S(2)}, u32[]{:S(2)}) collective-permute-start(bf16[256,768]{1,0:T(8,128)(2,1)S(1)} %get-tuple-element.117), channel_id=1, source_target_pairs={{0,8},{8,0},{16,24},{24,16},{1,9},{9,1},{17,25},{25,17},{2,10},{10... | collective-permute-start | bytes 1179656 | tf_op jit(solution)/shard_map/ppermute | solution.py:206
  42.4 14.9 %collective-permute-start.13 = (bf16[256,768]{1,0:T(8,128)(2,1)S(1)}, bf16[256,768]{1,0:T(8,128)(2,1)S(1)}, u32[]{:S(2)}, u32[]{:S(2)}) collective-permute-start(bf16[256,768]{1,0:T(8,128)(2,1)S(1)} %get-tuple-element.118), channel_id=1, source_target_pairs={{0,8},{24,16},{1,9},{25,17},{2,10},{26,18},{3,11},{27,19},{4,12},{... | collective-permute-start | bytes 1179656 | tf_op jit(solution)/shard_map/ppermute | solution.py:206
  47.1 13.7 %collective-permute-start.10 = (bf16[256,768]{1,0:T(8,128)(2,1)S(1)}, bf16[256,768]{1,0:T(8,128)(2,1)S(1)}, u32[]{:S(2)}, u32[]{:S(2)}) collective-permute-start(bf16[256,768]{1,0:T(8,128)(2,1)S(1)} %pick.7), channel_id=1, source_target_pairs={{8,16},{16,8},{9,17},{17,9},{10,18},{18,10},{11,19},{19,11},{12,20... | collective-permute-start | bytes 1179656 | tf_op jit(solution)/shard_map/ppermute | solution.py:206
  48.6 19.1 %collective-permute-start.11 = (bf16[256,768]{1,0:T(8,128)(2,1)S(1)}, bf16[256,768]{1,0:T(8,128)(2,1)S(1)}, u32[]{:S(2)}, u32[]{:S(2)}) collective-permute-start(bf16[256,768]{1,0:T(8,128)(2,1)S(1)} %pick.8), channel_id=1, source_target_pairs={{8,24},{16,0},{9,25},{17,1},{10,26},{18,2},{11,27},{19,3},{12,28},... | collective-permute-start | bytes 1179656 | tf_op jit(solution)/shard_map/ppermute | solution.py:206
  53.0 29.5 %collective-permute-start.8 = (bf16[288,768]{1,0:T(8,128)(2,1)S(1)}, bf16[288,768]{1,0:T(8,128)(2,1)S(1)}, u32[]{:S(2)}, u32[]{:S(2)}) collective-permute-start(bf16[288,768]{1,0:T(8,128)(2,1)S(1)} %get-tuple-element.113), channel_id=1, source_target_pairs={{0,1},{1,0},{2,3},{3,2},{4,5},{5,4},{6,7},{7,6},{8,9},{9,8},{10,11... | collective-permute-start | bytes 1327112 | tf_op jit(solution)/shard_map/ppermute | solution.py:408
  58.1 20.0 %collective-permute-start.14 = (bf16[256,768]{1,0:T(8,128)(2,1)S(1)}, bf16[256,768]{1,0:T(8,128)(2,1)S(1)}, u32[]{:S(2)}, u32[]{:S(2)}) collective-permute-start(bf16[256,768]{1,0:T(8,128)(2,1)S(1)} %pick.11), channel_id=1, source_target_pairs={{8,16},{16,8},{9,17},{17,9},{10,18},{18,10},{11,19},{19,11},{12,20... | collective-permute-start | bytes 1179656 | tf_op jit(solution)/shard_map/ppermute | solution.py:206
  59.5 22.0 %collective-permute-start.15 = (bf16[256,768]{1,0:T(8,128)(2,1)S(1)}, bf16[256,768]{1,0:T(8,128)(2,1)S(1)}, u32[]{:S(2)}, u32[]{:S(2)}) collective-permute-start(bf16[256,768]{1,0:T(8,128)(2,1)S(1)} %pick.12), channel_id=1, source_target_pairs={{8,24},{16,0},{9,25},{17,1},{10,26},{18,2},{11,27},{19,3},{12,28},... | collective-permute-start | bytes 1179656 | tf_op jit(solution)/shard_map/ppermute | solution.py:206
  69.3 4.3 %collective-permute-start.16 = (f32[64,256]{1,0:T(8,128)S(1)}, f32[64,256]{1,0:T(8,128)S(1)}, u32[]{:S(2)}, u32[]{:S(2)}) collective-permute-start(f32[64,256]{1,0:T(8,128)S(1)} %first_inner.1), channel_id=1, source_target_pairs={{0,2},{1,3},{2,0},{3,1},{4,6},{5,7},{6,4},{7,5},{8,10},{9,11},{10,... | collective-permute-start | bytes 196616 | tf_op jit(solution)/shard_map/ppermute | solution.py:408
  73.7 4.3 %collective-permute-start.17 = (f32[64,256]{1,0:T(8,128)S(1)}, f32[64,256]{1,0:T(8,128)S(1)}, u32[]{:S(2)}, u32[]{:S(2)}) collective-permute-start(f32[64,256]{1,0:T(8,128)S(1)} %add.9), channel_id=1, source_target_pairs={{0,4},{1,5},{2,6},{3,7},{4,0},{5,1},{6,2},{7,3},{8,12},{9,13},{10,... | collective-permute-start | bytes 196616 | tf_op jit(solution)/shard_map/ppermute | solution.py:408
  78.0 4.5 %collective-permute-start.18 = (f32[64,256]{1,0:T(8,128)S(1)}, f32[64,256]{1,0:T(8,128)S(1)}, u32[]{:S(2)}, u32[]{:S(2)}) collective-permute-start(f32[64,256]{1,0:T(8,128)S(1)} %add.10), channel_id=1, source_target_pairs={{0,1},{1,0},{2,3},{3,2},{4,5},{5,4},{6,7},{7,6},{8,9},{9,8},{10,11... | collective-permute-start | bytes 196616 | tf_op jit(solution)/shard_map/ppermute | solution.py:408
  83.4 8.4 %collective-permute-start.32 = (bf16[144,768]{1,0:T(8,128)(2,1)S(1)}, bf16[144,768]{1,0:T(8,128)(2,1)S(1)}, u32[]{:S(2)}, u32[]{:S(2)}) collective-permute-start(bf16[144,768]{1,0:T(8,128)(2,1)S(1)} %get-tuple-element.156.refs_0_), channel_id=1, source_target_pairs={{0,2},{1,5},{2,0},{3,7},{4,6},{5,1},{6,4},{7,3},{8,10},{9,13},{10,... | collective-permute-start | bytes 663560 | tf_op jit(solution)/shard_map/ppermute | solution.py:408
  84.7 11.9 %collective-permute-start.19 = (bf16[144,768]{1,0:T(8,128)(2,1)S(1)}, bf16[144,768]{1,0:T(8,128)(2,1)S(1)}, u32[]{:S(2)}, u32[]{:S(2)}) collective-permute-start(bf16[144,768]{1,0:T(8,128)(2,1)S(1)} %get-tuple-element.120.refs_0_), channel_id=1, source_target_pairs={{0,2},{1,5},{2,0},{3,7},{4,6},{5,1},{6,4},{7,3},{8,10},{9,13},{10,... | collective-permute-start | bytes 663560 | tf_op jit(solution)/shard_map/ppermute | solution.py:408
  86.5 12.6 %collective-permute-start.34 = (bf16[144,768]{1,0:T(8,128)(2,1)S(1)}, bf16[144,768]{1,0:T(8,128)(2,1)S(1)}, u32[]{:S(2)}, u32[]{:S(2)}) collective-permute-start(bf16[144,768]{1,0:T(8,128)(2,1)S(1)} %get-tuple-element.156.refs_0_), channel_id=1, source_target_pairs={{0,4},{1,3},{2,6},{3,1},{4,0},{5,7},{6,2},{7,5},{8,12},{9,11},{10,... | collective-permute-start | bytes 663560 | tf_op jit(solution)/shard_map/ppermute | solution.py:408
  91.9 8.1 %collective-permute-start.33 = (bf16[144,768]{1,0:T(8,128)(2,1)S(1)}, bf16[144,768]{1,0:T(8,128)(2,1)S(1)}, u32[]{:S(2)}, u32[]{:S(2)}) collective-permute-start(bf16[144,768]{1,0:T(8,128)(2,1)S(1)} %collective-permute-done.32.refs_0_), channel_id=1, source_target_pairs={{0,4},{1,3},{2,6},{3,1},{4,0},{5,7},{6,2},{7,5},{8,12},{9,11},{10,... | collective-permute-start | bytes 663560 | tf_op jit(solution)/shard_map/ppermute | solution.py:408
  93.4 7.2 %collective-permute-start.21 = (bf16[144,768]{1,0:T(8,128)(2,1)S(1)}, bf16[144,768]{1,0:T(8,128)(2,1)S(1)}, u32[]{:S(2)}, u32[]{:S(2)}) collective-permute-start(bf16[144,768]{1,0:T(8,128)(2,1)S(1)} %get-tuple-element.120.refs_0_), channel_id=1, source_target_pairs={{0,4},{1,3},{2,6},{3,1},{4,0},{5,7},{6,2},{7,5},{8,12},{9,11},{10,... | collective-permute-start | bytes 663560 | tf_op jit(solution)/shard_map/ppermute | solution.py:408
  96.6 5.9 %collective-permute-start.20 = (bf16[144,768]{1,0:T(8,128)(2,1)S(1)}, bf16[144,768]{1,0:T(8,128)(2,1)S(1)}, u32[]{:S(2)}, u32[]{:S(2)}) collective-permute-start(bf16[144,768]{1,0:T(8,128)(2,1)S(1)} %collective-permute-done.19.refs_0_), channel_id=1, source_target_pairs={{0,4},{1,3},{2,6},{3,1},{4,0},{5,7},{6,2},{7,5},{8,12},{9,11},{10,... | collective-permute-start | bytes 663560 | tf_op jit(solution)/shard_map/ppermute | solution.py:408
  100.5 2.6 %collective-permute-start.35 = (bf16[144,768]{1,0:T(8,128)(2,1)S(1)}, bf16[144,768]{1,0:T(8,128)(2,1)S(1)}, u32[]{:S(2)}, u32[]{:S(2)}) collective-permute-start(bf16[144,768]{1,0:T(8,128)(2,1)S(1)} %get-tuple-element.165), channel_id=1, source_target_pairs={{0,1},{1,0},{2,3},{3,2},{4,5},{5,4},{6,7},{7,6},{8,9},{9,8},{10,11... | collective-permute-start | bytes 663560 | tf_op jit(solution)/shard_map/ppermute | solution.py:408
  103.0 1.5 %collective-permute-start.22 = (bf16[144,768]{1,0:T(8,128)(2,1)S(1)}, bf16[144,768]{1,0:T(8,128)(2,1)S(1)}, u32[]{:S(2)}, u32[]{:S(2)}) collective-permute-start(bf16[144,768]{1,0:T(8,128)(2,1)S(1)} %get-tuple-element.129), channel_id=1, source_target_pairs={{0,1},{1,0},{2,3},{3,2},{4,5},{5,4},{6,7},{7,6},{8,9},{9,8},{10,11... | collective-permute-start | bytes 663560 | tf_op jit(solution)/shard_map/ppermute | solution.py:408
  104.0 6.4 %collective-permute-start.36 = (bf16[144,768]{1,0:T(8,128)(2,1)S(1)}, bf16[144,768]{1,0:T(8,128)(2,1)S(1)}, u32[]{:S(2)}, u32[]{:S(2)}) collective-permute-start(bf16[144,768]{1,0:T(8,128)(2,1)S(1)} %get-tuple-element.167.refs_0_), channel_id=1, source_target_pairs={{0,2},{1,5},{2,0},{3,7},{4,6},{5,1},{6,4},{7,3},{8,10},{9,13},{10,... | collective-permute-start | bytes 663560 | tf_op jit(solution)/shard_map/ppermute | solution.py:408
  105.4 9.7 %collective-permute-start.23 = (bf16[144,768]{1,0:T(8,128)(2,1)S(1)}, bf16[144,768]{1,0:T(8,128)(2,1)S(1)}, u32[]{:S(2)}, u32[]{:S(2)}) collective-permute-start(bf16[144,768]{1,0:T(8,128)(2,1)S(1)} %get-tuple-element.131.refs_0_), channel_id=1, source_target_pairs={{0,2},{1,5},{2,0},{3,7},{4,6},{5,1},{6,4},{7,3},{8,10},{9,13},{10,... | collective-permute-start | bytes 663560 | tf_op jit(solution)/shard_map/ppermute | solution.py:408
  107.1 10.6 %collective-permute-start.38 = (bf16[144,768]{1,0:T(8,128)(2,1)S(1)}, bf16[144,768]{1,0:T(8,128)(2,1)S(1)}, u32[]{:S(2)}, u32[]{:S(2)}) collective-permute-start(bf16[144,768]{1,0:T(8,128)(2,1)S(1)} %get-tuple-element.167.refs_0_), channel_id=1, source_target_pairs={{0,4},{1,3},{2,6},{3,1},{4,0},{5,7},{6,2},{7,5},{8,12},{9,11},{10,... | collective-permute-start | bytes 663560 | tf_op jit(solution)/shard_map/ppermute | solution.py:408
  110.4 8.1 %collective-permute-start.37 = (bf16[144,768]{1,0:T(8,128)(2,1)S(1)}, bf16[144,768]{1,0:T(8,128)(2,1)S(1)}, u32[]{:S(2)}, u32[]{:S(2)}) collective-permute-start(bf16[144,768]{1,0:T(8,128)(2,1)S(1)} %collective-permute-done.36.refs_0_), channel_id=1, source_target_pairs={{0,4},{1,3},{2,6},{3,1},{4,0},{5,7},{6,2},{7,5},{8,12},{9,11},{10,... | collective-permute-start | bytes 663560 | tf_op jit(solution)/shard_map/ppermute | solution.py:408
  111.9 7.2 %collective-permute-start.25 = (bf16[144,768]{1,0:T(8,128)(2,1)S(1)}, bf16[144,768]{1,0:T(8,128)(2,1)S(1)}, u32[]{:S(2)}, u32[]{:S(2)}) collective-permute-start(bf16[144,768]{1,0:T(8,128)(2,1)S(1)} %get-tuple-element.131.refs_0_), channel_id=1, source_target_pairs={{0,4},{1,3},{2,6},{3,1},{4,0},{5,7},{6,2},{7,5},{8,12},{9,11},{10,... | collective-permute-start | bytes 663560 | tf_op jit(solution)/shard_map/ppermute | solution.py:408
  115.1 6.3 %collective-permute-start.24 = (bf16[144,768]{1,0:T(8,128)(2,1)S(1)}, bf16[144,768]{1,0:T(8,128)(2,1)S(1)}, u32[]{:S(2)}, u32[]{:S(2)}) collective-permute-start(bf16[144,768]{1,0:T(8,128)(2,1)S(1)} %collective-permute-done.23.refs_0_), channel_id=1, source_target_pairs={{0,4},{1,3},{2,6},{3,1},{4,0},{5,7},{6,2},{7,5},{8,12},{9,11},{10,... | collective-permute-start | bytes 663560 | tf_op jit(solution)/shard_map/ppermute | solution.py:408
  119.0 3.3 %collective-permute-start.39 = (bf16[144,768]{1,0:T(8,128)(2,1)S(1)}, bf16[144,768]{1,0:T(8,128)(2,1)S(1)}, u32[]{:S(2)}, u32[]{:S(2)}) collective-permute-start(bf16[144,768]{1,0:T(8,128)(2,1)S(1)} %get-tuple-element.176), channel_id=1, source_target_pairs={{0,1},{1,0},{2,3},{3,2},{4,5},{5,4},{6,7},{7,6},{8,9},{9,8},{10,11... | collective-permute-start | bytes 663560 | tf_op jit(solution)/shard_map/ppermute | solution.py:408
  121.9 1.5 %collective-permute-start.26 = (bf16[144,768]{1,0:T(8,128)(2,1)S(1)}, bf16[144,768]{1,0:T(8,128)(2,1)S(1)}, u32[]{:S(2)}, u32[]{:S(2)}) collective-permute-start(bf16[144,768]{1,0:T(8,128)(2,1)S(1)} %get-tuple-element.140), channel_id=1, source_target_pairs={{0,1},{1,0},{2,3},{3,2},{4,5},{5,4},{6,7},{7,6},{8,9},{9,8},{10,11... | collective-permute-start | bytes 663560 | tf_op jit(solution)/shard_map/ppermute | solution.py:408
  123.1 6.6 %collective-permute-start.40 = (bf16[144,768]{1,0:T(8,128)(2,1)S(1)}, bf16[144,768]{1,0:T(8,128)(2,1)S(1)}, u32[]{:S(2)}, u32[]{:S(2)}) collective-permute-start(bf16[144,768]{1,0:T(8,128)(2,1)S(1)} %get-tuple-element.178.refs_0_), channel_id=1, source_target_pairs={{0,2},{1,5},{2,0},{3,7},{4,6},{5,1},{6,4},{7,3},{8,10},{9,13},{10,... | collective-permute-start | bytes 663560 | tf_op jit(solution)/shard_map/ppermute | solution.py:408
  124.3 10.2 %collective-permute-start.27 = (bf16[144,768]{1,0:T(8,128)(2,1)S(1)}, bf16[144,768]{1,0:T(8,128)(2,1)S(1)}, u32[]{:S(2)}, u32[]{:S(2)}) collective-permute-start(bf16[144,768]{1,0:T(8,128)(2,1)S(1)} %get-tuple-element.142.refs_0_), channel_id=1, source_target_pairs={{0,2},{1,5},{2,0},{3,7},{4,6},{5,1},{6,4},{7,3},{8,10},{9,13},{10,... | collective-permute-start | bytes 663560 | tf_op jit(solution)/shard_map/ppermute | solution.py:408
  126.2 11.1 %collective-permute-start.42 = (bf16[144,768]{1,0:T(8,128)(2,1)S(1)}, bf16[144,768]{1,0:T(8,128)(2,1)S(1)}, u32[]{:S(2)}, u32[]{:S(2)}) collective-permute-start(bf16[144,768]{1,0:T(8,128)(2,1)S(1)} %get-tuple-element.178.refs_0_), channel_id=1, source_target_pairs={{0,4},{1,3},{2,6},{3,1},{4,0},{5,7},{6,2},{7,5},{8,12},{9,11},{10,... | collective-permute-start | bytes 663560 | tf_op jit(solution)/shard_map/ppermute | solution.py:408
  129.7 8.4 %collective-permute-start.41 = (bf16[144,768]{1,0:T(8,128)(2,1)S(1)}, bf16[144,768]{1,0:T(8,128)(2,1)S(1)}, u32[]{:S(2)}, u32[]{:S(2)}) collective-permute-start(bf16[144,768]{1,0:T(8,128)(2,1)S(1)} %collective-permute-done.40.refs_0_), channel_id=1, source_target_pairs={{0,4},{1,3},{2,6},{3,1},{4,0},{5,7},{6,2},{7,5},{8,12},{9,11},{10,... | collective-permute-start | bytes 663560 | tf_op jit(solution)/shard_map/ppermute | solution.py:408
  131.3 7.4 %collective-permute-start.29 = (bf16[144,768]{1,0:T(8,128)(2,1)S(1)}, bf16[144,768]{1,0:T(8,128)(2,1)S(1)}, u32[]{:S(2)}, u32[]{:S(2)}) collective-permute-start(bf16[144,768]{1,0:T(8,128)(2,1)S(1)} %get-tuple-element.142.refs_0_), channel_id=1, source_target_pairs={{0,4},{1,3},{2,6},{3,1},{4,0},{5,7},{6,2},{7,5},{8,12},{9,11},{10,... | collective-permute-start | bytes 663560 | tf_op jit(solution)/shard_map/ppermute | solution.py:408
  134.4 5.9 %collective-permute-start.28 = (bf16[144,768]{1,0:T(8,128)(2,1)S(1)}, bf16[144,768]{1,0:T(8,128)(2,1)S(1)}, u32[]{:S(2)}, u32[]{:S(2)}) collective-permute-start(bf16[144,768]{1,0:T(8,128)(2,1)S(1)} %collective-permute-done.27.refs_0_), channel_id=1, source_target_pairs={{0,4},{1,3},{2,6},{3,1},{4,0},{5,7},{6,2},{7,5},{8,12},{9,11},{10,... | collective-permute-start | bytes 663560 | tf_op jit(solution)/shard_map/ppermute | solution.py:408
  138.6 2.7 %collective-permute-start.43 = (bf16[144,768]{1,0:T(8,128)(2,1)S(1)}, bf16[144,768]{1,0:T(8,128)(2,1)S(1)}, u32[]{:S(2)}, u32[]{:S(2)}) collective-permute-start(bf16[144,768]{1,0:T(8,128)(2,1)S(1)} %get-tuple-element.187), channel_id=1, source_target_pairs={{0,1},{1,0},{2,3},{3,2},{4,5},{5,4},{6,7},{7,6},{8,9},{9,8},{10,11... | collective-permute-start | bytes 663560 | tf_op jit(solution)/shard_map/ppermute | solution.py:408
  140.9 2.1 %collective-permute-start.30 = (bf16[144,768]{1,0:T(8,128)(2,1)S(1)}, bf16[144,768]{1,0:T(8,128)(2,1)S(1)}, u32[]{:S(2)}, u32[]{:S(2)}) collective-permute-start(bf16[144,768]{1,0:T(8,128)(2,1)S(1)} %get-tuple-element.151), channel_id=1, source_target_pairs={{0,1},{1,0},{2,3},{3,2},{4,5},{5,4},{6,7},{7,6},{8,9},{9,8},{10,11... | collective-permute-start | bytes 663560 | tf_op jit(solution)/shard_map/ppermute | solution.py:408
  141.8 8.8 %collective-permute-start.44 = (bf16[64,768]{1,0:T(8,128)(2,1)S(1)}, bf16[64,768]{1,0:T(8,128)(2,1)S(1)}, u32[]{:S(2)}, u32[]{:S(2)}) collective-permute-start(bf16[64,768]{1,0:T(8,128)(2,1)S(1)} %get-tuple-element.189), channel_id=1, source_target_pairs={{0,16},{8,24},{16,0},{24,8},{1,17},{9,25},{17,1},{25,9},{2,18},{10... | collective-permute-start | bytes 294920 | tf_op jit(solution)/shard_map/ppermute | solution.py:420
  141.8 8.7 %collective-permute-start.45 = (bf16[64,768]{1,0:T(8,128)(2,1)S(1)}, bf16[64,768]{1,0:T(8,128)(2,1)S(1)}, u32[]{:S(2)}, u32[]{:S(2)}) collective-permute-start(bf16[64,768]{1,0:T(8,128)(2,1)S(1)} %get-tuple-element.190), channel_id=1, source_target_pairs={{0,24},{8,16},{16,8},{24,0},{1,25},{9,17},{17,9},{25,1},{2,26},{10... | collective-permute-start | bytes 294920 | tf_op jit(solution)/shard_map/ppermute | solution.py:420
  143.4 8.9 %collective-permute-start.31 = (bf16[64,768]{1,0:T(8,128)(2,1)S(1)}, bf16[64,768]{1,0:T(8,128)(2,1)S(1)}, u32[]{:S(2)}, u32[]{:S(2)}) collective-permute-start(bf16[64,768]{1,0:T(8,128)(2,1)S(1)} %get-tuple-element.154), channel_id=1, source_target_pairs={{0,8},{8,0},{16,24},{24,16},{1,9},{9,1},{17,25},{25,17},{2,10},{10... | collective-permute-start | bytes 294920 | tf_op jit(solution)/shard_map/ppermute | solution.py:420
  (6 other events, 161.5 us)

commit v3 on v2

--- a/solution.py
+++ b/solution.py
@@ -15,6 +15,7 @@
 MIB = 2**20
 
 adapter_scale = 0.5
+ORDER_US = {'near1': 5, 'far1': 5, 'ends1': 10, 'first': 20}
 
 F32 = jnp.float32
 BF16 = jnp.bfloat16
@@ -46,7 +47,7 @@
         out_specs=[IN_VMEM] * len(shapes),
         scratch_shapes=scratch,
         compiler_params=pltpu.CompilerParams(vmem_limit_bytes=12 * MIB),
-        cost_estimate=pl.CostEstimate(flops=0, bytes_accessed=0, transcendentals=0),
+        cost_estimate=pl.CostEstimate(flops=int(ORDER_US.get(name, 0) * 1.15e9), bytes_accessed=0, transcendentals=0),
         name=name,
     )(*args)
     return r if many else r[0]
@@ -130,9 +131,30 @@
     end_blocks(owned, plan_ref, own_ref, (low_ref, high_ref))
 
 
-def front_kernel(owned, plan_ref, own_ref, tokens_ref, target_ref, slot_ref, low_ref, high_ref, *refs):
+def front_kernel(owned, plan_ref, own_ref, tokens_ref, target_ref, slot_ref, weight_ref, *refs):
+    *refs, sems = refs
+    low_ref, high_ref, sent_ref, *refs = refs
+    copies = apart(weight_ref, sent_ref, sems)
     end_blocks(owned, plan_ref, own_ref, (low_ref, high_ref))
     sort_kernel(tokens_ref, target_ref, slot_ref, *refs)
+    for copy in copies:
+        copy.wait()
+
+
+def apart(weight_ref, sent_ref, sems):
+    width = weight_ref.shape[1]
+    other = 1 - lax.axis_index("mp") % 2
+    copies = []
+    for q in range(sent_ref.shape[0] // width):
+        start = pl.multiple_of((2 * q + other) * width, width)
+        copies.append(
+            pltpu.make_async_copy(
+                weight_ref.at[pl.ds(start, width), :], sent_ref.at[pl.ds(q * width, width), :], sems.at[q]
+            )
+        )
+    for copy in copies:
+        copy.start()
+    return copies
 
 
 def pass_kernel(owned, dest_of, n_blocks, plan_ref, own_ref, *refs):
@@ -194,49 +216,8 @@
         put(jnp.logical_and(group == end, owner != beside), lambda: far_ref[at, :])
 
 
-def fetch_copies(plan, own, owned, front):
-    copies = plan.shape[1]
-    rank = own[0].shape[0] // owned
-    shape = ((copies * rank, own[0].shape[1]), BF16)
-
-    def make(kernel, *args, out=shape, after=()):
-        return call(kernel, out, [IN_SMEM] + [IN_VMEM] * len(args), plan, *args, name="pick", after=after)
-
-    def send(x, pairs):
-        return lax.ppermute(x, "store", pairs)
-
-    def passing(dest_of, i, *blocks, after=()):
-        return make(functools.partial(pass_kernel, owned, dest_of, len(blocks)), own[i], *blocks, after=after)
-
-    pairs, ends, middle, across = [(0, 1), (1, 0), (2, 3), (3, 2)], [(0, 1), (3, 2)], [(1, 2), (2, 1)], [(1, 3), (2, 0)]
-    low, high, got = {}, {}, []
-    (low[0], high[0]), chunks, rest = front(shape)
-    low[0], high[0] = send(low[0], pairs), send(high[0], ends)
-    low[1], high[1] = make(
-        functools.partial(end_blocks_kernel, owned), own[1], out=[shape, shape], after=[low[0], *chunks[1:]]
-    )
-    low[1], high[1] = send(low[1], pairs), send(high[1], ends)
-    for i in range(2):
-        far = send(passing((3, 3, 0, 0), i, low[i]), across)
-        passed = send(passing((2, 2, 1, 1), i, low[i], high[i]), middle)
-        got.append(make(functools.partial(gather_kernel, owned), low[i], high[i], passed, far))
-    return got, chunks, rest, low[0]
-
-
 def apart_kernel(weight_ref, sent_ref, sems):
-    width = weight_ref.shape[1]
-    other = 1 - lax.axis_index("mp") % 2
-    copies = []
-    for q in range(sent_ref.shape[0] // width):
-        start = pl.multiple_of((2 * q + other) * width, width)
-        copies.append(
-            pltpu.make_async_copy(
-                weight_ref.at[pl.ds(start, width), :], sent_ref.at[pl.ds(q * width, width), :], sems.at[q]
-            )
-        )
-    for copy in copies:
-        copy.start()
-    for copy in copies:
+    for copy in apart(weight_ref, sent_ref, sems):
         copy.wait()
 
 
@@ -422,32 +403,50 @@
     down = adapter_down_weight.reshape(owned * rank, width)
     up = adapter_up_weight.reshape(owned * rank, width)
 
-    def front(shape):
-        low, high, perm, *chunks = call(
-            functools.partial(front_kernel, owned),
-            [shape, shape, ((groups * CAP, n_tokens), BF16)] + [((CAP, width + rows), BF16)] * groups,
-            [IN_SMEM] + [IN_VMEM] * 4,
-            plan,
-            *(
-                pltpu.with_memory_space_constraint(x, pltpu.HBM)
-                for x in (down, tokens, target.reshape(1, n_tokens), slot.reshape(1, n_tokens))
-            ),
-            name="front",
-        )
-        return (low, high), [c if k == 0 else store(c, k) for k, c in enumerate(chunks)], perm
-
-    (down_copy, up_copy), chunks, perm, early = fetch_copies(plan, [down, up], owned, front)
-
-    other = call(
-        apart_kernel,
-        ((parts // 2 * width, width), BF16),
-        [pl.BlockSpec(memory_space=pl.ANY)],
-        pltpu.with_memory_space_constraint(base_projection_weight, pltpu.HBM),
-        name="apart",
+    copies = plan.shape[1]
+    shape = ((copies * rank, width), BF16)
+    def pick(kernel, out, *args, name=None, after=()):
+        return call(kernel, out, [IN_SMEM] + [IN_VMEM] * len(args), plan, *args, name=name, after=after)
+
+    def line(x, pairs):
+        return lax.ppermute(x, "store", pairs)
+
+    def passing(dest_of, own, *blocks, name=None, after=()):
+        kernel = functools.partial(pass_kernel, owned, dest_of, len(blocks))
+        return pick(kernel, shape, own, *blocks, name=name, after=after)
+
+    pairs, ends, middle, across = [(0, 1), (1, 0), (2, 3), (3, 2)], [(0, 1), (3, 2)], [(1, 2), (2, 1)], [(1, 3), (2, 0)]
+    sent = ((parts // 2 * width, width), BF16)
+    far_weight = pltpu.with_memory_space_constraint(base_projection_weight, pltpu.HBM)
+    low0, high0, other, perm, *chunks = call(
+        functools.partial(front_kernel, owned),
+        [shape, shape, sent, ((groups * CAP, n_tokens), BF16)] + [((CAP, width + rows), BF16)] * groups,
+        [IN_SMEM] + [IN_VMEM] * 4 + [pl.BlockSpec(memory_space=pl.ANY)],
+        plan,
+        *(
+            pltpu.with_memory_space_constraint(x, pltpu.HBM)
+            for x in (down, tokens, target.reshape(1, n_tokens), slot.reshape(1, n_tokens))
+        ),
+        far_weight,
+        name="front",
         scratch=[pltpu.SemaphoreType.DMA((parts // 2,))],
-        after=[perm],
     )
-    weight, other = pinned(base_projection_weight), pinned(sibling(other))
+    low0 = line(low0, pairs)
+    high0 = line(high0, ends)
+    chunks = [c if k == 0 else store(c, k) for k, c in enumerate(chunks)]
+    other = sibling(other)
+    low1, high1 = pick(functools.partial(end_blocks_kernel, owned), [shape, shape], up, name="ends1", after=[low0, *chunks[1:]])
+    low1 = line(low1, pairs)
+    high1 = line(high1, ends)
+    far0 = passing((3, 3, 0, 0), down, low0, name="far0")
+    far0 = line(far0, across)
+    pass0 = passing((2, 2, 1, 1), down, low0, high0, name="near0")
+    pass0 = line(pass0, middle)
+    far1 = line(passing((3, 3, 0, 0), up, low1, name="far1"), across)
+    pass1 = line(passing((2, 2, 1, 1), up, low1, high1, name="near1"), middle)
+    down_copy = pick(functools.partial(gather_kernel, owned), shape, low0, high0, pass0, far0, name="gather0")
+    up_copy = pick(functools.partial(gather_kernel, owned), shape, low1, high1, pass1, far1, name="gather1")
+    weight, other = pinned(base_projection_weight), pinned(other)
 
     halves = range(groups // 2)
     n = len(halves)
@@ -493,7 +492,7 @@
         gain,
         *chunks,
         name="first",
-        after=[early, other],
+        after=[low0, other],
     )
     state, slots, msg = outs[:n], outs[n : 2 * n], outs[-1]
     sums = exchange(n, msg)

time: 154 us -> 146 us (0.948)
  waiting for transfers between devices: 71.1 us -> 61.6 us
  starting transfers between devices: 48.3 us -> 51.3 us
    ppermute x32, waiting for transfers between devices: 35.3 us -> 25.2 us  [mp(): return lax.ppermute(x, 'mp', [(i, pairs_of(i)) for i in range(parts)])]
    ppermute x32, starting transfers between devices: 28.4 us -> 30.6 us  [mp(): return lax.ppermute(x, 'mp', [(i, pairs_of(i)) for i in range(parts)])]
    pallas_call x41 -> x40, Pallas kernels: 32.5 us -> 31.7 us  [call(): pl.pallas_call(kernel, out_shape=shapes, in_specs=specs, out_specs=[IN_VM...]
  transfers between devices with their start and end apart: 46 -> 46, of which waited for: 20 -> 19; matrix products, arithmetic and copies ran while one was open for 0% -> 0% of each run, Pallas kernels for 17% -> 18%
where the time goes in v3:
time: 146 us
  waiting for transfers between devices  61.6 us (42%)
  starting transfers between devices  51.3 us (35%)
  Pallas kernels  31.7 us (22%)
    pallas_call x40, Pallas kernels, call(): pl.pallas_call(kernel, out_shape=shapes, in_specs=specs, out_specs=[IN_VM...  31.7 us
    ppermute x32, starting transfers between devices, mp(): return lax.ppermute(x, 'mp', [(i, pairs_of(i)) for i in range(parts)])  30.6 us
    ppermute x32, waiting for transfers between devices, mp(): return lax.ppermute(x, 'mp', [(i, pairs_of(i)) for i in range(parts)])  25.2 us
    ppermute x6, waiting for transfers between devices, store(): return lax.ppermute(x, 'store', [(g, g ^ k) for g in range(groups)])  20.7 us
    ppermute x8, waiting for transfers between devices, line(): return lax.ppermute(x, 'store', pairs)  15.7 us
    ppermute x8, starting transfers between devices, line(): return lax.ppermute(x, 'store', pairs)  12.7 us
    ppermute x6, starting transfers between devices, store(): return lax.ppermute(x, 'store', [(g, g ^ k) for g in range(groups)])  8 us
  transfers between devices with their start and end apart: 46, of which 19 were waited for; matrix products, arithmetic and copies ran while one was open for 0% of the time, Pallas kernels for 18%

profile of v3, /device:TPU:0, one launch (start us, length us, event | category | flops | bytes accessed | tf_op | source)
XLA Modules:
  0.0 145.9 jit_solution(14319643160070065633)
XLA Ops:
  0.7 3.7 %front.1 = (bf16[256,768]{1,0:T(8,128)(2,1)S(1)}, bf16[256,768]{1,0:T(8,128)(2,1)S(1)}, bf16[3072,768]{1,0:T(8,128)(2,1)S(1)}, bf16[256,256]{1,0:T(8,128)(2,1)S(...) custom-call(s32[4,4]{1,0:T(4,128)S(1)} %copy-done.3, ...), custom_call_target="tpu_custom_call" | custom-call | tf_op jit(solution)/shard_map/front/pallas_call | solution.py:43
  4.9 2.6 %collective-permute-start.4 = (bf16[256,768]{1,0:T(8,128)(2,1)S(1)}, bf16[256,768]{1,0:T(8,128)(2,1)S(1)}, u32[]{:S(2)}, u32[]{:S(2)}) collective-permute-start(bf16[256,768]{1,0:T(8,128)(2,1)S(1)} %get-tuple-element.105), channel_id=1, source_target_pairs={{0,8},{8,0},{16,24},{24,16},{1,9},{9,1},{17,25},{25,17},{2,10},{10... | collective-permute-start | bytes 1179656 | tf_op jit(solution)/shard_map/ppermute | solution.py:412
  7.6 2.9 %collective-permute-start.2 = (bf16[64,896]{1,0:T(8,128)(2,1)S(1)}, bf16[64,896]{1,0:T(8,128)(2,1)S(1)}, u32[]{:S(2)}, u32[]{:S(2)}) collective-permute-start(bf16[64,896]{1,0:T(8,128)(2,1)S(1)} %get-tuple-element.103), channel_id=1, source_target_pairs={{0,16},{8,24},{16,0},{24,8},{1,17},{9,25},{17,1},{25,9},{2,18},{10... | collective-permute-start | bytes 344072 | tf_op jit(solution)/shard_map/ppermute | solution.py:401
  10.6 1.3 collective-permute-start.3
  11.9 10.2 %collective-permute-done.1.refs_2_.refs_3_ = bf16[64,896]{1,0:T(8,128)(2,1)S(1)} collective-permute-done((bf16[64,896]{1,0:T(8,128)(2,1)S(1)}, bf16[64,896]{1,0:T(8,128)(2,1)S(1)}, u32[]{:S(2)}, u32[]{:S(2)}) %collective-permute-start.1) | collective-permute-done | bytes 114720 | tf_op jit(solution)/shard_map/ppermute | solution.py:401
  22.2 1.7 %collective-permute-start.9 = (bf16[256,768]{1,0:T(8,128)(2,1)S(1)}, bf16[256,768]{1,0:T(8,128)(2,1)S(1)}, u32[]{:S(2)}, u32[]{:S(2)}) collective-permute-start(bf16[256,768]{1,0:T(8,128)(2,1)S(1)} %get-tuple-element.118), channel_id=1, source_target_pairs={{0,8},{24,16},{1,9},{25,17},{2,10},{26,18},{3,11},{27,19},{4,12},{... | collective-permute-start | bytes 1179656 | tf_op jit(solution)/shard_map/ppermute | solution.py:412
  23.8 3.0 %collective-permute-done.3.refs_4_.refs_5_ = bf16[64,896]{1,0:T(8,128)(2,1)S(1)} collective-permute-done((bf16[64,896]{1,0:T(8,128)(2,1)S(1)}, bf16[64,896]{1,0:T(8,128)(2,1)S(1)}, u32[]{:S(2)}, u32[]{:S(2)}) %collective-permute-start.3) | collective-permute-done | bytes 114720 | tf_op jit(solution)/shard_map/ppermute | solution.py:401
  27.1 1.5 %collective-permute-start.5 = (bf16[288,768]{1,0:T(8,128)(2,1)S(1)}, bf16[288,768]{1,0:T(8,128)(2,1)S(1)}, u32[]{:S(2)}, u32[]{:S(2)}) collective-permute-start(bf16[288,768]{1,0:T(8,128)(2,1)S(1)} %get-tuple-element.106.refs_0_.msg_ref), channel_id=1, source_target_pairs={{0,2},{1,5},{2,0},{3,7},{4,6},{5,1},{6,4},{7,3},{8,10},{9,13},{10,... | collective-permute-start | bytes 1327112 | tf_op jit(solution)/shard_map/ppermute | solution.py:389
  29.5 3.9 %collective-permute-start.13 = (bf16[256,768]{1,0:T(8,128)(2,1)S(1)}, bf16[256,768]{1,0:T(8,128)(2,1)S(1)}, u32[]{:S(2)}, u32[]{:S(2)}) collective-permute-start(bf16[256,768]{1,0:T(8,128)(2,1)S(1)} %get-tuple-element.120), channel_id=1, source_target_pairs={{0,8},{24,16},{1,9},{25,17},{2,10},{26,18},{3,11},{27,19},{4,12},{... | collective-permute-start | bytes 1179656 | tf_op jit(solution)/shard_map/ppermute | solution.py:412
  35.9 1.6 %collective-permute-start.11 = (bf16[256,768]{1,0:T(8,128)(2,1)S(1)}, bf16[256,768]{1,0:T(8,128)(2,1)S(1)}, u32[]{:S(2)}, u32[]{:S(2)}) collective-permute-start(bf16[256,768]{1,0:T(8,128)(2,1)S(1)} %far0.1), channel_id=1, source_target_pairs={{8,24},{16,0},{9,25},{17,1},{10,26},{18,2},{11,27},{19,3},{12,28},... | collective-permute-start | bytes 1179656 | tf_op jit(solution)/shard_map/ppermute | solution.py:412
  37.5 4.3 %collective-permute-done.12.refs_0_.low_ref = bf16[256,768]{1,0:T(8,128)(2,1)S(1)} collective-permute-done((bf16[256,768]{1,0:T(8,128)(2,1)S(1)}, bf16[256,768]{1,0:T(8,128)(2,1)S(1)}, u32[]{:S(2)}, u32[]{:S(2)}) %collective-permute-start.12) | collective-permute-done | bytes 393248 | tf_op jit(solution)/shard_map/ppermute | solution.py:412
  41.7 1.5 %collective-permute-start.7 = (bf16[288,768]{1,0:T(8,128)(2,1)S(1)}, bf16[288,768]{1,0:T(8,128)(2,1)S(1)}, u32[]{:S(2)}, u32[]{:S(2)}) collective-permute-start(bf16[288,768]{1,0:T(8,128)(2,1)S(1)} %get-tuple-element.106.refs_0_.msg_ref), channel_id=1, source_target_pairs={{0,4},{1,3},{2,6},{3,1},{4,0},{5,7},{6,2},{7,5},{8,12},{9,11},{10,... | collective-permute-start | bytes 1327112 | tf_op jit(solution)/shard_map/ppermute | solution.py:389
  43.8 5.4 %collective-permute-done.13.refs_1_.high_ref = bf16[256,768]{1,0:T(8,128)(2,1)S(1)} collective-permute-done((bf16[256,768]{1,0:T(8,128)(2,1)S(1)}, bf16[256,768]{1,0:T(8,128)(2,1)S(1)}, u32[]{:S(2)}, u32[]{:S(2)}) %collective-permute-start.13) | collective-permute-done | bytes 393248 | tf_op jit(solution)/shard_map/ppermute | solution.py:412
  51.5 1.4 blocks.22
  52.9 1.9 %collective-permute-done.6.refs_0_ = bf16[288,768]{1,0:T(8,128)(2,1)S(1)} collective-permute-done((bf16[288,768]{1,0:T(8,128)(2,1)S(1)}, bf16[288,768]{1,0:T(8,128)(2,1)S(1)}, u32[]{:S(2)}, u32[]{:S(2)}) %collective-permute-start.6) | collective-permute-done | bytes 442400 | tf_op jit(solution)/shard_map/ppermute | solution.py:389
  56.5 1.3 collective-permute-start.15
  59.4 1.6 %collective-permute-start.16 = (f32[64,256]{1,0:T(8,128)S(1)}, f32[64,256]{1,0:T(8,128)S(1)}, u32[]{:S(2)}, u32[]{:S(2)}) collective-permute-start(f32[64,256]{1,0:T(8,128)S(1)} %first_inner.1), channel_id=1, source_target_pairs={{0,2},{1,3},{2,0},{3,1},{4,6},{5,7},{6,4},{7,5},{8,10},{9,11},{10,... | collective-permute-start | bytes 196616 | tf_op jit(solution)/shard_map/ppermute | solution.py:389
  60.9 3.0 %collective-permute-done.16 = f32[64,256]{1,0:T(8,128)S(1)} collective-permute-done((f32[64,256]{1,0:T(8,128)S(1)}, f32[64,256]{1,0:T(8,128)S(1)}, u32[]{:S(2)}, u32[]{:S(2)}) %collective-permute-start.16) | collective-permute-done | bytes 65568 | tf_op jit(solution)/shard_map/ppermute | solution.py:389
  64.0 1.6 %collective-permute-start.17 = (f32[64,256]{1,0:T(8,128)S(1)}, f32[64,256]{1,0:T(8,128)S(1)}, u32[]{:S(2)}, u32[]{:S(2)}) collective-permute-start(f32[64,256]{1,0:T(8,128)S(1)} %add.9), channel_id=1, source_target_pairs={{0,4},{1,5},{2,6},{3,7},{4,0},{5,1},{6,2},{7,3},{8,12},{9,13},{10,... | collective-permute-start | bytes 196616 | tf_op jit(solution)/shard_map/ppermute | solution.py:389
  65.5 2.7 %collective-permute-done.17 = f32[64,256]{1,0:T(8,128)S(1)} collective-permute-done((f32[64,256]{1,0:T(8,128)S(1)}, f32[64,256]{1,0:T(8,128)S(1)}, u32[]{:S(2)}, u32[]{:S(2)}) %collective-permute-start.17) | collective-permute-done | bytes 65568 | tf_op jit(solution)/shard_map/ppermute | solution.py:389
  68.4 6.0 %collective-permute-done.15.far_ref = bf16[256,768]{1,0:T(8,128)(2,1)S(1)} collective-permute-done((bf16[256,768]{1,0:T(8,128)(2,1)S(1)}, bf16[256,768]{1,0:T(8,128)(2,1)S(1)}, u32[]{:S(2)}, u32[]{:S(2)}) %collective-permute-start.15) | collective-permute-done | bytes 393248 | tf_op jit(solution)/shard_map/ppermute | solution.py:412
  74.4 1.0 gather1.1.upc_ref
  76.4 1.6 %collective-permute-start.32 = (bf16[144,768]{1,0:T(8,128)(2,1)S(1)}, bf16[144,768]{1,0:T(8,128)(2,1)S(1)}, u32[]{:S(2)}, u32[]{:S(2)}) collective-permute-start(bf16[144,768]{1,0:T(8,128)(2,1)S(1)} %get-tuple-element.158.refs_0_), channel_id=1, source_target_pairs={{0,2},{1,5},{2,0},{3,7},{4,6},{5,1},{6,4},{7,3},{8,10},{9,13},{10,... | collective-permute-start | bytes 663560 | tf_op jit(solution)/shard_map/ppermute | solution.py:389
  79.4 1.5 %collective-permute-start.34 = (bf16[144,768]{1,0:T(8,128)(2,1)S(1)}, bf16[144,768]{1,0:T(8,128)(2,1)S(1)}, u32[]{:S(2)}, u32[]{:S(2)}) collective-permute-start(bf16[144,768]{1,0:T(8,128)(2,1)S(1)} %get-tuple-element.158.refs_0_), channel_id=1, source_target_pairs={{0,4},{1,3},{2,6},{3,1},{4,0},{5,7},{6,2},{7,5},{8,12},{9,11},{10,... | collective-permute-start | bytes 663560 | tf_op jit(solution)/shard_map/ppermute | solution.py:389
  80.9 2.4 %collective-permute-done.32.refs_0_ = bf16[144,768]{1,0:T(8,128)(2,1)S(1)} collective-permute-done((bf16[144,768]{1,0:T(8,128)(2,1)S(1)}, bf16[144,768]{1,0:T(8,128)(2,1)S(1)}, u32[]{:S(2)}, u32[]{:S(2)}) %collective-permute-start.32) | collective-permute-done | bytes 221216 | tf_op jit(solution)/shard_map/ppermute | solution.py:389
  83.3 1.5 %collective-permute-start.33 = (bf16[144,768]{1,0:T(8,128)(2,1)S(1)}, bf16[144,768]{1,0:T(8,128)(2,1)S(1)}, u32[]{:S(2)}, u32[]{:S(2)}) collective-permute-start(bf16[144,768]{1,0:T(8,128)(2,1)S(1)} %collective-permute-done.32.refs_0_), channel_id=1, source_target_pairs={{0,4},{1,3},{2,6},{3,1},{4,0},{5,7},{6,2},{7,5},{8,12},{9,11},{10,... | collective-permute-start | bytes 663560 | tf_op jit(solution)/shard_map/ppermute | solution.py:389
  85.4 2.7 %collective-permute-done.19.refs_0_ = bf16[144,768]{1,0:T(8,128)(2,1)S(1)} collective-permute-done((bf16[144,768]{1,0:T(8,128)(2,1)S(1)}, bf16[144,768]{1,0:T(8,128)(2,1)S(1)}, u32[]{:S(2)}, u32[]{:S(2)}) %collective-permute-start.19) | collective-permute-done | bytes 221216 | tf_op jit(solution)/shard_map/ppermute | solution.py:389
  88.1 1.5 %collective-permute-start.20 = (bf16[144,768]{1,0:T(8,128)(2,1)S(1)}, bf16[144,768]{1,0:T(8,128)(2,1)S(1)}, u32[]{:S(2)}, u32[]{:S(2)}) collective-permute-start(bf16[144,768]{1,0:T(8,128)(2,1)S(1)} %collective-permute-done.19.refs_0_), channel_id=1, source_target_pairs={{0,4},{1,3},{2,6},{3,1},{4,0},{5,7},{6,2},{7,5},{8,12},{9,11},{10,... | collective-permute-start | bytes 663560 | tf_op jit(solution)/shard_map/ppermute | solution.py:389
  92.9 1.1 collective-permute-done.20.refs_0_
  95.6 1.6 %collective-permute-start.36 = (bf16[144,768]{1,0:T(8,128)(2,1)S(1)}, bf16[144,768]{1,0:T(8,128)(2,1)S(1)}, u32[]{:S(2)}, u32[]{:S(2)}) collective-permute-start(bf16[144,768]{1,0:T(8,128)(2,1)S(1)} %get-tuple-element.169.refs_0_), channel_id=1, source_target_pairs={{0,2},{1,5},{2,0},{3,7},{4,6},{5,1},{6,4},{7,3},{8,10},{9,13},{10,... | collective-permute-start | bytes 663560 | tf_op jit(solution)/shard_map/ppermute | solution.py:389
  98.6 1.5 %collective-permute-start.38 = (bf16[144,768]{1,0:T(8,128)(2,1)S(1)}, bf16[144,768]{1,0:T(8,128)(2,1)S(1)}, u32[]{:S(2)}, u32[]{:S(2)}) collective-permute-start(bf16[144,768]{1,0:T(8,128)(2,1)S(1)} %get-tuple-element.169.refs_0_), channel_id=1, source_target_pairs={{0,4},{1,3},{2,6},{3,1},{4,0},{5,7},{6,2},{7,5},{8,12},{9,11},{10,... | collective-permute-start | bytes 663560 | tf_op jit(solution)/shard_map/ppermute | solution.py:389
  100.2 1.9 %collective-permute-done.36.refs_0_ = bf16[144,768]{1,0:T(8,128)(2,1)S(1)} collective-permute-done((bf16[144,768]{1,0:T(8,128)(2,1)S(1)}, bf16[144,768]{1,0:T(8,128)(2,1)S(1)}, u32[]{:S(2)}, u32[]{:S(2)}) %collective-permute-start.36) | collective-permute-done | bytes 221216 | tf_op jit(solution)/shard_map/ppermute | solution.py:389
  102.0 1.5 %collective-permute-start.37 = (bf16[144,768]{1,0:T(8,128)(2,1)S(1)}, bf16[144,768]{1,0:T(8,128)(2,1)S(1)}, u32[]{:S(2)}, u32[]{:S(2)}) collective-permute-start(bf16[144,768]{1,0:T(8,128)(2,1)S(1)} %collective-permute-done.36.refs_0_), channel_id=1, source_target_pairs={{0,4},{1,3},{2,6},{3,1},{4,0},{5,7},{6,2},{7,5},{8,12},{9,11},{10,... | collective-permute-start | bytes 663560 | tf_op jit(solution)/shard_map/ppermute | solution.py:389
  104.1 2.7 %collective-permute-done.23.refs_0_ = bf16[144,768]{1,0:T(8,128)(2,1)S(1)} collective-permute-done((bf16[144,768]{1,0:T(8,128)(2,1)S(1)}, bf16[144,768]{1,0:T(8,128)(2,1)S(1)}, u32[]{:S(2)}, u32[]{:S(2)}) %collective-permute-start.23) | collective-permute-done | bytes 221216 | tf_op jit(solution)/shard_map/ppermute | solution.py:389
  106.8 1.5 %collective-permute-start.24 = (bf16[144,768]{1,0:T(8,128)(2,1)S(1)}, bf16[144,768]{1,0:T(8,128)(2,1)S(1)}, u32[]{:S(2)}, u32[]{:S(2)}) collective-permute-start(bf16[144,768]{1,0:T(8,128)(2,1)S(1)} %collective-permute-done.23.refs_0_), channel_id=1, source_target_pairs={{0,4},{1,3},{2,6},{3,1},{4,0},{5,7},{6,2},{7,5},{8,12},{9,11},{10,... | collective-permute-start | bytes 663560 | tf_op jit(solution)/shard_map/ppermute | solution.py:389
  111.6 1.3 collective-permute-done.24.refs_0_
  113.8 0.9 finish.14
  114.7 1.5 %collective-permute-start.40 = (bf16[144,768]{1,0:T(8,128)(2,1)S(1)}, bf16[144,768]{1,0:T(8,128)(2,1)S(1)}, u32[]{:S(2)}, u32[]{:S(2)}) collective-permute-start(bf16[144,768]{1,0:T(8,128)(2,1)S(1)} %get-tuple-element.180.refs_0_), channel_id=1, source_target_pairs={{0,2},{1,5},{2,0},{3,7},{4,6},{5,1},{6,4},{7,3},{8,10},{9,13},{10,... | collective-permute-start | bytes 663560 | tf_op jit(solution)/shard_map/ppermute | solution.py:389
  117.8 1.5 %collective-permute-start.42 = (bf16[144,768]{1,0:T(8,128)(2,1)S(1)}, bf16[144,768]{1,0:T(8,128)(2,1)S(1)}, u32[]{:S(2)}, u32[]{:S(2)}) collective-permute-start(bf16[144,768]{1,0:T(8,128)(2,1)S(1)} %get-tuple-element.180.refs_0_), channel_id=1, source_target_pairs={{0,4},{1,3},{2,6},{3,1},{4,0},{5,7},{6,2},{7,5},{8,12},{9,11},{10,... | collective-permute-start | bytes 663560 | tf_op jit(solution)/shard_map/ppermute | solution.py:389
  119.3 2.0 %collective-permute-done.40.refs_0_ = bf16[144,768]{1,0:T(8,128)(2,1)S(1)} collective-permute-done((bf16[144,768]{1,0:T(8,128)(2,1)S(1)}, bf16[144,768]{1,0:T(8,128)(2,1)S(1)}, u32[]{:S(2)}, u32[]{:S(2)}) %collective-permute-start.40) | collective-permute-done | bytes 221216 | tf_op jit(solution)/shard_map/ppermute | solution.py:389
  121.3 1.7 %collective-permute-start.41 = (bf16[144,768]{1,0:T(8,128)(2,1)S(1)}, bf16[144,768]{1,0:T(8,128)(2,1)S(1)}, u32[]{:S(2)}, u32[]{:S(2)}) collective-permute-start(bf16[144,768]{1,0:T(8,128)(2,1)S(1)} %collective-permute-done.40.refs_0_), channel_id=1, source_target_pairs={{0,4},{1,3},{2,6},{3,1},{4,0},{5,7},{6,2},{7,5},{8,12},{9,11},{10,... | collective-permute-start | bytes 663560 | tf_op jit(solution)/shard_map/ppermute | solution.py:389
  123.3 2.7 %collective-permute-done.27.refs_0_ = bf16[144,768]{1,0:T(8,128)(2,1)S(1)} collective-permute-done((bf16[144,768]{1,0:T(8,128)(2,1)S(1)}, bf16[144,768]{1,0:T(8,128)(2,1)S(1)}, u32[]{:S(2)}, u32[]{:S(2)}) %collective-permute-start.27) | collective-permute-done | bytes 221216 | tf_op jit(solution)/shard_map/ppermute | solution.py:389
  126.0 1.7 %collective-permute-start.28 = (bf16[144,768]{1,0:T(8,128)(2,1)S(1)}, bf16[144,768]{1,0:T(8,128)(2,1)S(1)}, u32[]{:S(2)}, u32[]{:S(2)}) collective-permute-start(bf16[144,768]{1,0:T(8,128)(2,1)S(1)} %collective-permute-done.27.refs_0_), channel_id=1, source_target_pairs={{0,4},{1,3},{2,6},{3,1},{4,0},{5,7},{6,2},{7,5},{8,12},{9,11},{10,... | collective-permute-start | bytes 663560 | tf_op jit(solution)/shard_map/ppermute | solution.py:389
  133.4 1.1 collective-permute-start.44
  134.5 2.3 %collective-permute-start.45 = (bf16[64,768]{1,0:T(8,128)(2,1)S(1)}, bf16[64,768]{1,0:T(8,128)(2,1)S(1)}, u32[]{:S(2)}, u32[]{:S(2)}) collective-permute-start(bf16[64,768]{1,0:T(8,128)(2,1)S(1)} %get-tuple-element.192), channel_id=1, source_target_pairs={{0,24},{8,16},{16,8},{24,0},{1,25},{9,17},{17,9},{25,1},{2,26},{10... | collective-permute-start | bytes 294920 | tf_op jit(solution)/shard_map/ppermute | solution.py:401
  137.4 6.5 %collective-permute-done.44.refs_2_ = bf16[64,768]{1,0:T(8,128)(2,1)S(1)} collective-permute-done((bf16[64,768]{1,0:T(8,128)(2,1)S(1)}, bf16[64,768]{1,0:T(8,128)(2,1)S(1)}, u32[]{:S(2)}, u32[]{:S(2)}) %collective-permute-start.44) | collective-permute-done | bytes 98336 | tf_op jit(solution)/shard_map/ppermute | solution.py:401
  143.9 1.0 collective-permute-done.31.refs_1_
  144.8 1.1 unsort.1
  (104 shorter events, 32.8 us)
Async XLA Ops:
  0.7 26.1 %copy-start.2 = (f32[6144]{0:T(1024)S(1)}, f32[6144]{0:T(1024)}, u32[]{:S(2)}) copy-start(f32[6144]{0:T(1024)} %param.9) | copy-start | bytes 73732
  4.4 22.5 %collective-permute-start = (bf16[3072,768]{1,0:T(8,128)(2,1)S(1)}, bf16[3072,768]{1,0:T(8,128)(2,1)S(1)}, u32[]{:S(2)}, u32[]{:S(2)}) collective-permute-start(bf16[3072,768]{1,0:T(8,128)(2,1)S(1)} %get-tuple-element.100), channel_id=1, source_target_pairs={{0,1},{1,0},{2,3},{3,2},{4,5},{5,4},{6,7},{7,6},{8,9},{9,8},{10,11... | collective-permute-start | bytes 14155784 | tf_op jit(solution)/shard_map/ppermute | solution.py:389
  4.9 21.9 %collective-permute-start.4 = (bf16[256,768]{1,0:T(8,128)(2,1)S(1)}, bf16[256,768]{1,0:T(8,128)(2,1)S(1)}, u32[]{:S(2)}, u32[]{:S(2)}) collective-permute-start(bf16[256,768]{1,0:T(8,128)(2,1)S(1)} %get-tuple-element.105), channel_id=1, source_target_pairs={{0,8},{8,0},{16,24},{24,16},{1,9},{9,1},{17,25},{25,17},{2,10},{10... | collective-permute-start | bytes 1179656 | tf_op jit(solution)/shard_map/ppermute | solution.py:412
  7.5 14.6 %collective-permute-start.1 = (bf16[64,896]{1,0:T(8,128)(2,1)S(1)}, bf16[64,896]{1,0:T(8,128)(2,1)S(1)}, u32[]{:S(2)}, u32[]{:S(2)}) collective-permute-start(bf16[64,896]{1,0:T(8,128)(2,1)S(1)} %get-tuple-element.102), channel_id=1, source_target_pairs={{0,8},{8,0},{16,24},{24,16},{1,9},{9,1},{17,25},{25,17},{2,10},{10... | collective-permute-start | bytes 344072 | tf_op jit(solution)/shard_map/ppermute | solution.py:401
  7.6 16.2 %collective-permute-start.2 = (bf16[64,896]{1,0:T(8,128)(2,1)S(1)}, bf16[64,896]{1,0:T(8,128)(2,1)S(1)}, u32[]{:S(2)}, u32[]{:S(2)}) collective-permute-start(bf16[64,896]{1,0:T(8,128)(2,1)S(1)} %get-tuple-element.103), channel_id=1, source_target_pairs={{0,16},{8,24},{16,0},{24,8},{1,17},{9,25},{17,1},{25,9},{2,18},{10... | collective-permute-start | bytes 344072 | tf_op jit(solution)/shard_map/ppermute | solution.py:401
  10.6 16.2 %collective-permute-start.3 = (bf16[64,896]{1,0:T(8,128)(2,1)S(1)}, bf16[64,896]{1,0:T(8,128)(2,1)S(1)}, u32[]{:S(2)}, u32[]{:S(2)}) collective-permute-start(bf16[64,896]{1,0:T(8,128)(2,1)S(1)} %get-tuple-element.104), channel_id=1, source_target_pairs={{0,24},{8,16},{16,8},{24,0},{1,25},{9,17},{17,9},{25,1},{2,26},{10... | collective-permute-start | bytes 344072 | tf_op jit(solution)/shard_map/ppermute | solution.py:401
  22.2 11.3 %collective-permute-start.9 = (bf16[256,768]{1,0:T(8,128)(2,1)S(1)}, bf16[256,768]{1,0:T(8,128)(2,1)S(1)}, u32[]{:S(2)}, u32[]{:S(2)}) collective-permute-start(bf16[256,768]{1,0:T(8,128)(2,1)S(1)} %get-tuple-element.118), channel_id=1, source_target_pairs={{0,8},{24,16},{1,9},{25,17},{2,10},{26,18},{3,11},{27,19},{4,12},{... | collective-permute-start | bytes 1179656 | tf_op jit(solution)/shard_map/ppermute | solution.py:412
  27.1 16.2 %collective-permute-start.5 = (bf16[288,768]{1,0:T(8,128)(2,1)S(1)}, bf16[288,768]{1,0:T(8,128)(2,1)S(1)}, u32[]{:S(2)}, u32[]{:S(2)}) collective-permute-start(bf16[288,768]{1,0:T(8,128)(2,1)S(1)} %get-tuple-element.106.refs_0_.msg_ref), channel_id=1, source_target_pairs={{0,2},{1,5},{2,0},{3,7},{4,6},{5,1},{6,4},{7,3},{8,10},{9,13},{10,... | collective-permute-start | bytes 1327112 | tf_op jit(solution)/shard_map/ppermute | solution.py:389
  29.5 12.3 %collective-permute-start.12 = (bf16[256,768]{1,0:T(8,128)(2,1)S(1)}, bf16[256,768]{1,0:T(8,128)(2,1)S(1)}, u32[]{:S(2)}, u32[]{:S(2)}) collective-permute-start(bf16[256,768]{1,0:T(8,128)(2,1)S(1)} %get-tuple-element.119), channel_id=1, source_target_pairs={{0,8},{8,0},{16,24},{24,16},{1,9},{9,1},{17,25},{25,17},{2,10},{10... | collective-permute-start | bytes 1179656 | tf_op jit(solution)/shard_map/ppermute | solution.py:412
  29.5 19.6 %collective-permute-start.13 = (bf16[256,768]{1,0:T(8,128)(2,1)S(1)}, bf16[256,768]{1,0:T(8,128)(2,1)S(1)}, u32[]{:S(2)}, u32[]{:S(2)}) collective-permute-start(bf16[256,768]{1,0:T(8,128)(2,1)S(1)} %get-tuple-element.120), channel_id=1, source_target_pairs={{0,8},{24,16},{1,9},{25,17},{2,10},{26,18},{3,11},{27,19},{4,12},{... | collective-permute-start | bytes 1179656 | tf_op jit(solution)/shard_map/ppermute | solution.py:412
  33.5 17.2 %slice-start = ((s8[9437184]{0:T(1024)(128)(4,1)}), s8[4194304]{0:T(1024)(128)(4,1)S(1)}, s32[]{:S(2)}) async-start(s8[9437184]{0:T(1024)(128)(4,1)} %bitcast.5), calls=%async_computation | async-start | bytes 8388608
  34.3 23.5 %collective-permute-start.10 = (bf16[256,768]{1,0:T(8,128)(2,1)S(1)}, bf16[256,768]{1,0:T(8,128)(2,1)S(1)}, u32[]{:S(2)}, u32[]{:S(2)}) collective-permute-start(bf16[256,768]{1,0:T(8,128)(2,1)S(1)} %near0.1), channel_id=1, source_target_pairs={{8,16},{16,8},{9,17},{17,9},{10,18},{18,10},{11,19},{19,11},{12,20... | collective-permute-start | bytes 1179656 | tf_op jit(solution)/shard_map/ppermute | solution.py:412
  35.9 21.8 %collective-permute-start.11 = (bf16[256,768]{1,0:T(8,128)(2,1)S(1)}, bf16[256,768]{1,0:T(8,128)(2,1)S(1)}, u32[]{:S(2)}, u32[]{:S(2)}) collective-permute-start(bf16[256,768]{1,0:T(8,128)(2,1)S(1)} %far0.1), channel_id=1, source_target_pairs={{8,24},{16,0},{9,25},{17,1},{10,26},{18,2},{11,27},{19,3},{12,28},... | collective-permute-start | bytes 1179656 | tf_op jit(solution)/shard_map/ppermute | solution.py:412
  41.7 9.7 %collective-permute-start.7 = (bf16[288,768]{1,0:T(8,128)(2,1)S(1)}, bf16[288,768]{1,0:T(8,128)(2,1)S(1)}, u32[]{:S(2)}, u32[]{:S(2)}) collective-permute-start(bf16[288,768]{1,0:T(8,128)(2,1)S(1)} %get-tuple-element.106.refs_0_.msg_ref), channel_id=1, source_target_pairs={{0,4},{1,3},{2,6},{3,1},{4,0},{5,7},{6,2},{7,5},{8,12},{9,11},{10,... | collective-permute-start | bytes 1327112 | tf_op jit(solution)/shard_map/ppermute | solution.py:389
  43.3 11.5 %collective-permute-start.6 = (bf16[288,768]{1,0:T(8,128)(2,1)S(1)}, bf16[288,768]{1,0:T(8,128)(2,1)S(1)}, u32[]{:S(2)}, u32[]{:S(2)}) collective-permute-start(bf16[288,768]{1,0:T(8,128)(2,1)S(1)} %collective-permute-done.5.refs_0_), channel_id=1, source_target_pairs={{0,4},{1,3},{2,6},{3,1},{4,0},{5,7},{6,2},{7,5},{8,12},{9,11},{10,... | collective-permute-start | bytes 1327112 | tf_op jit(solution)/shard_map/ppermute | solution.py:389
  50.0 18.4 %collective-permute-start.14 = (bf16[256,768]{1,0:T(8,128)(2,1)S(1)}, bf16[256,768]{1,0:T(8,128)(2,1)S(1)}, u32[]{:S(2)}, u32[]{:S(2)}) collective-permute-start(bf16[256,768]{1,0:T(8,128)(2,1)S(1)} %near1.1), channel_id=1, source_target_pairs={{8,16},{16,8},{9,17},{17,9},{10,18},{18,10},{11,19},{19,11},{12,20... | collective-permute-start | bytes 1179656 | tf_op jit(solution)/shard_map/ppermute | solution.py:412
  55.6 19.9 %collective-permute-start.8 = (bf16[288,768]{1,0:T(8,128)(2,1)S(1)}, bf16[288,768]{1,0:T(8,128)(2,1)S(1)}, u32[]{:S(2)}, u32[]{:S(2)}) collective-permute-start(bf16[288,768]{1,0:T(8,128)(2,1)S(1)} %get-tuple-element.115), channel_id=1, source_target_pairs={{0,1},{1,0},{2,3},{3,2},{4,5},{5,4},{6,7},{7,6},{8,9},{9,8},{10,11... | collective-permute-start | bytes 1327112 | tf_op jit(solution)/shard_map/ppermute | solution.py:389
  56.5 18.0 %collective-permute-start.15 = (bf16[256,768]{1,0:T(8,128)(2,1)S(1)}, bf16[256,768]{1,0:T(8,128)(2,1)S(1)}, u32[]{:S(2)}, u32[]{:S(2)}) collective-permute-start(bf16[256,768]{1,0:T(8,128)(2,1)S(1)} %far1.1), channel_id=1, source_target_pairs={{8,24},{16,0},{9,25},{17,1},{10,26},{18,2},{11,27},{19,3},{12,28},... | collective-permute-start | bytes 1179656 | tf_op jit(solution)/shard_map/ppermute | solution.py:412
  59.4 4.6 %collective-permute-start.16 = (f32[64,256]{1,0:T(8,128)S(1)}, f32[64,256]{1,0:T(8,128)S(1)}, u32[]{:S(2)}, u32[]{:S(2)}) collective-permute-start(f32[64,256]{1,0:T(8,128)S(1)} %first_inner.1), channel_id=1, source_target_pairs={{0,2},{1,3},{2,0},{3,1},{4,6},{5,7},{6,4},{7,5},{8,10},{9,11},{10,... | collective-permute-start | bytes 196616 | tf_op jit(solution)/shard_map/ppermute | solution.py:389
  64.0 4.3 %collective-permute-start.17 = (f32[64,256]{1,0:T(8,128)S(1)}, f32[64,256]{1,0:T(8,128)S(1)}, u32[]{:S(2)}, u32[]{:S(2)}) collective-permute-start(f32[64,256]{1,0:T(8,128)S(1)} %add.9), channel_id=1, source_target_pairs={{0,4},{1,5},{2,6},{3,7},{4,0},{5,1},{6,2},{7,3},{8,12},{9,13},{10,... | collective-permute-start | bytes 196616 | tf_op jit(solution)/shard_map/ppermute | solution.py:389
  68.3 7.1 %collective-permute-start.18 = (f32[64,256]{1,0:T(8,128)S(1)}, f32[64,256]{1,0:T(8,128)S(1)}, u32[]{:S(2)}, u32[]{:S(2)}) collective-permute-start(f32[64,256]{1,0:T(8,128)S(1)} %add.10), channel_id=1, source_target_pairs={{0,1},{1,0},{2,3},{3,2},{4,5},{5,4},{6,7},{7,6},{8,9},{9,8},{10,11... | collective-permute-start | bytes 196616 | tf_op jit(solution)/shard_map/ppermute | solution.py:389
  76.4 7.0 %collective-permute-start.32 = (bf16[144,768]{1,0:T(8,128)(2,1)S(1)}, bf16[144,768]{1,0:T(8,128)(2,1)S(1)}, u32[]{:S(2)}, u32[]{:S(2)}) collective-permute-start(bf16[144,768]{1,0:T(8,128)(2,1)S(1)} %get-tuple-element.158.refs_0_), channel_id=1, source_target_pairs={{0,2},{1,5},{2,0},{3,7},{4,6},{5,1},{6,4},{7,3},{8,10},{9,13},{10,... | collective-permute-start | bytes 663560 | tf_op jit(solution)/shard_map/ppermute | solution.py:389
  78.8 9.3 %collective-permute-start.19 = (bf16[144,768]{1,0:T(8,128)(2,1)S(1)}, bf16[144,768]{1,0:T(8,128)(2,1)S(1)}, u32[]{:S(2)}, u32[]{:S(2)}) collective-permute-start(bf16[144,768]{1,0:T(8,128)(2,1)S(1)} %get-tuple-element.122.refs_0_), channel_id=1, source_target_pairs={{0,2},{1,5},{2,0},{3,7},{4,6},{5,1},{6,4},{7,3},{8,10},{9,13},{10,... | collective-permute-start | bytes 663560 | tf_op jit(solution)/shard_map/ppermute | solution.py:389
  79.4 11.2 %collective-permute-start.34 = (bf16[144,768]{1,0:T(8,128)(2,1)S(1)}, bf16[144,768]{1,0:T(8,128)(2,1)S(1)}, u32[]{:S(2)}, u32[]{:S(2)}) collective-permute-start(bf16[144,768]{1,0:T(8,128)(2,1)S(1)} %get-tuple-element.158.refs_0_), channel_id=1, source_target_pairs={{0,4},{1,3},{2,6},{3,1},{4,0},{5,7},{6,2},{7,5},{8,12},{9,11},{10,... | collective-permute-start | bytes 663560 | tf_op jit(solution)/shard_map/ppermute | solution.py:389
  83.3 8.1 %collective-permute-start.33 = (bf16[144,768]{1,0:T(8,128)(2,1)S(1)}, bf16[144,768]{1,0:T(8,128)(2,1)S(1)}, u32[]{:S(2)}, u32[]{:S(2)}) collective-permute-start(bf16[144,768]{1,0:T(8,128)(2,1)S(1)} %collective-permute-done.32.refs_0_), channel_id=1, source_target_pairs={{0,4},{1,3},{2,6},{3,1},{4,0},{5,7},{6,2},{7,5},{8,12},{9,11},{10,... | collective-permute-start | bytes 663560 | tf_op jit(solution)/shard_map/ppermute | solution.py:389
  84.8 7.2 %collective-permute-start.21 = (bf16[144,768]{1,0:T(8,128)(2,1)S(1)}, bf16[144,768]{1,0:T(8,128)(2,1)S(1)}, u32[]{:S(2)}, u32[]{:S(2)}) collective-permute-start(bf16[144,768]{1,0:T(8,128)(2,1)S(1)} %get-tuple-element.122.refs_0_), channel_id=1, source_target_pairs={{0,4},{1,3},{2,6},{3,1},{4,0},{5,7},{6,2},{7,5},{8,12},{9,11},{10,... | collective-permute-start | bytes 663560 | tf_op jit(solution)/shard_map/ppermute | solution.py:389
  88.1 5.9 %collective-permute-start.20 = (bf16[144,768]{1,0:T(8,128)(2,1)S(1)}, bf16[144,768]{1,0:T(8,128)(2,1)S(1)}, u32[]{:S(2)}, u32[]{:S(2)}) collective-permute-start(bf16[144,768]{1,0:T(8,128)(2,1)S(1)} %collective-permute-done.19.refs_0_), channel_id=1, source_target_pairs={{0,4},{1,3},{2,6},{3,1},{4,0},{5,7},{6,2},{7,5},{8,12},{9,11},{10,... | collective-permute-start | bytes 663560 | tf_op jit(solution)/shard_map/ppermute | solution.py:389
  92.0 2.7 %collective-permute-start.35 = (bf16[144,768]{1,0:T(8,128)(2,1)S(1)}, bf16[144,768]{1,0:T(8,128)(2,1)S(1)}, u32[]{:S(2)}, u32[]{:S(2)}) collective-permute-start(bf16[144,768]{1,0:T(8,128)(2,1)S(1)} %get-tuple-element.167), channel_id=1, source_target_pairs={{0,1},{1,0},{2,3},{3,2},{4,5},{5,4},{6,7},{7,6},{8,9},{9,8},{10,11... | collective-permute-start | bytes 663560 | tf_op jit(solution)/shard_map/ppermute | solution.py:389
  94.5 2.6 %collective-permute-start.22 = (bf16[144,768]{1,0:T(8,128)(2,1)S(1)}, bf16[144,768]{1,0:T(8,128)(2,1)S(1)}, u32[]{:S(2)}, u32[]{:S(2)}) collective-permute-start(bf16[144,768]{1,0:T(8,128)(2,1)S(1)} %get-tuple-element.131), channel_id=1, source_target_pairs={{0,1},{1,0},{2,3},{3,2},{4,5},{5,4},{6,7},{7,6},{8,9},{9,8},{10,11... | collective-permute-start | bytes 663560 | tf_op jit(solution)/shard_map/ppermute | solution.py:389
  95.6 6.5 %collective-permute-start.36 = (bf16[144,768]{1,0:T(8,128)(2,1)S(1)}, bf16[144,768]{1,0:T(8,128)(2,1)S(1)}, u32[]{:S(2)}, u32[]{:S(2)}) collective-permute-start(bf16[144,768]{1,0:T(8,128)(2,1)S(1)} %get-tuple-element.169.refs_0_), channel_id=1, source_target_pairs={{0,2},{1,5},{2,0},{3,7},{4,6},{5,1},{6,4},{7,3},{8,10},{9,13},{10,... | collective-permute-start | bytes 663560 | tf_op jit(solution)/shard_map/ppermute | solution.py:389
  98.0 8.8 %collective-permute-start.23 = (bf16[144,768]{1,0:T(8,128)(2,1)S(1)}, bf16[144,768]{1,0:T(8,128)(2,1)S(1)}, u32[]{:S(2)}, u32[]{:S(2)}) collective-permute-start(bf16[144,768]{1,0:T(8,128)(2,1)S(1)} %get-tuple-element.133.refs_0_), channel_id=1, source_target_pairs={{0,2},{1,5},{2,0},{3,7},{4,6},{5,1},{6,4},{7,3},{8,10},{9,13},{10,... | collective-permute-start | bytes 663560 | tf_op jit(solution)/shard_map/ppermute | solution.py:389
  98.6 10.7 %collective-permute-start.38 = (bf16[144,768]{1,0:T(8,128)(2,1)S(1)}, bf16[144,768]{1,0:T(8,128)(2,1)S(1)}, u32[]{:S(2)}, u32[]{:S(2)}) collective-permute-start(bf16[144,768]{1,0:T(8,128)(2,1)S(1)} %get-tuple-element.169.refs_0_), channel_id=1, source_target_pairs={{0,4},{1,3},{2,6},{3,1},{4,0},{5,7},{6,2},{7,5},{8,12},{9,11},{10,... | collective-permute-start | bytes 663560 | tf_op jit(solution)/shard_map/ppermute | solution.py:389
  102.0 8.1 %collective-permute-start.37 = (bf16[144,768]{1,0:T(8,128)(2,1)S(1)}, bf16[144,768]{1,0:T(8,128)(2,1)S(1)}, u32[]{:S(2)}, u32[]{:S(2)}) collective-permute-start(bf16[144,768]{1,0:T(8,128)(2,1)S(1)} %collective-permute-done.36.refs_0_), channel_id=1, source_target_pairs={{0,4},{1,3},{2,6},{3,1},{4,0},{5,7},{6,2},{7,5},{8,12},{9,11},{10,... | collective-permute-start | bytes 663560 | tf_op jit(solution)/shard_map/ppermute | solution.py:389
  103.6 7.2 %collective-permute-start.25 = (bf16[144,768]{1,0:T(8,128)(2,1)S(1)}, bf16[144,768]{1,0:T(8,128)(2,1)S(1)}, u32[]{:S(2)}, u32[]{:S(2)}) collective-permute-start(bf16[144,768]{1,0:T(8,128)(2,1)S(1)} %get-tuple-element.133.refs_0_), channel_id=1, source_target_pairs={{0,4},{1,3},{2,6},{3,1},{4,0},{5,7},{6,2},{7,5},{8,12},{9,11},{10,... | collective-permute-start | bytes 663560 | tf_op jit(solution)/shard_map/ppermute | solution.py:389
  106.8 6.1 %collective-permute-start.24 = (bf16[144,768]{1,0:T(8,128)(2,1)S(1)}, bf16[144,768]{1,0:T(8,128)(2,1)S(1)}, u32[]{:S(2)}, u32[]{:S(2)}) collective-permute-start(bf16[144,768]{1,0:T(8,128)(2,1)S(1)} %collective-permute-done.23.refs_0_), channel_id=1, source_target_pairs={{0,4},{1,3},{2,6},{3,1},{4,0},{5,7},{6,2},{7,5},{8,12},{9,11},{10,... | collective-permute-start | bytes 663560 | tf_op jit(solution)/shard_map/ppermute | solution.py:389
  110.7 3.1 %collective-permute-start.39 = (bf16[144,768]{1,0:T(8,128)(2,1)S(1)}, bf16[144,768]{1,0:T(8,128)(2,1)S(1)}, u32[]{:S(2)}, u32[]{:S(2)}) collective-permute-start(bf16[144,768]{1,0:T(8,128)(2,1)S(1)} %get-tuple-element.178), channel_id=1, source_target_pairs={{0,1},{1,0},{2,3},{3,2},{4,5},{5,4},{6,7},{7,6},{8,9},{9,8},{10,11... | collective-permute-start | bytes 663560 | tf_op jit(solution)/shard_map/ppermute | solution.py:389
  113.4 2.9 %collective-permute-start.26 = (bf16[144,768]{1,0:T(8,128)(2,1)S(1)}, bf16[144,768]{1,0:T(8,128)(2,1)S(1)}, u32[]{:S(2)}, u32[]{:S(2)}) collective-permute-start(bf16[144,768]{1,0:T(8,128)(2,1)S(1)} %get-tuple-element.142), channel_id=1, source_target_pairs={{0,1},{1,0},{2,3},{3,2},{4,5},{5,4},{6,7},{7,6},{8,9},{9,8},{10,11... | collective-permute-start | bytes 663560 | tf_op jit(solution)/shard_map/ppermute | solution.py:389
  114.7 6.6 %collective-permute-start.40 = (bf16[144,768]{1,0:T(8,128)(2,1)S(1)}, bf16[144,768]{1,0:T(8,128)(2,1)S(1)}, u32[]{:S(2)}, u32[]{:S(2)}) collective-permute-start(bf16[144,768]{1,0:T(8,128)(2,1)S(1)} %get-tuple-element.180.refs_0_), channel_id=1, source_target_pairs={{0,2},{1,5},{2,0},{3,7},{4,6},{5,1},{6,4},{7,3},{8,10},{9,13},{10,... | collective-permute-start | bytes 663560 | tf_op jit(solution)/shard_map/ppermute | solution.py:389
  117.2 8.9 %collective-permute-start.27 = (bf16[144,768]{1,0:T(8,128)(2,1)S(1)}, bf16[144,768]{1,0:T(8,128)(2,1)S(1)}, u32[]{:S(2)}, u32[]{:S(2)}) collective-permute-start(bf16[144,768]{1,0:T(8,128)(2,1)S(1)} %get-tuple-element.144.refs_0_), channel_id=1, source_target_pairs={{0,2},{1,5},{2,0},{3,7},{4,6},{5,1},{6,4},{7,3},{8,10},{9,13},{10,... | collective-permute-start | bytes 663560 | tf_op jit(solution)/shard_map/ppermute | solution.py:389
  117.8 11.2 %collective-permute-start.42 = (bf16[144,768]{1,0:T(8,128)(2,1)S(1)}, bf16[144,768]{1,0:T(8,128)(2,1)S(1)}, u32[]{:S(2)}, u32[]{:S(2)}) collective-permute-start(bf16[144,768]{1,0:T(8,128)(2,1)S(1)} %get-tuple-element.180.refs_0_), channel_id=1, source_target_pairs={{0,4},{1,3},{2,6},{3,1},{4,0},{5,7},{6,2},{7,5},{8,12},{9,11},{10,... | collective-permute-start | bytes 663560 | tf_op jit(solution)/shard_map/ppermute | solution.py:389
  121.3 8.5 %collective-permute-start.41 = (bf16[144,768]{1,0:T(8,128)(2,1)S(1)}, bf16[144,768]{1,0:T(8,128)(2,1)S(1)}, u32[]{:S(2)}, u32[]{:S(2)}) collective-permute-start(bf16[144,768]{1,0:T(8,128)(2,1)S(1)} %collective-permute-done.40.refs_0_), channel_id=1, source_target_pairs={{0,4},{1,3},{2,6},{3,1},{4,0},{5,7},{6,2},{7,5},{8,12},{9,11},{10,... | collective-permute-start | bytes 663560 | tf_op jit(solution)/shard_map/ppermute | solution.py:389
  123.0 7.4 %collective-permute-start.29 = (bf16[144,768]{1,0:T(8,128)(2,1)S(1)}, bf16[144,768]{1,0:T(8,128)(2,1)S(1)}, u32[]{:S(2)}, u32[]{:S(2)}) collective-permute-start(bf16[144,768]{1,0:T(8,128)(2,1)S(1)} %get-tuple-element.144.refs_0_), channel_id=1, source_target_pairs={{0,4},{1,3},{2,6},{3,1},{4,0},{5,7},{6,2},{7,5},{8,12},{9,11},{10,... | collective-permute-start | bytes 663560 | tf_op jit(solution)/shard_map/ppermute | solution.py:389
  126.0 5.9 %collective-permute-start.28 = (bf16[144,768]{1,0:T(8,128)(2,1)S(1)}, bf16[144,768]{1,0:T(8,128)(2,1)S(1)}, u32[]{:S(2)}, u32[]{:S(2)}) collective-permute-start(bf16[144,768]{1,0:T(8,128)(2,1)S(1)} %collective-permute-done.27.refs_0_), channel_id=1, source_target_pairs={{0,4},{1,3},{2,6},{3,1},{4,0},{5,7},{6,2},{7,5},{8,12},{9,11},{10,... | collective-permute-start | bytes 663560 | tf_op jit(solution)/shard_map/ppermute | solution.py:389
  130.4 2.6 %collective-permute-start.43 = (bf16[144,768]{1,0:T(8,128)(2,1)S(1)}, bf16[144,768]{1,0:T(8,128)(2,1)S(1)}, u32[]{:S(2)}, u32[]{:S(2)}) collective-permute-start(bf16[144,768]{1,0:T(8,128)(2,1)S(1)} %get-tuple-element.189), channel_id=1, source_target_pairs={{0,1},{1,0},{2,3},{3,2},{4,5},{5,4},{6,7},{7,6},{8,9},{9,8},{10,11... | collective-permute-start | bytes 663560 | tf_op jit(solution)/shard_map/ppermute | solution.py:389
  132.5 4.3 %collective-permute-start.30 = (bf16[144,768]{1,0:T(8,128)(2,1)S(1)}, bf16[144,768]{1,0:T(8,128)(2,1)S(1)}, u32[]{:S(2)}, u32[]{:S(2)}) collective-permute-start(bf16[144,768]{1,0:T(8,128)(2,1)S(1)} %get-tuple-element.153), channel_id=1, source_target_pairs={{0,1},{1,0},{2,3},{3,2},{4,5},{5,4},{6,7},{7,6},{8,9},{9,8},{10,11... | collective-permute-start | bytes 663560 | tf_op jit(solution)/shard_map/ppermute | solution.py:389
  133.4 10.5 %collective-permute-start.44 = (bf16[64,768]{1,0:T(8,128)(2,1)S(1)}, bf16[64,768]{1,0:T(8,128)(2,1)S(1)}, u32[]{:S(2)}, u32[]{:S(2)}) collective-permute-start(bf16[64,768]{1,0:T(8,128)(2,1)S(1)} %get-tuple-element.191), channel_id=1, source_target_pairs={{0,16},{8,24},{16,0},{24,8},{1,17},{9,25},{17,1},{25,9},{2,18},{10... | collective-permute-start | bytes 294920 | tf_op jit(solution)/shard_map/ppermute | solution.py:401
  134.5 9.4 %collective-permute-start.45 = (bf16[64,768]{1,0:T(8,128)(2,1)S(1)}, bf16[64,768]{1,0:T(8,128)(2,1)S(1)}, u32[]{:S(2)}, u32[]{:S(2)}) collective-permute-start(bf16[64,768]{1,0:T(8,128)(2,1)S(1)} %get-tuple-element.192), channel_id=1, source_target_pairs={{0,24},{8,16},{16,8},{24,0},{1,25},{9,17},{17,9},{25,1},{2,26},{10... | collective-permute-start | bytes 294920 | tf_op jit(solution)/shard_map/ppermute | solution.py:401
  137.2 7.7 %collective-permute-start.31 = (bf16[64,768]{1,0:T(8,128)(2,1)S(1)}, bf16[64,768]{1,0:T(8,128)(2,1)S(1)}, u32[]{:S(2)}, u32[]{:S(2)}) collective-permute-start(bf16[64,768]{1,0:T(8,128)(2,1)S(1)} %get-tuple-element.156), channel_id=1, source_target_pairs={{0,8},{8,0},{16,24},{24,16},{1,9},{9,1},{17,25},{25,17},{2,10},{10... | collective-permute-start | bytes 294920 | tf_op jit(solution)/shard_map/ppermute | solution.py:401
  (6 other events, 38.6 us)

commit v4 on v3

--- a/solution.py
+++ b/solution.py
@@ -219,6 +219,10 @@
 def apart_kernel(weight_ref, sent_ref, sems):
     for copy in apart(weight_ref, sent_ref, sems):
         copy.wait()
+
+
+def tie(x, deps):
+    return lax.optimization_barrier((x, *deps))[0] if deps else x
 
 
 def two_parts(row):
@@ -436,12 +440,12 @@
     chunks = [c if k == 0 else store(c, k) for k, c in enumerate(chunks)]
     other = sibling(other)
     low1, high1 = pick(functools.partial(end_blocks_kernel, owned), [shape, shape], up, name="ends1", after=[low0, *chunks[1:]])
-    low1 = line(low1, pairs)
-    high1 = line(high1, ends)
     far0 = passing((3, 3, 0, 0), down, low0, name="far0")
     far0 = line(far0, across)
     pass0 = passing((2, 2, 1, 1), down, low0, high0, name="near0")
     pass0 = line(pass0, middle)
+    low1 = line(low1, pairs)
+    high1 = line(tie(high1, [far0]), ends)
     far1 = line(passing((3, 3, 0, 0), up, low1, name="far1"), across)
     pass1 = line(passing((2, 2, 1, 1), up, low1, high1, name="near1"), middle)
     down_copy = pick(functools.partial(gather_kernel, owned), shape, low0, high0, pass0, far0, name="gather0")

time: 146 us -> 140 us (0.959)
  waiting for transfers between devices: 61.6 us -> 50 us
  starting transfers between devices: 51.3 us -> 56.8 us
    ppermute x6, waiting for transfers between devices: 20.7 us -> 11.2 us  [store(): return lax.ppermute(x, 'store', [(g, g ^ k) for g in range(groups)])]
    ppermute x8, waiting for transfers between devices: 15.7 us -> 9.24 us  [line(): return lax.ppermute(x, 'store', pairs)]
    ppermute x8, starting transfers between devices: 12.7 us -> 17.6 us  [line(): return lax.ppermute(x, 'store', pairs)]
    ppermute x32, waiting for transfers between devices: 25.2 us -> 29.6 us  [mp(): return lax.ppermute(x, 'mp', [(i, pairs_of(i)) for i in range(parts)])]
  transfers between devices with their start and end apart: 46 -> 46, of which waited for: 19 -> 20; matrix products, arithmetic and copies ran while one was open for 0% -> 0% of each run, Pallas kernels for 18% -> 19%
where the time goes in v4:
time: 140 us
  starting transfers between devices  56.8 us (41%)
  waiting for transfers between devices  50 us (36%)
  Pallas kernels  31.8 us (23%)
    pallas_call x40, Pallas kernels, call(): pl.pallas_call(kernel, out_shape=shapes, in_specs=specs, out_specs=[IN_VM...  31.8 us
    ppermute x32, starting transfers between devices, mp(): return lax.ppermute(x, 'mp', [(i, pairs_of(i)) for i in range(parts)])  30.9 us
    ppermute x32, waiting for transfers between devices, mp(): return lax.ppermute(x, 'mp', [(i, pairs_of(i)) for i in range(parts)])  29.6 us
    ppermute x8, starting transfers between devices, line(): return lax.ppermute(x, 'store', pairs)  17.6 us
    ppermute x6, waiting for transfers between devices, store(): return lax.ppermute(x, 'store', [(g, g ^ k) for g in range(groups)])  11.2 us
    ppermute x8, waiting for transfers between devices, line(): return lax.ppermute(x, 'store', pairs)  9.24 us
    ppermute x6, starting transfers between devices, store(): return lax.ppermute(x, 'store', [(g, g ^ k) for g in range(groups)])  8.24 us
  transfers between devices with their start and end apart: 46, of which 20 were waited for; matrix products, arithmetic and copies ran while one was open for 0% of the time, Pallas kernels for 19%

profile of v4, /device:TPU:0, one launch (start us, length us, event | category | flops | bytes accessed | tf_op | source)
XLA Modules:
  0.0 139.9 jit_solution(3141747001849193158)
XLA Ops:
  0.7 3.7 %front.1 = (bf16[256,768]{1,0:T(8,128)(2,1)S(1)}, bf16[256,768]{1,0:T(8,128)(2,1)S(1)}, bf16[3072,768]{1,0:T(8,128)(2,1)S(1)}, bf16[256,256]{1,0:T(8,128)(2,1)S(...) custom-call(s32[4,4]{1,0:T(4,128)S(1)} %copy-done.3, ...), custom_call_target="tpu_custom_call" | custom-call | tf_op jit(solution)/shard_map/front/pallas_call | solution.py:43
  4.9 2.6 %collective-permute-start.4 = (bf16[256,768]{1,0:T(8,128)(2,1)S(1)}, bf16[256,768]{1,0:T(8,128)(2,1)S(1)}, u32[]{:S(2)}, u32[]{:S(2)}) collective-permute-start(bf16[256,768]{1,0:T(8,128)(2,1)S(1)} %get-tuple-element.106), channel_id=1, source_target_pairs={{0,8},{8,0},{16,24},{24,16},{1,9},{9,1},{17,25},{25,17},{2,10},{10... | collective-permute-start | bytes 1179656 | tf_op jit(solution)/shard_map/ppermute | solution.py:416
  7.7 2.9 %collective-permute-start.2 = (bf16[64,896]{1,0:T(8,128)(2,1)S(1)}, bf16[64,896]{1,0:T(8,128)(2,1)S(1)}, u32[]{:S(2)}, u32[]{:S(2)}) collective-permute-start(bf16[64,896]{1,0:T(8,128)(2,1)S(1)} %get-tuple-element.104), channel_id=1, source_target_pairs={{0,16},{8,24},{16,0},{24,8},{1,17},{9,25},{17,1},{25,9},{2,18},{10... | collective-permute-start | bytes 344072 | tf_op jit(solution)/shard_map/ppermute | solution.py:405
  10.6 1.3 collective-permute-start.3
  12.0 8.0 %collective-permute-done.4.refs_5_.refs_0_.low_ref.refs_2_ = bf16[256,768]{1,0:T(8,128)(2,1)S(1)} collective-permute-done((bf16[256,768]{1,0:T(8,128)(2,1)S(1)}, bf16[256,768]{1,0:T(8,128)(2,1)S(1)}, u32[]{:S(2)}, u32[]{:S(2)}) %collective-permute-start.4) | collective-permute-done | bytes 393248 | tf_op jit(solution)/shard_map/ppermute | solution.py:416
  20.0 1.5 %collective-permute-start.9 = (bf16[256,768]{1,0:T(8,128)(2,1)S(1)}, bf16[256,768]{1,0:T(8,128)(2,1)S(1)}, u32[]{:S(2)}, u32[]{:S(2)}) collective-permute-start(bf16[256,768]{1,0:T(8,128)(2,1)S(1)} %get-tuple-element.119), channel_id=1, source_target_pairs={{0,8},{24,16},{1,9},{25,17},{2,10},{26,18},{3,11},{27,19},{4,12},{... | collective-permute-start | bytes 1179656 | tf_op jit(solution)/shard_map/ppermute | solution.py:416
  22.3 1.3 collective-permute-start.11
  23.6 3.7 %collective-permute-done.3.refs_4_.refs_5_ = bf16[64,896]{1,0:T(8,128)(2,1)S(1)} collective-permute-done((bf16[64,896]{1,0:T(8,128)(2,1)S(1)}, bf16[64,896]{1,0:T(8,128)(2,1)S(1)}, u32[]{:S(2)}, u32[]{:S(2)}) %collective-permute-start.3) | collective-permute-done | bytes 114720 | tf_op jit(solution)/shard_map/ppermute | solution.py:405
  27.6 1.5 %collective-permute-start.5 = (bf16[288,768]{1,0:T(8,128)(2,1)S(1)}, bf16[288,768]{1,0:T(8,128)(2,1)S(1)}, u32[]{:S(2)}, u32[]{:S(2)}) collective-permute-start(bf16[288,768]{1,0:T(8,128)(2,1)S(1)} %get-tuple-element.107.refs_0_.msg_ref), channel_id=1, source_target_pairs={{0,2},{1,5},{2,0},{3,7},{4,6},{5,1},{6,4},{7,3},{8,10},{9,13},{10,... | collective-permute-start | bytes 1327112 | tf_op jit(solution)/shard_map/ppermute | solution.py:393
  30.0 3.4 %collective-permute-start.12 = (bf16[256,768]{1,0:T(8,128)(2,1)S(1)}, bf16[256,768]{1,0:T(8,128)(2,1)S(1)}, u32[]{:S(2)}, u32[]{:S(2)}) collective-permute-start(bf16[256,768]{1,0:T(8,128)(2,1)S(1)} %get-tuple-element.120), channel_id=1, source_target_pairs={{0,8},{8,0},{16,24},{24,16},{1,9},{9,1},{17,25},{25,17},{2,10},{10... | collective-permute-start | bytes 1179656 | tf_op jit(solution)/shard_map/ppermute | solution.py:416
  35.0 0.9 collective-permute-done.11.far_ref
  36.0 6.0 %collective-permute-start.13 = (bf16[256,768]{1,0:T(8,128)(2,1)S(1)}, bf16[256,768]{1,0:T(8,128)(2,1)S(1)}, u32[]{:S(2)}, u32[]{:S(2)}) collective-permute-start(bf16[256,768]{1,0:T(8,128)(2,1)S(1)} %get-tuple-element.122), channel_id=1, source_target_pairs={{0,8},{24,16},{1,9},{25,17},{2,10},{26,18},{3,11},{27,19},{4,12},{... | collective-permute-start | bytes 1179656 | tf_op jit(solution)/shard_map/ppermute | solution.py:416
  42.0 1.6 %collective-permute-start.7 = (bf16[288,768]{1,0:T(8,128)(2,1)S(1)}, bf16[288,768]{1,0:T(8,128)(2,1)S(1)}, u32[]{:S(2)}, u32[]{:S(2)}) collective-permute-start(bf16[288,768]{1,0:T(8,128)(2,1)S(1)} %get-tuple-element.107.refs_0_.msg_ref), channel_id=1, source_target_pairs={{0,4},{1,3},{2,6},{3,1},{4,0},{5,7},{6,2},{7,5},{8,12},{9,11},{10,... | collective-permute-start | bytes 1327112 | tf_op jit(solution)/shard_map/ppermute | solution.py:393
  45.1 1.3 collective-permute-start.15
  47.2 3.1 %collective-permute-done.7.refs_1_ = bf16[288,768]{1,0:T(8,128)(2,1)S(1)} collective-permute-done((bf16[288,768]{1,0:T(8,128)(2,1)S(1)}, bf16[288,768]{1,0:T(8,128)(2,1)S(1)}, u32[]{:S(2)}, u32[]{:S(2)}) %collective-permute-start.7) | collective-permute-done | bytes 442400 | tf_op jit(solution)/shard_map/ppermute | solution.py:393
  50.3 1.4 blocks.22
  51.7 3.3 %collective-permute-done.6.refs_0_ = bf16[288,768]{1,0:T(8,128)(2,1)S(1)} collective-permute-done((bf16[288,768]{1,0:T(8,128)(2,1)S(1)}, bf16[288,768]{1,0:T(8,128)(2,1)S(1)}, u32[]{:S(2)}, u32[]{:S(2)}) %collective-permute-start.6) | collective-permute-done | bytes 442400 | tf_op jit(solution)/shard_map/ppermute | solution.py:393
  59.1 1.6 %collective-permute-start.16 = (f32[64,256]{1,0:T(8,128)S(1)}, f32[64,256]{1,0:T(8,128)S(1)}, u32[]{:S(2)}, u32[]{:S(2)}) collective-permute-start(f32[64,256]{1,0:T(8,128)S(1)} %first_inner.1), channel_id=1, source_target_pairs={{0,2},{1,3},{2,0},{3,1},{4,6},{5,7},{6,4},{7,5},{8,10},{9,11},{10,... | collective-permute-start | bytes 196616 | tf_op jit(solution)/shard_map/ppermute | solution.py:393
  60.6 3.0 %collective-permute-done.16 = f32[64,256]{1,0:T(8,128)S(1)} collective-permute-done((f32[64,256]{1,0:T(8,128)S(1)}, f32[64,256]{1,0:T(8,128)S(1)}, u32[]{:S(2)}, u32[]{:S(2)}) %collective-permute-start.16) | collective-permute-done | bytes 65568 | tf_op jit(solution)/shard_map/ppermute | solution.py:393
  63.6 1.6 %collective-permute-start.17 = (f32[64,256]{1,0:T(8,128)S(1)}, f32[64,256]{1,0:T(8,128)S(1)}, u32[]{:S(2)}, u32[]{:S(2)}) collective-permute-start(f32[64,256]{1,0:T(8,128)S(1)} %add.9), channel_id=1, source_target_pairs={{0,4},{1,5},{2,6},{3,7},{4,0},{5,1},{6,2},{7,3},{8,12},{9,13},{10,... | collective-permute-start | bytes 196616 | tf_op jit(solution)/shard_map/ppermute | solution.py:393
  65.2 2.8 %collective-permute-done.17 = f32[64,256]{1,0:T(8,128)S(1)} collective-permute-done((f32[64,256]{1,0:T(8,128)S(1)}, f32[64,256]{1,0:T(8,128)S(1)}, u32[]{:S(2)}, u32[]{:S(2)}) %collective-permute-start.17) | collective-permute-done | bytes 65568 | tf_op jit(solution)/shard_map/ppermute | solution.py:393
  68.1 1.0 gather1.1.upc_ref
  70.2 1.6 %collective-permute-start.32 = (bf16[144,768]{1,0:T(8,128)(2,1)S(1)}, bf16[144,768]{1,0:T(8,128)(2,1)S(1)}, u32[]{:S(2)}, u32[]{:S(2)}) collective-permute-start(bf16[144,768]{1,0:T(8,128)(2,1)S(1)} %get-tuple-element.160.refs_0_), channel_id=1, source_target_pairs={{0,2},{1,5},{2,0},{3,7},{4,6},{5,1},{6,4},{7,3},{8,10},{9,13},{10,... | collective-permute-start | bytes 663560 | tf_op jit(solution)/shard_map/ppermute | solution.py:393
  73.2 1.5 %collective-permute-start.34 = (bf16[144,768]{1,0:T(8,128)(2,1)S(1)}, bf16[144,768]{1,0:T(8,128)(2,1)S(1)}, u32[]{:S(2)}, u32[]{:S(2)}) collective-permute-start(bf16[144,768]{1,0:T(8,128)(2,1)S(1)} %get-tuple-element.160.refs_0_), channel_id=1, source_target_pairs={{0,4},{1,3},{2,6},{3,1},{4,0},{5,7},{6,2},{7,5},{8,12},{9,11},{10,... | collective-permute-start | bytes 663560 | tf_op jit(solution)/shard_map/ppermute | solution.py:393
  74.8 2.0 %collective-permute-done.32.refs_0_ = bf16[144,768]{1,0:T(8,128)(2,1)S(1)} collective-permute-done((bf16[144,768]{1,0:T(8,128)(2,1)S(1)}, bf16[144,768]{1,0:T(8,128)(2,1)S(1)}, u32[]{:S(2)}, u32[]{:S(2)}) %collective-permute-start.32) | collective-permute-done | bytes 221216 | tf_op jit(solution)/shard_map/ppermute | solution.py:393
  76.8 1.5 %collective-permute-start.33 = (bf16[144,768]{1,0:T(8,128)(2,1)S(1)}, bf16[144,768]{1,0:T(8,128)(2,1)S(1)}, u32[]{:S(2)}, u32[]{:S(2)}) collective-permute-start(bf16[144,768]{1,0:T(8,128)(2,1)S(1)} %collective-permute-done.32.refs_0_), channel_id=1, source_target_pairs={{0,4},{1,3},{2,6},{3,1},{4,0},{5,7},{6,2},{7,5},{8,12},{9,11},{10,... | collective-permute-start | bytes 663560 | tf_op jit(solution)/shard_map/ppermute | solution.py:393
  78.8 2.7 %collective-permute-done.19.refs_0_ = bf16[144,768]{1,0:T(8,128)(2,1)S(1)} collective-permute-done((bf16[144,768]{1,0:T(8,128)(2,1)S(1)}, bf16[144,768]{1,0:T(8,128)(2,1)S(1)}, u32[]{:S(2)}, u32[]{:S(2)}) %collective-permute-start.19) | collective-permute-done | bytes 221216 | tf_op jit(solution)/shard_map/ppermute | solution.py:393
  81.5 1.5 %collective-permute-start.20 = (bf16[144,768]{1,0:T(8,128)(2,1)S(1)}, bf16[144,768]{1,0:T(8,128)(2,1)S(1)}, u32[]{:S(2)}, u32[]{:S(2)}) collective-permute-start(bf16[144,768]{1,0:T(8,128)(2,1)S(1)} %collective-permute-done.19.refs_0_), channel_id=1, source_target_pairs={{0,4},{1,3},{2,6},{3,1},{4,0},{5,7},{6,2},{7,5},{8,12},{9,11},{10,... | collective-permute-start | bytes 663560 | tf_op jit(solution)/shard_map/ppermute | solution.py:393
  86.3 1.1 collective-permute-done.20.refs_0_
  89.3 1.6 %collective-permute-start.36 = (bf16[144,768]{1,0:T(8,128)(2,1)S(1)}, bf16[144,768]{1,0:T(8,128)(2,1)S(1)}, u32[]{:S(2)}, u32[]{:S(2)}) collective-permute-start(bf16[144,768]{1,0:T(8,128)(2,1)S(1)} %get-tuple-element.171.refs_0_), channel_id=1, source_target_pairs={{0,2},{1,5},{2,0},{3,7},{4,6},{5,1},{6,4},{7,3},{8,10},{9,13},{10,... | collective-permute-start | bytes 663560 | tf_op jit(solution)/shard_map/ppermute | solution.py:393
  92.4 1.5 %collective-permute-start.38 = (bf16[144,768]{1,0:T(8,128)(2,1)S(1)}, bf16[144,768]{1,0:T(8,128)(2,1)S(1)}, u32[]{:S(2)}, u32[]{:S(2)}) collective-permute-start(bf16[144,768]{1,0:T(8,128)(2,1)S(1)} %get-tuple-element.171.refs_0_), channel_id=1, source_target_pairs={{0,4},{1,3},{2,6},{3,1},{4,0},{5,7},{6,2},{7,5},{8,12},{9,11},{10,... | collective-permute-start | bytes 663560 | tf_op jit(solution)/shard_map/ppermute | solution.py:393
  93.9 2.0 %collective-permute-done.36.refs_0_ = bf16[144,768]{1,0:T(8,128)(2,1)S(1)} collective-permute-done((bf16[144,768]{1,0:T(8,128)(2,1)S(1)}, bf16[144,768]{1,0:T(8,128)(2,1)S(1)}, u32[]{:S(2)}, u32[]{:S(2)}) %collective-permute-start.36) | collective-permute-done | bytes 221216 | tf_op jit(solution)/shard_map/ppermute | solution.py:393
  95.9 1.7 %collective-permute-start.37 = (bf16[144,768]{1,0:T(8,128)(2,1)S(1)}, bf16[144,768]{1,0:T(8,128)(2,1)S(1)}, u32[]{:S(2)}, u32[]{:S(2)}) collective-permute-start(bf16[144,768]{1,0:T(8,128)(2,1)S(1)} %collective-permute-done.36.refs_0_), channel_id=1, source_target_pairs={{0,4},{1,3},{2,6},{3,1},{4,0},{5,7},{6,2},{7,5},{8,12},{9,11},{10,... | collective-permute-start | bytes 663560 | tf_op jit(solution)/shard_map/ppermute | solution.py:393
  98.0 2.7 %collective-permute-done.23.refs_0_ = bf16[144,768]{1,0:T(8,128)(2,1)S(1)} collective-permute-done((bf16[144,768]{1,0:T(8,128)(2,1)S(1)}, bf16[144,768]{1,0:T(8,128)(2,1)S(1)}, u32[]{:S(2)}, u32[]{:S(2)}) %collective-permute-start.23) | collective-permute-done | bytes 221216 | tf_op jit(solution)/shard_map/ppermute | solution.py:393
  100.7 1.7 %collective-permute-start.24 = (bf16[144,768]{1,0:T(8,128)(2,1)S(1)}, bf16[144,768]{1,0:T(8,128)(2,1)S(1)}, u32[]{:S(2)}, u32[]{:S(2)}) collective-permute-start(bf16[144,768]{1,0:T(8,128)(2,1)S(1)} %collective-permute-done.23.refs_0_), channel_id=1, source_target_pairs={{0,4},{1,3},{2,6},{3,1},{4,0},{5,7},{6,2},{7,5},{8,12},{9,11},{10,... | collective-permute-start | bytes 663560 | tf_op jit(solution)/shard_map/ppermute | solution.py:393
  105.6 1.0 collective-permute-done.24.refs_0_
  108.5 1.6 %collective-permute-start.40 = (bf16[144,768]{1,0:T(8,128)(2,1)S(1)}, bf16[144,768]{1,0:T(8,128)(2,1)S(1)}, u32[]{:S(2)}, u32[]{:S(2)}) collective-permute-start(bf16[144,768]{1,0:T(8,128)(2,1)S(1)} %get-tuple-element.182.refs_0_), channel_id=1, source_target_pairs={{0,2},{1,5},{2,0},{3,7},{4,6},{5,1},{6,4},{7,3},{8,10},{9,13},{10,... | collective-permute-start | bytes 663560 | tf_op jit(solution)/shard_map/ppermute | solution.py:393
  111.5 1.5 %collective-permute-start.42 = (bf16[144,768]{1,0:T(8,128)(2,1)S(1)}, bf16[144,768]{1,0:T(8,128)(2,1)S(1)}, u32[]{:S(2)}, u32[]{:S(2)}) collective-permute-start(bf16[144,768]{1,0:T(8,128)(2,1)S(1)} %get-tuple-element.182.refs_0_), channel_id=1, source_target_pairs={{0,4},{1,3},{2,6},{3,1},{4,0},{5,7},{6,2},{7,5},{8,12},{9,11},{10,... | collective-permute-start | bytes 663560 | tf_op jit(solution)/shard_map/ppermute | solution.py:393
  113.0 2.0 %collective-permute-done.40.refs_0_ = bf16[144,768]{1,0:T(8,128)(2,1)S(1)} collective-permute-done((bf16[144,768]{1,0:T(8,128)(2,1)S(1)}, bf16[144,768]{1,0:T(8,128)(2,1)S(1)}, u32[]{:S(2)}, u32[]{:S(2)}) %collective-permute-start.40) | collective-permute-done | bytes 221216 | tf_op jit(solution)/shard_map/ppermute | solution.py:393
  115.1 1.5 %collective-permute-start.41 = (bf16[144,768]{1,0:T(8,128)(2,1)S(1)}, bf16[144,768]{1,0:T(8,128)(2,1)S(1)}, u32[]{:S(2)}, u32[]{:S(2)}) collective-permute-start(bf16[144,768]{1,0:T(8,128)(2,1)S(1)} %collective-permute-done.40.refs_0_), channel_id=1, source_target_pairs={{0,4},{1,3},{2,6},{3,1},{4,0},{5,7},{6,2},{7,5},{8,12},{9,11},{10,... | collective-permute-start | bytes 663560 | tf_op jit(solution)/shard_map/ppermute | solution.py:393
  117.1 2.7 %collective-permute-done.27.refs_0_ = bf16[144,768]{1,0:T(8,128)(2,1)S(1)} collective-permute-done((bf16[144,768]{1,0:T(8,128)(2,1)S(1)}, bf16[144,768]{1,0:T(8,128)(2,1)S(1)}, u32[]{:S(2)}, u32[]{:S(2)}) %collective-permute-start.27) | collective-permute-done | bytes 221216 | tf_op jit(solution)/shard_map/ppermute | solution.py:393
  119.8 1.5 %collective-permute-start.28 = (bf16[144,768]{1,0:T(8,128)(2,1)S(1)}, bf16[144,768]{1,0:T(8,128)(2,1)S(1)}, u32[]{:S(2)}, u32[]{:S(2)}) collective-permute-start(bf16[144,768]{1,0:T(8,128)(2,1)S(1)} %collective-permute-done.27.refs_0_), channel_id=1, source_target_pairs={{0,4},{1,3},{2,6},{3,1},{4,0},{5,7},{6,2},{7,5},{8,12},{9,11},{10,... | collective-permute-start | bytes 663560 | tf_op jit(solution)/shard_map/ppermute | solution.py:393
  124.8 0.9 collective-permute-done.28.refs_0_
  127.1 2.0 %collective-permute-start.44 = (bf16[64,768]{1,0:T(8,128)(2,1)S(1)}, bf16[64,768]{1,0:T(8,128)(2,1)S(1)}, u32[]{:S(2)}, u32[]{:S(2)}) collective-permute-start(bf16[64,768]{1,0:T(8,128)(2,1)S(1)} %get-tuple-element.193), channel_id=1, source_target_pairs={{0,16},{8,24},{16,0},{24,8},{1,17},{9,25},{17,1},{25,9},{2,18},{10... | collective-permute-start | bytes 294920 | tf_op jit(solution)/shard_map/ppermute | solution.py:405
  129.1 1.8 %collective-permute-start.45 = (bf16[64,768]{1,0:T(8,128)(2,1)S(1)}, bf16[64,768]{1,0:T(8,128)(2,1)S(1)}, u32[]{:S(2)}, u32[]{:S(2)}) collective-permute-start(bf16[64,768]{1,0:T(8,128)(2,1)S(1)} %get-tuple-element.194), channel_id=1, source_target_pairs={{0,24},{8,16},{16,8},{24,0},{1,25},{9,17},{17,9},{25,1},{2,26},{10... | collective-permute-start | bytes 294920 | tf_op jit(solution)/shard_map/ppermute | solution.py:405
  131.4 6.6 %collective-permute-done.44.refs_2_ = bf16[64,768]{1,0:T(8,128)(2,1)S(1)} collective-permute-done((bf16[64,768]{1,0:T(8,128)(2,1)S(1)}, bf16[64,768]{1,0:T(8,128)(2,1)S(1)}, u32[]{:S(2)}, u32[]{:S(2)}) %collective-permute-start.44) | collective-permute-done | bytes 98336 | tf_op jit(solution)/shard_map/ppermute | solution.py:405
  138.0 0.9 collective-permute-done.31.refs_1_
  138.9 1.1 unsort.1
  (104 shorter events, 33.5 us)
Async XLA Ops:
  0.7 20.8 %copy-start = (bf16[8,64,768]{2,1,0:T(8,128)(2,1)S(1)}, bf16[8,64,768]{2,1,0:T(8,128)(2,1)}, u32[]{:S(2)}) copy-start(bf16[8,64,768]{2,1,0:T(8,128)(2,1)} %param.11) | copy-start | bytes 2359300
  0.7 26.7 %copy-start.2 = (f32[6144]{0:T(1024)S(1)}, f32[6144]{0:T(1024)}, u32[]{:S(2)}) copy-start(f32[6144]{0:T(1024)} %param.9) | copy-start | bytes 73732
  4.4 22.9 %collective-permute-start = (bf16[3072,768]{1,0:T(8,128)(2,1)S(1)}, bf16[3072,768]{1,0:T(8,128)(2,1)S(1)}, u32[]{:S(2)}, u32[]{:S(2)}) collective-permute-start(bf16[3072,768]{1,0:T(8,128)(2,1)S(1)} %get-tuple-element.101), channel_id=1, source_target_pairs={{0,1},{1,0},{2,3},{3,2},{4,5},{5,4},{6,7},{7,6},{8,9},{9,8},{10,11... | collective-permute-start | bytes 14155784 | tf_op jit(solution)/shard_map/ppermute | solution.py:393
  4.9 15.1 %collective-permute-start.4 = (bf16[256,768]{1,0:T(8,128)(2,1)S(1)}, bf16[256,768]{1,0:T(8,128)(2,1)S(1)}, u32[]{:S(2)}, u32[]{:S(2)}) collective-permute-start(bf16[256,768]{1,0:T(8,128)(2,1)S(1)} %get-tuple-element.106), channel_id=1, source_target_pairs={{0,8},{8,0},{16,24},{24,16},{1,9},{9,1},{17,25},{25,17},{2,10},{10... | collective-permute-start | bytes 1179656 | tf_op jit(solution)/shard_map/ppermute | solution.py:416
  7.6 14.7 %collective-permute-start.1 = (bf16[64,896]{1,0:T(8,128)(2,1)S(1)}, bf16[64,896]{1,0:T(8,128)(2,1)S(1)}, u32[]{:S(2)}, u32[]{:S(2)}) collective-permute-start(bf16[64,896]{1,0:T(8,128)(2,1)S(1)} %get-tuple-element.103), channel_id=1, source_target_pairs={{0,8},{8,0},{16,24},{24,16},{1,9},{9,1},{17,25},{25,17},{2,10},{10... | collective-permute-start | bytes 344072 | tf_op jit(solution)/shard_map/ppermute | solution.py:405
  7.7 15.9 %collective-permute-start.2 = (bf16[64,896]{1,0:T(8,128)(2,1)S(1)}, bf16[64,896]{1,0:T(8,128)(2,1)S(1)}, u32[]{:S(2)}, u32[]{:S(2)}) collective-permute-start(bf16[64,896]{1,0:T(8,128)(2,1)S(1)} %get-tuple-element.104), channel_id=1, source_target_pairs={{0,16},{8,24},{16,0},{24,8},{1,17},{9,25},{17,1},{25,9},{2,18},{10... | collective-permute-start | bytes 344072 | tf_op jit(solution)/shard_map/ppermute | solution.py:405
  10.6 16.7 %collective-permute-start.3 = (bf16[64,896]{1,0:T(8,128)(2,1)S(1)}, bf16[64,896]{1,0:T(8,128)(2,1)S(1)}, u32[]{:S(2)}, u32[]{:S(2)}) collective-permute-start(bf16[64,896]{1,0:T(8,128)(2,1)S(1)} %get-tuple-element.105), channel_id=1, source_target_pairs={{0,24},{8,16},{16,8},{24,0},{1,25},{9,17},{17,9},{25,1},{2,26},{10... | collective-permute-start | bytes 344072 | tf_op jit(solution)/shard_map/ppermute | solution.py:405
  20.0 13.4 %collective-permute-start.9 = (bf16[256,768]{1,0:T(8,128)(2,1)S(1)}, bf16[256,768]{1,0:T(8,128)(2,1)S(1)}, u32[]{:S(2)}, u32[]{:S(2)}) collective-permute-start(bf16[256,768]{1,0:T(8,128)(2,1)S(1)} %get-tuple-element.119), channel_id=1, source_target_pairs={{0,8},{24,16},{1,9},{25,17},{2,10},{26,18},{3,11},{27,19},{4,12},{... | collective-permute-start | bytes 1179656 | tf_op jit(solution)/shard_map/ppermute | solution.py:416
  22.3 13.7 %collective-permute-start.11 = (bf16[256,768]{1,0:T(8,128)(2,1)S(1)}, bf16[256,768]{1,0:T(8,128)(2,1)S(1)}, u32[]{:S(2)}, u32[]{:S(2)}) collective-permute-start(bf16[256,768]{1,0:T(8,128)(2,1)S(1)} %far0.1), channel_id=1, source_target_pairs={{8,24},{16,0},{9,25},{17,1},{10,26},{18,2},{11,27},{19,3},{12,28},... | collective-permute-start | bytes 1179656 | tf_op jit(solution)/shard_map/ppermute | solution.py:416
  27.6 16.0 %collective-permute-start.5 = (bf16[288,768]{1,0:T(8,128)(2,1)S(1)}, bf16[288,768]{1,0:T(8,128)(2,1)S(1)}, u32[]{:S(2)}, u32[]{:S(2)}) collective-permute-start(bf16[288,768]{1,0:T(8,128)(2,1)S(1)} %get-tuple-element.107.refs_0_.msg_ref), channel_id=1, source_target_pairs={{0,2},{1,5},{2,0},{3,7},{4,6},{5,1},{6,4},{7,3},{8,10},{9,13},{10,... | collective-permute-start | bytes 1327112 | tf_op jit(solution)/shard_map/ppermute | solution.py:393
  30.0 14.3 %collective-permute-start.12 = (bf16[256,768]{1,0:T(8,128)(2,1)S(1)}, bf16[256,768]{1,0:T(8,128)(2,1)S(1)}, u32[]{:S(2)}, u32[]{:S(2)}) collective-permute-start(bf16[256,768]{1,0:T(8,128)(2,1)S(1)} %get-tuple-element.120), channel_id=1, source_target_pairs={{0,8},{8,0},{16,24},{24,16},{1,9},{9,1},{17,25},{25,17},{2,10},{10... | collective-permute-start | bytes 1179656 | tf_op jit(solution)/shard_map/ppermute | solution.py:416
  34.2 23.2 %collective-permute-start.10 = (bf16[256,768]{1,0:T(8,128)(2,1)S(1)}, bf16[256,768]{1,0:T(8,128)(2,1)S(1)}, u32[]{:S(2)}, u32[]{:S(2)}) collective-permute-start(bf16[256,768]{1,0:T(8,128)(2,1)S(1)} %near0.1), channel_id=1, source_target_pairs={{8,16},{16,8},{9,17},{17,9},{10,18},{18,10},{11,19},{19,11},{12,20... | collective-permute-start | bytes 1179656 | tf_op jit(solution)/shard_map/ppermute | solution.py:416
  36.0 20.0 %collective-permute-start.13 = (bf16[256,768]{1,0:T(8,128)(2,1)S(1)}, bf16[256,768]{1,0:T(8,128)(2,1)S(1)}, u32[]{:S(2)}, u32[]{:S(2)}) collective-permute-start(bf16[256,768]{1,0:T(8,128)(2,1)S(1)} %get-tuple-element.122), channel_id=1, source_target_pairs={{0,8},{24,16},{1,9},{25,17},{2,10},{26,18},{3,11},{27,19},{4,12},{... | collective-permute-start | bytes 1179656 | tf_op jit(solution)/shard_map/ppermute | solution.py:416
  42.0 8.4 %collective-permute-start.7 = (bf16[288,768]{1,0:T(8,128)(2,1)S(1)}, bf16[288,768]{1,0:T(8,128)(2,1)S(1)}, u32[]{:S(2)}, u32[]{:S(2)}) collective-permute-start(bf16[288,768]{1,0:T(8,128)(2,1)S(1)} %get-tuple-element.107.refs_0_.msg_ref), channel_id=1, source_target_pairs={{0,4},{1,3},{2,6},{3,1},{4,0},{5,7},{6,2},{7,5},{8,12},{9,11},{10,... | collective-permute-start | bytes 1327112 | tf_op jit(solution)/shard_map/ppermute | solution.py:393
  43.5 11.5 %collective-permute-start.6 = (bf16[288,768]{1,0:T(8,128)(2,1)S(1)}, bf16[288,768]{1,0:T(8,128)(2,1)S(1)}, u32[]{:S(2)}, u32[]{:S(2)}) collective-permute-start(bf16[288,768]{1,0:T(8,128)(2,1)S(1)} %collective-permute-done.5.refs_0_), channel_id=1, source_target_pairs={{0,4},{1,3},{2,6},{3,1},{4,0},{5,7},{6,2},{7,5},{8,12},{9,11},{10,... | collective-permute-start | bytes 1327112 | tf_op jit(solution)/shard_map/ppermute | solution.py:393
  45.1 23.0 %collective-permute-start.15 = (bf16[256,768]{1,0:T(8,128)(2,1)S(1)}, bf16[256,768]{1,0:T(8,128)(2,1)S(1)}, u32[]{:S(2)}, u32[]{:S(2)}) collective-permute-start(bf16[256,768]{1,0:T(8,128)(2,1)S(1)} %far1.1), channel_id=1, source_target_pairs={{8,24},{16,0},{9,25},{17,1},{10,26},{18,2},{11,27},{19,3},{12,28},... | collective-permute-start | bytes 1179656 | tf_op jit(solution)/shard_map/ppermute | solution.py:416
  55.9 13.4 %collective-permute-start.8 = (bf16[288,768]{1,0:T(8,128)(2,1)S(1)}, bf16[288,768]{1,0:T(8,128)(2,1)S(1)}, u32[]{:S(2)}, u32[]{:S(2)}) collective-permute-start(bf16[288,768]{1,0:T(8,128)(2,1)S(1)} %get-tuple-element.116), channel_id=1, source_target_pairs={{0,1},{1,0},{2,3},{3,2},{4,5},{5,4},{6,7},{7,6},{8,9},{9,8},{10,11... | collective-permute-start | bytes 1327112 | tf_op jit(solution)/shard_map/ppermute | solution.py:393
  56.7 11.3 %collective-permute-start.14 = (bf16[256,768]{1,0:T(8,128)(2,1)S(1)}, bf16[256,768]{1,0:T(8,128)(2,1)S(1)}, u32[]{:S(2)}, u32[]{:S(2)}) collective-permute-start(bf16[256,768]{1,0:T(8,128)(2,1)S(1)} %near1.1), channel_id=1, source_target_pairs={{8,16},{16,8},{9,17},{17,9},{10,18},{18,10},{11,19},{19,11},{12,20... | collective-permute-start | bytes 1179656 | tf_op jit(solution)/shard_map/ppermute | solution.py:416
  59.1 4.5 %collective-permute-start.16 = (f32[64,256]{1,0:T(8,128)S(1)}, f32[64,256]{1,0:T(8,128)S(1)}, u32[]{:S(2)}, u32[]{:S(2)}) collective-permute-start(f32[64,256]{1,0:T(8,128)S(1)} %first_inner.1), channel_id=1, source_target_pairs={{0,2},{1,3},{2,0},{3,1},{4,6},{5,7},{6,4},{7,5},{8,10},{9,11},{10,... | collective-permute-start | bytes 196616 | tf_op jit(solution)/shard_map/ppermute | solution.py:393
  63.6 4.3 %collective-permute-start.17 = (f32[64,256]{1,0:T(8,128)S(1)}, f32[64,256]{1,0:T(8,128)S(1)}, u32[]{:S(2)}, u32[]{:S(2)}) collective-permute-start(f32[64,256]{1,0:T(8,128)S(1)} %add.9), channel_id=1, source_target_pairs={{0,4},{1,5},{2,6},{3,7},{4,0},{5,1},{6,2},{7,3},{8,12},{9,13},{10,... | collective-permute-start | bytes 196616 | tf_op jit(solution)/shard_map/ppermute | solution.py:393
  68.0 1.3 collective-permute-start.18
  70.2 6.6 %collective-permute-start.32 = (bf16[144,768]{1,0:T(8,128)(2,1)S(1)}, bf16[144,768]{1,0:T(8,128)(2,1)S(1)}, u32[]{:S(2)}, u32[]{:S(2)}) collective-permute-start(bf16[144,768]{1,0:T(8,128)(2,1)S(1)} %get-tuple-element.160.refs_0_), channel_id=1, source_target_pairs={{0,2},{1,5},{2,0},{3,7},{4,6},{5,1},{6,4},{7,3},{8,10},{9,13},{10,... | collective-permute-start | bytes 663560 | tf_op jit(solution)/shard_map/ppermute | solution.py:393
  72.6 8.9 %collective-permute-start.19 = (bf16[144,768]{1,0:T(8,128)(2,1)S(1)}, bf16[144,768]{1,0:T(8,128)(2,1)S(1)}, u32[]{:S(2)}, u32[]{:S(2)}) collective-permute-start(bf16[144,768]{1,0:T(8,128)(2,1)S(1)} %get-tuple-element.124.refs_0_), channel_id=1, source_target_pairs={{0,2},{1,5},{2,0},{3,7},{4,6},{5,1},{6,4},{7,3},{8,10},{9,13},{10,... | collective-permute-start | bytes 663560 | tf_op jit(solution)/shard_map/ppermute | solution.py:393
  73.2 10.8 %collective-permute-start.34 = (bf16[144,768]{1,0:T(8,128)(2,1)S(1)}, bf16[144,768]{1,0:T(8,128)(2,1)S(1)}, u32[]{:S(2)}, u32[]{:S(2)}) collective-permute-start(bf16[144,768]{1,0:T(8,128)(2,1)S(1)} %get-tuple-element.160.refs_0_), channel_id=1, source_target_pairs={{0,4},{1,3},{2,6},{3,1},{4,0},{5,7},{6,2},{7,5},{8,12},{9,11},{10,... | collective-permute-start | bytes 663560 | tf_op jit(solution)/shard_map/ppermute | solution.py:393
  76.8 8.1 %collective-permute-start.33 = (bf16[144,768]{1,0:T(8,128)(2,1)S(1)}, bf16[144,768]{1,0:T(8,128)(2,1)S(1)}, u32[]{:S(2)}, u32[]{:S(2)}) collective-permute-start(bf16[144,768]{1,0:T(8,128)(2,1)S(1)} %collective-permute-done.32.refs_0_), channel_id=1, source_target_pairs={{0,4},{1,3},{2,6},{3,1},{4,0},{5,7},{6,2},{7,5},{8,12},{9,11},{10,... | collective-permute-start | bytes 663560 | tf_op jit(solution)/shard_map/ppermute | solution.py:393
  78.3 7.2 %collective-permute-start.21 = (bf16[144,768]{1,0:T(8,128)(2,1)S(1)}, bf16[144,768]{1,0:T(8,128)(2,1)S(1)}, u32[]{:S(2)}, u32[]{:S(2)}) collective-permute-start(bf16[144,768]{1,0:T(8,128)(2,1)S(1)} %get-tuple-element.124.refs_0_), channel_id=1, source_target_pairs={{0,4},{1,3},{2,6},{3,1},{4,0},{5,7},{6,2},{7,5},{8,12},{9,11},{10,... | collective-permute-start | bytes 663560 | tf_op jit(solution)/shard_map/ppermute | solution.py:393
  81.5 5.9 %collective-permute-start.20 = (bf16[144,768]{1,0:T(8,128)(2,1)S(1)}, bf16[144,768]{1,0:T(8,128)(2,1)S(1)}, u32[]{:S(2)}, u32[]{:S(2)}) collective-permute-start(bf16[144,768]{1,0:T(8,128)(2,1)S(1)} %collective-permute-done.19.refs_0_), channel_id=1, source_target_pairs={{0,4},{1,3},{2,6},{3,1},{4,0},{5,7},{6,2},{7,5},{8,12},{9,11},{10,... | collective-permute-start | bytes 663560 | tf_op jit(solution)/shard_map/ppermute | solution.py:393
  85.4 3.0 %collective-permute-start.35 = (bf16[144,768]{1,0:T(8,128)(2,1)S(1)}, bf16[144,768]{1,0:T(8,128)(2,1)S(1)}, u32[]{:S(2)}, u32[]{:S(2)}) collective-permute-start(bf16[144,768]{1,0:T(8,128)(2,1)S(1)} %get-tuple-element.169), channel_id=1, source_target_pairs={{0,1},{1,0},{2,3},{3,2},{4,5},{5,4},{6,7},{7,6},{8,9},{9,8},{10,11... | collective-permute-start | bytes 663560 | tf_op jit(solution)/shard_map/ppermute | solution.py:393
  88.0 2.9 %collective-permute-start.22 = (bf16[144,768]{1,0:T(8,128)(2,1)S(1)}, bf16[144,768]{1,0:T(8,128)(2,1)S(1)}, u32[]{:S(2)}, u32[]{:S(2)}) collective-permute-start(bf16[144,768]{1,0:T(8,128)(2,1)S(1)} %get-tuple-element.133), channel_id=1, source_target_pairs={{0,1},{1,0},{2,3},{3,2},{4,5},{5,4},{6,7},{7,6},{8,9},{9,8},{10,11... | collective-permute-start | bytes 663560 | tf_op jit(solution)/shard_map/ppermute | solution.py:393
  89.3 6.6 %collective-permute-start.36 = (bf16[144,768]{1,0:T(8,128)(2,1)S(1)}, bf16[144,768]{1,0:T(8,128)(2,1)S(1)}, u32[]{:S(2)}, u32[]{:S(2)}) collective-permute-start(bf16[144,768]{1,0:T(8,128)(2,1)S(1)} %get-tuple-element.171.refs_0_), channel_id=1, source_target_pairs={{0,2},{1,5},{2,0},{3,7},{4,6},{5,1},{6,4},{7,3},{8,10},{9,13},{10,... | collective-permute-start | bytes 663560 | tf_op jit(solution)/shard_map/ppermute | solution.py:393
  91.8 8.9 %collective-permute-start.23 = (bf16[144,768]{1,0:T(8,128)(2,1)S(1)}, bf16[144,768]{1,0:T(8,128)(2,1)S(1)}, u32[]{:S(2)}, u32[]{:S(2)}) collective-permute-start(bf16[144,768]{1,0:T(8,128)(2,1)S(1)} %get-tuple-element.135.refs_0_), channel_id=1, source_target_pairs={{0,2},{1,5},{2,0},{3,7},{4,6},{5,1},{6,4},{7,3},{8,10},{9,13},{10,... | collective-permute-start | bytes 663560 | tf_op jit(solution)/shard_map/ppermute | solution.py:393
  92.4 11.0 %collective-permute-start.38 = (bf16[144,768]{1,0:T(8,128)(2,1)S(1)}, bf16[144,768]{1,0:T(8,128)(2,1)S(1)}, u32[]{:S(2)}, u32[]{:S(2)}) collective-permute-start(bf16[144,768]{1,0:T(8,128)(2,1)S(1)} %get-tuple-element.171.refs_0_), channel_id=1, source_target_pairs={{0,4},{1,3},{2,6},{3,1},{4,0},{5,7},{6,2},{7,5},{8,12},{9,11},{10,... | collective-permute-start | bytes 663560 | tf_op jit(solution)/shard_map/ppermute | solution.py:393
  95.9 8.3 %collective-permute-start.37 = (bf16[144,768]{1,0:T(8,128)(2,1)S(1)}, bf16[144,768]{1,0:T(8,128)(2,1)S(1)}, u32[]{:S(2)}, u32[]{:S(2)}) collective-permute-start(bf16[144,768]{1,0:T(8,128)(2,1)S(1)} %collective-permute-done.36.refs_0_), channel_id=1, source_target_pairs={{0,4},{1,3},{2,6},{3,1},{4,0},{5,7},{6,2},{7,5},{8,12},{9,11},{10,... | collective-permute-start | bytes 663560 | tf_op jit(solution)/shard_map/ppermute | solution.py:393
  97.6 7.2 %collective-permute-start.25 = (bf16[144,768]{1,0:T(8,128)(2,1)S(1)}, bf16[144,768]{1,0:T(8,128)(2,1)S(1)}, u32[]{:S(2)}, u32[]{:S(2)}) collective-permute-start(bf16[144,768]{1,0:T(8,128)(2,1)S(1)} %get-tuple-element.135.refs_0_), channel_id=1, source_target_pairs={{0,4},{1,3},{2,6},{3,1},{4,0},{5,7},{6,2},{7,5},{8,12},{9,11},{10,... | collective-permute-start | bytes 663560 | tf_op jit(solution)/shard_map/ppermute | solution.py:393
  100.7 5.9 %collective-permute-start.24 = (bf16[144,768]{1,0:T(8,128)(2,1)S(1)}, bf16[144,768]{1,0:T(8,128)(2,1)S(1)}, u32[]{:S(2)}, u32[]{:S(2)}) collective-permute-start(bf16[144,768]{1,0:T(8,128)(2,1)S(1)} %collective-permute-done.23.refs_0_), channel_id=1, source_target_pairs={{0,4},{1,3},{2,6},{3,1},{4,0},{5,7},{6,2},{7,5},{8,12},{9,11},{10,... | collective-permute-start | bytes 663560 | tf_op jit(solution)/shard_map/ppermute | solution.py:393
  104.7 2.9 %collective-permute-start.39 = (bf16[144,768]{1,0:T(8,128)(2,1)S(1)}, bf16[144,768]{1,0:T(8,128)(2,1)S(1)}, u32[]{:S(2)}, u32[]{:S(2)}) collective-permute-start(bf16[144,768]{1,0:T(8,128)(2,1)S(1)} %get-tuple-element.180), channel_id=1, source_target_pairs={{0,1},{1,0},{2,3},{3,2},{4,5},{5,4},{6,7},{7,6},{8,9},{9,8},{10,11... | collective-permute-start | bytes 663560 | tf_op jit(solution)/shard_map/ppermute | solution.py:393
  107.1 2.9 %collective-permute-start.26 = (bf16[144,768]{1,0:T(8,128)(2,1)S(1)}, bf16[144,768]{1,0:T(8,128)(2,1)S(1)}, u32[]{:S(2)}, u32[]{:S(2)}) collective-permute-start(bf16[144,768]{1,0:T(8,128)(2,1)S(1)} %get-tuple-element.144), channel_id=1, source_target_pairs={{0,1},{1,0},{2,3},{3,2},{4,5},{5,4},{6,7},{7,6},{8,9},{9,8},{10,11... | collective-permute-start | bytes 663560 | tf_op jit(solution)/shard_map/ppermute | solution.py:393
  108.5 6.6 %collective-permute-start.40 = (bf16[144,768]{1,0:T(8,128)(2,1)S(1)}, bf16[144,768]{1,0:T(8,128)(2,1)S(1)}, u32[]{:S(2)}, u32[]{:S(2)}) collective-permute-start(bf16[144,768]{1,0:T(8,128)(2,1)S(1)} %get-tuple-element.182.refs_0_), channel_id=1, source_target_pairs={{0,2},{1,5},{2,0},{3,7},{4,6},{5,1},{6,4},{7,3},{8,10},{9,13},{10,... | collective-permute-start | bytes 663560 | tf_op jit(solution)/shard_map/ppermute | solution.py:393
  110.9 8.9 %collective-permute-start.27 = (bf16[144,768]{1,0:T(8,128)(2,1)S(1)}, bf16[144,768]{1,0:T(8,128)(2,1)S(1)}, u32[]{:S(2)}, u32[]{:S(2)}) collective-permute-start(bf16[144,768]{1,0:T(8,128)(2,1)S(1)} %get-tuple-element.146.refs_0_), channel_id=1, source_target_pairs={{0,2},{1,5},{2,0},{3,7},{4,6},{5,1},{6,4},{7,3},{8,10},{9,13},{10,... | collective-permute-start | bytes 663560 | tf_op jit(solution)/shard_map/ppermute | solution.py:393
  111.5 11.0 %collective-permute-start.42 = (bf16[144,768]{1,0:T(8,128)(2,1)S(1)}, bf16[144,768]{1,0:T(8,128)(2,1)S(1)}, u32[]{:S(2)}, u32[]{:S(2)}) collective-permute-start(bf16[144,768]{1,0:T(8,128)(2,1)S(1)} %get-tuple-element.182.refs_0_), channel_id=1, source_target_pairs={{0,4},{1,3},{2,6},{3,1},{4,0},{5,7},{6,2},{7,5},{8,12},{9,11},{10,... | collective-permute-start | bytes 663560 | tf_op jit(solution)/shard_map/ppermute | solution.py:393
  115.1 8.3 %collective-permute-start.41 = (bf16[144,768]{1,0:T(8,128)(2,1)S(1)}, bf16[144,768]{1,0:T(8,128)(2,1)S(1)}, u32[]{:S(2)}, u32[]{:S(2)}) collective-permute-start(bf16[144,768]{1,0:T(8,128)(2,1)S(1)} %collective-permute-done.40.refs_0_), channel_id=1, source_target_pairs={{0,4},{1,3},{2,6},{3,1},{4,0},{5,7},{6,2},{7,5},{8,12},{9,11},{10,... | collective-permute-start | bytes 663560 | tf_op jit(solution)/shard_map/ppermute | solution.py:393
  116.6 7.5 %collective-permute-start.29 = (bf16[144,768]{1,0:T(8,128)(2,1)S(1)}, bf16[144,768]{1,0:T(8,128)(2,1)S(1)}, u32[]{:S(2)}, u32[]{:S(2)}) collective-permute-start(bf16[144,768]{1,0:T(8,128)(2,1)S(1)} %get-tuple-element.146.refs_0_), channel_id=1, source_target_pairs={{0,4},{1,3},{2,6},{3,1},{4,0},{5,7},{6,2},{7,5},{8,12},{9,11},{10,... | collective-permute-start | bytes 663560 | tf_op jit(solution)/shard_map/ppermute | solution.py:393
  119.8 5.9 %collective-permute-start.28 = (bf16[144,768]{1,0:T(8,128)(2,1)S(1)}, bf16[144,768]{1,0:T(8,128)(2,1)S(1)}, u32[]{:S(2)}, u32[]{:S(2)}) collective-permute-start(bf16[144,768]{1,0:T(8,128)(2,1)S(1)} %collective-permute-done.27.refs_0_), channel_id=1, source_target_pairs={{0,4},{1,3},{2,6},{3,1},{4,0},{5,7},{6,2},{7,5},{8,12},{9,11},{10,... | collective-permute-start | bytes 663560 | tf_op jit(solution)/shard_map/ppermute | solution.py:393
  123.9 2.8 %collective-permute-start.43 = (bf16[144,768]{1,0:T(8,128)(2,1)S(1)}, bf16[144,768]{1,0:T(8,128)(2,1)S(1)}, u32[]{:S(2)}, u32[]{:S(2)}) collective-permute-start(bf16[144,768]{1,0:T(8,128)(2,1)S(1)} %get-tuple-element.191), channel_id=1, source_target_pairs={{0,1},{1,0},{2,3},{3,2},{4,5},{5,4},{6,7},{7,6},{8,9},{9,8},{10,11... | collective-permute-start | bytes 663560 | tf_op jit(solution)/shard_map/ppermute | solution.py:393
  126.2 4.7 %collective-permute-start.30 = (bf16[144,768]{1,0:T(8,128)(2,1)S(1)}, bf16[144,768]{1,0:T(8,128)(2,1)S(1)}, u32[]{:S(2)}, u32[]{:S(2)}) collective-permute-start(bf16[144,768]{1,0:T(8,128)(2,1)S(1)} %get-tuple-element.155), channel_id=1, source_target_pairs={{0,1},{1,0},{2,3},{3,2},{4,5},{5,4},{6,7},{7,6},{8,9},{9,8},{10,11... | collective-permute-start | bytes 663560 | tf_op jit(solution)/shard_map/ppermute | solution.py:393
  127.1 10.9 %collective-permute-start.44 = (bf16[64,768]{1,0:T(8,128)(2,1)S(1)}, bf16[64,768]{1,0:T(8,128)(2,1)S(1)}, u32[]{:S(2)}, u32[]{:S(2)}) collective-permute-start(bf16[64,768]{1,0:T(8,128)(2,1)S(1)} %get-tuple-element.193), channel_id=1, source_target_pairs={{0,16},{8,24},{16,0},{24,8},{1,17},{9,25},{17,1},{25,9},{2,18},{10... | collective-permute-start | bytes 294920 | tf_op jit(solution)/shard_map/ppermute | solution.py:405
  129.1 8.8 %collective-permute-start.45 = (bf16[64,768]{1,0:T(8,128)(2,1)S(1)}, bf16[64,768]{1,0:T(8,128)(2,1)S(1)}, u32[]{:S(2)}, u32[]{:S(2)}) collective-permute-start(bf16[64,768]{1,0:T(8,128)(2,1)S(1)} %get-tuple-element.194), channel_id=1, source_target_pairs={{0,24},{8,16},{16,8},{24,0},{1,25},{9,17},{17,9},{25,1},{2,26},{10... | collective-permute-start | bytes 294920 | tf_op jit(solution)/shard_map/ppermute | solution.py:405
  131.3 7.6 %collective-permute-start.31 = (bf16[64,768]{1,0:T(8,128)(2,1)S(1)}, bf16[64,768]{1,0:T(8,128)(2,1)S(1)}, u32[]{:S(2)}, u32[]{:S(2)}) collective-permute-start(bf16[64,768]{1,0:T(8,128)(2,1)S(1)} %get-tuple-element.158), channel_id=1, source_target_pairs={{0,8},{8,0},{16,24},{24,16},{1,9},{9,1},{17,25},{25,17},{2,10},{10... | collective-permute-start | bytes 294920 | tf_op jit(solution)/shard_map/ppermute | solution.py:405
  (6 other events, 38.1 us)
